TPU v7x, 32 devices: a whole 2x2x4 slice. The times are simulated.
32 devices in a mesh: dp: 32 (over z, y, x, core).
Axes of the slice: x: 2, y: 2, z: 4, core: 2. Of those that a mesh axis runs over, the one named last changes fastest.
Arguments:
- tokens: bfloat16 [32768, 576], P('dp'), may hold values from -6 to 6
- cotangent: bfloat16 [32768, 576], P('dp'), may hold values from -16 to 16, as said below
- w_query: bfloat16 [331776], P('dp'), may hold values from -0.25 to 0.25
- w_key: bfloat16 [110592], P('dp'), may hold values from -0.25 to 0.25
- w_value: bfloat16 [110592], P('dp'), may hold values from -0.25 to 0.25
- w_out: bfloat16 [331776], P('dp'), may hold values from -2 to 2
- w_gate: bfloat16 [884736], P('dp'), may hold values from -0.25 to 0.25
- w_up: bfloat16 [884736], P('dp'), may hold values from -0.25 to 0.25
- w_down: bfloat16 [884736], P('dp'), may hold values from -0.15625 to 0.15625
- norm_gains: bfloat16 [2, 576], replicated, may hold values from 0.5 to 1.5
Outputs:
- output: bfloat16 [32768, 576], P('dp')
- input_grad: bfloat16 [32768, 576], P('dp')
- query_grad: float32 [331776], P('dp')
- key_grad: float32 [110592], P('dp')
- value_grad: float32 [110592], P('dp')
- out_grad: float32 [331776], P('dp')
- gate_grad: float32 [884736], P('dp')
- up_grad: float32 [884736], P('dp')
- down_grad: float32 [884736], P('dp')
- gain_grad: float32 [2, 576], replicated
Inputs may be any that keep to these rules, and one draw needn't show every extreme that they name: `cotangent`: rows of one sequence share a scale; scales vary over the sequences.
All inputs are finite; a program needn't handle non-finite values.
Results may differ from a plain program's by a relative error of at most 0.013.
Values may be sent and summed in bfloat16 or wider, within the bound.
No kernel may reach another device: no remote copies, remote signals or barrier semaphores. Data moves between devices by JAX's collectives and lax.ppermute only.
A program may use at most 128 MiB of HBM per device.

v0:
```python
import functools

import jax
import jax.numpy as jnp
from jax import lax
from jax.experimental import pallas as pl
from jax.experimental.pallas import tpu as pltpu
from jax.sharding import PartitionSpec as P

HEADS = 9
KV_HEADS = 3
HEAD_DIM = 64
LENGTH = 1024


EPS = 1e-05
THETA = 100000.0
NEG_BIG = -1e30
LANES = 128
VMEM_LIMIT = 56 * 1024 * 1024
CORE_MASK = 1
LIGHT = pl.CostEstimate(flops=10**8, bytes_accessed=10**6, transcendentals=0)


def masks_of(devices):
    plane = tuple(2 * step for step in range(4))
    line = tuple(8 * step for step in range(devices // 8))
    return (plane, line)


def swap(field, mask, devices):
    return lax.ppermute(field, "dp", [(place, place ^ mask) for place in range(devices)])


def tree_sum(terms):
    while len(terms) > 1:
        terms = [terms[at] + terms[at + 1] for at in range(0, len(terms), 2)]
    return terms[0]


def widen(field):
    return field.astype(jnp.float32)


def slot_mask(core, slot, devices):
    line = devices // 8
    return core * CORE_MASK + 2 * (slot // line) + 8 * (slot % line)


def tiles_of(wide):
    return -(-wide // LANES)


def tile_widths(wide):
    return [min(LANES, wide - at) for at in range(0, wide, LANES)]


def flat_starts(shapes, devices):
    starts = [0]
    for rows, wide in shapes:
        starts.append(starts[-1] + rows * wide // (devices * LANES))
    return starts


def tiled_shapes(shapes):
    return [(tiles_of(wide), rows, LANES) for rows, wide in shapes if wide % LANES]


def unpack_kernel(place_ref, *refs, devices, shapes, joined, origins):
    count = len(origins)
    pieces, refs = refs[:count], refs[count:]
    out_count = 1 if joined else len(shapes)
    outs, flats, refs = refs[:out_count], refs[out_count : out_count + len(shapes)], refs[out_count + len(shapes) :]
    stage, landed, arrival, tiled_refs = refs[0], refs[1], refs[2], list(refs[3:])
    place = place_ref[0]
    starts = flat_starts(shapes, devices)
    block = pieces[0].shape[0]
    copies = [
        pltpu.make_async_copy(piece, landed.at[index], arrival.at[index])
        for index, piece in enumerate(pieces)
    ]
    for copy in copies:
        copy.start()
    for index, (core, plane, offset) in enumerate(origins):
        copies[index].wait()
        piece_ref = landed.at[index]
        cuts = []
        for flat, start, stop in zip(flats, starts, starts[1:]):
            low, high = max(start, offset), min(stop, offset + piece_ref.shape[1])
            if low < high:
                cuts.append((flat, stop - start, low - start, low - offset, high - offset))

        def load(slot, carry, core=core, plane=plane, piece_ref=piece_ref, cuts=cuts):
            owner = place ^ slot_mask(core, plane * block + slot, devices)
            piece = piece_ref[slot].astype(jnp.float32)
            if any(low % 8 for _, _, _, low, _ in cuts):
                stage[slot % 4] = piece
            for flat, each, inner, low, high in cuts:
                rows = stage[slot % 4, low:high, :] if low % 8 else piece[low:high]
                flat[pl.ds(owner * each + inner, high - low), :] = rows
            return carry

        lax.fori_loop(0, block, load, 0)
    column = 0
    for index, ((rows, wide), flat) in enumerate(zip(shapes, flats)):
        out = outs[0 if joined else index]
        whole = wide // LANES
        if wide % LANES == 0:
            for at in range(whole):
                tile = flat[pl.ds(at, rows, stride=whole), :]
                out[:, column + at * LANES : column + (at + 1) * LANES] = tile.astype(jnp.bfloat16)
        else:
            target = tiled_refs.pop(0)
            pairs, tiles_in = rows // 2, 2 * wide // LANES
            for at in range(whole + 1):
                target[at, pl.ds(0, pairs, stride=2), :] = flat[pl.ds(at, pairs, stride=tiles_in), :]
            rolled = None
            for at in range(whole, tiles_in):
                after = pltpu.roll(flat[pl.ds(at, pairs, stride=tiles_in), :], LANES // 2, 1)
                if rolled is not None:
                    lane = lax.broadcasted_iota(jnp.int32, after.shape, 1)
                    target[at - whole - 1, pl.ds(1, pairs, stride=2), :] = jnp.where(
                        lane < LANES // 2, rolled, after
                    )
                rolled = after
            target[whole, pl.ds(1, pairs, stride=2), :] = rolled
            for at, width in enumerate(tile_widths(wide)):
                tile = target[at]
                if joined and width < LANES:
                    lane = lax.broadcasted_iota(jnp.int32, tile.shape, 1)
                    tile = jnp.where(lane < width, tile, 0.0)
                    width = LANES
                start = column + at * LANES
                out[:, start : start + width] = tile[:, :width].astype(jnp.bfloat16)
        if joined:
            column += tiles_of(wide) * LANES


def unpack_pieces(place, pieces, origins, shapes, devices, joined):
    rows_in = pieces[0].shape[1]
    outs = shapes
    if joined:
        outs = [(shapes[0][0], sum(tiles_of(wide) for _, wide in shapes) * LANES)]
    return pl.pallas_call(
        functools.partial(
            unpack_kernel, devices=devices, shapes=shapes, joined=joined, origins=origins
        ),
        out_shape=[jax.ShapeDtypeStruct(shape, jnp.bfloat16) for shape in outs],
        in_specs=[pl.BlockSpec(memory_space=pltpu.SMEM)]
        + [pl.BlockSpec(memory_space=pl.ANY)] * len(pieces),
        out_specs=[pl.BlockSpec(memory_space=pltpu.VMEM)] * len(outs),
        scratch_shapes=[
            pltpu.VMEM((rows * wide // LANES, LANES), jnp.float32) for rows, wide in shapes
        ]
        + [
            pltpu.VMEM((4, rows_in, LANES), jnp.float32),
            pltpu.VMEM((len(pieces),) + pieces[0].shape, jnp.bfloat16),
            pltpu.SemaphoreType.DMA((len(pieces),)),
        ]
        + [pltpu.VMEM(shape, jnp.float32) for shape in tiled_shapes(shapes)],
        compiler_params=pltpu.CompilerParams(vmem_limit_bytes=VMEM_LIMIT),
        cost_estimate=LIGHT,
        name="unpack",
    )(place, *pieces)


def pack_kernel(place_ref, *refs, devices, shapes, tiled_in, extra):
    count = len(shapes) + (1 if extra else 0)
    sources, kept_ref, sent_ref, stage = refs[:count], refs[count], refs[count + 1], refs[count + 2]
    flats = refs[count + 3 : count + 3 + len(shapes)]
    tiled_refs = list(refs[count + 3 + len(shapes) :])
    place = place_ref[0]
    starts = flat_starts(shapes, devices)
    for index, ((rows, wide), flat) in enumerate(zip(shapes, flats)):
        source, whole = sources[index], wide // LANES
        if wide % LANES == 0:
            for at in range(whole):
                flat[pl.ds(at, rows, stride=whole), :] = (
                    source[at] if tiled_in[index] else source[:, at * LANES : (at + 1) * LANES]
                )
            continue
        if not tiled_in[index]:
            tiled = tiled_refs.pop(0)
            for at, width in enumerate(tile_widths(wide)):
                tiled[at, :, :width] = source[:, at * LANES : at * LANES + width]
            source = tiled
        pairs, tiles_in = rows // 2, 2 * wide // LANES
        for at in range(whole):
            flat[pl.ds(at, pairs, stride=tiles_in), :] = source[at, pl.ds(0, pairs, stride=2), :]
        before = source[whole, pl.ds(0, pairs, stride=2), :]
        lane = lax.broadcasted_iota(jnp.int32, before.shape, 1)
        for at in range(whole + 1):
            rolled = pltpu.roll(source[at, pl.ds(1, pairs, stride=2), :], LANES // 2, 1)
            flat[pl.ds(whole + at, pairs, stride=tiles_in), :] = jnp.where(
                lane < LANES // 2, before, rolled
            )
            before = rolled
    row_tiles = []
    if extra:
        row = jnp.concatenate([sources[-1][at : at + 1, :] for at in range(extra[0])], 1)
        row_tiles = [
            row[:, at * LANES : (at + 1) * LANES] for at in range(extra[0] * extra[1] // LANES)
        ]
    direct = not extra and all(start % 8 == 0 for start in starts)
    if not direct:
        for at in range(4):
            for index, tile in enumerate(row_tiles):
                stage[at, starts[-1] + index : starts[-1] + index + 1, :] = tile
            used = starts[-1] + len(row_tiles)
            if used < stage.shape[1]:
                stage[at, used:, :] = jnp.zeros((stage.shape[1] - used, LANES), jnp.float32)
    for core, pieces in enumerate((kept_ref, sent_ref)):

        def store(slot, carry, core=core, pieces=pieces):
            owner = place ^ slot_mask(core, slot, devices)
            parts = []
            for flat, start, stop in zip(flats, starts, starts[1:]):
                rows = flat[pl.ds(owner * (stop - start), stop - start), :]
                if direct:
                    parts.append(rows)
                else:
                    stage[slot % 4, start:stop, :] = rows
            spare = stage.shape[1] - starts[-1]
            if direct and spare:
                parts.append(jnp.zeros((spare, LANES), jnp.float32))
            piece = jnp.concatenate(parts, 0) if direct else stage[slot % 4]
            pieces[slot] = piece.astype(jnp.bfloat16)
            return carry

        lax.fori_loop(0, devices // 2, store, 0)


def pack_grads(place, grads, shapes, devices, extra):
    rows_out = sum(rows * wide for rows, wide in shapes) // (devices * LANES)
    sources = list(grads)
    if extra is not None:
        rows_out += extra.size // LANES
        sources.append(extra)
    rows_out = -(-rows_out // 16) * 16
    tiled_in = tuple(grad.ndim == 3 for grad in grads)
    half = jax.ShapeDtypeStruct((devices // 2, rows_out, LANES), jnp.bfloat16)
    untiled = [shape for shape, tiled in zip(shapes, tiled_in) if not tiled]
    return pl.pallas_call(
        functools.partial(
            pack_kernel, devices=devices, shapes=shapes, tiled_in=tiled_in,
            extra=None if extra is None else extra.shape,
        ),
        out_shape=[half, half],
        in_specs=[pl.BlockSpec(memory_space=pltpu.SMEM)]
        + [pl.BlockSpec(memory_space=pltpu.VMEM)] * len(sources),
        out_specs=[pl.BlockSpec(memory_space=pltpu.VMEM)] * 2,
        scratch_shapes=[pltpu.VMEM((4, rows_out, LANES), jnp.float32)]
        + [pltpu.VMEM((rows * wide // LANES, LANES), jnp.float32) for rows, wide in shapes]
        + [pltpu.VMEM(shape, jnp.float32) for shape in tiled_shapes(untiled)],
        compiler_params=pltpu.CompilerParams(vmem_limit_bytes=VMEM_LIMIT),
        cost_estimate=LIGHT,
        name="pack",
    )(place, *sources)


BLOCK = 256


def dot_nt(left, right):
    return lax.dot_general(
        left, right, (((1,), (1,)), ((), ())), preferred_element_type=jnp.float32
    )


def dot_tn(left, right):
    return lax.dot_general(
        left, right, (((0,), (0,)), ((), ())), preferred_element_type=jnp.float32
    )


def dot_nn(left, right):
    return jnp.dot(left, right, preferred_element_type=jnp.float32)


def key_columns(head):
    first = tiles_of(HEADS * HEAD_DIM) * LANES + head * HEAD_DIM
    return slice(first, first + HEAD_DIM)


def value_columns(head):
    first = (tiles_of(HEADS * HEAD_DIM) + tiles_of(KV_HEADS * HEAD_DIM)) * LANES + head * HEAD_DIM
    return slice(first, first + HEAD_DIM)


def attend_kernel(fields_ref, mixed_ref, total_ref, *, head, group):
    length = fields_ref.shape[0]
    keys = fields_ref[:, key_columns(head)]
    values = fields_ref[:, value_columns(head)]
    lower = lax.broadcasted_iota(jnp.int32, (BLOCK, BLOCK), 0) >= lax.broadcasted_iota(
        jnp.int32, (BLOCK, BLOCK), 1
    )
    lane = lax.broadcasted_iota(jnp.int32, (BLOCK, LANES), 1)
    for start in range(0, length, BLOCK):
        mixed, totals_row = [], jnp.zeros((BLOCK, LANES), jnp.float32)
        for member in range(group):
            at = (head * group + member) * HEAD_DIM
            query = fields_ref[start : start + BLOCK, at : at + HEAD_DIM]
            diagonal = jnp.where(lower, dot_nt(query, keys[start : start + BLOCK]), NEG_BIG)
            maxima = jnp.max(diagonal, 1, keepdims=True)
            if start:
                before = dot_nt(query, keys[:start])
                maxima = jnp.maximum(maxima, jnp.max(before, 1, keepdims=True))
            expo = jnp.exp(diagonal - maxima)
            totals = jnp.sum(expo, 1, keepdims=True)
            result = dot_nn(expo.astype(jnp.bfloat16), values[start : start + BLOCK])
            if start:
                expo = jnp.exp(before - maxima)
                totals = totals + jnp.sum(expo, 1, keepdims=True)
                result = result + dot_nn(expo.astype(jnp.bfloat16), values[:start])
            mixed.append(result / totals)
            totals_row = jnp.where(lane == member, maxima + jnp.log(totals), totals_row)
        mixed_ref[start : start + BLOCK, :] = jnp.concatenate(mixed, 1).astype(jnp.bfloat16)
        total_ref[start : start + BLOCK, :] = totals_row


def attend(fields, head, group):
    length = fields.shape[0]
    return pl.pallas_call(
        functools.partial(attend_kernel, head=head, group=group),
        out_shape=[
            jax.ShapeDtypeStruct((length, group * HEAD_DIM), jnp.bfloat16),
            jax.ShapeDtypeStruct((length, LANES), jnp.float32),
        ],
        in_specs=[pl.BlockSpec(memory_space=pltpu.VMEM)],
        out_specs=[pl.BlockSpec(memory_space=pltpu.VMEM)] * 2,
        compiler_params=pltpu.CompilerParams(vmem_limit_bytes=VMEM_LIMIT),
        cost_estimate=LIGHT,
        name="attend",
    )(fields)


def attend_back_kernel(
    fields_ref, back_ref, mixed_ref, total_ref,
    query_back_ref, key_back_ref, queries, backs, totals, deltas, query_sum, key_sum, value_sum,
    *, head, group,
):
    length = fields_ref.shape[0]
    ones = jnp.ones((8, HEAD_DIM), jnp.float32)
    totals[...] = total_ref[...].T[:8]
    for member in range(group):
        at = (head * group + member) * HEAD_DIM
        queries[member] = fields_ref[:, at : at + HEAD_DIM]
        back = back_ref[:, at : at + HEAD_DIM]
        backs[member] = back
        product = back.astype(jnp.float32) * mixed_ref[
            :, member * HEAD_DIM : (member + 1) * HEAD_DIM
        ].astype(jnp.float32)
        deltas[member] = lax.dot_general(
            ones, product, (((1,), (1,)), ((), ())),
            precision=lax.Precision.HIGHEST, preferred_element_type=jnp.float32,
        )
    keys_all = fields_ref[:, key_columns(head)]
    values_all = fields_ref[:, value_columns(head)]
    upper = lax.broadcasted_iota(jnp.int32, (BLOCK, BLOCK), 0) <= lax.broadcasted_iota(
        jnp.int32, (BLOCK, BLOCK), 1
    )
    for member in range(group):
        total_row = totals[member : member + 1, :]
        delta_row = deltas[member][0:1]
        for start in range(0, length, BLOCK):
            keys = keys_all[start : start + BLOCK]
            values = values_all[start : start + BLOCK]
            query = queries[member, start:, :]
            back = backs[member, start:, :]
            scores = dot_nt(keys, query)
            probs = jnp.exp(scores - total_row[:, start:])
            first = jnp.where(upper, probs[:, :BLOCK], 0.0)
            probs = first if start + BLOCK == length else jnp.concatenate(
                [first, probs[:, BLOCK:]], 1
            )
            prob_back = dot_nt(values, back)
            score_back = (probs * (prob_back - delta_row[:, start:])).astype(jnp.bfloat16)
            value_part = dot_nn(probs.astype(jnp.bfloat16), back)
            key_part = dot_nn(score_back, query)
            query_part = dot_tn(score_back, keys)
            if member:
                key_sum[start : start + BLOCK, :] += key_part
                value_sum[start : start + BLOCK, :] += value_part
            else:
                key_sum[start : start + BLOCK, :] = key_part
                value_sum[start : start + BLOCK, :] = value_part
            if start:
                query_sum[member, start:, :] += query_part
            else:
                query_sum[member] = query_part
    query_back_ref[...] = (
        jnp.concatenate([query_sum[member] for member in range(group)], 1) * HEAD_DIM ** (-0.5)
    )
    key_back_ref[...] = jnp.concatenate([key_sum[...], value_sum[...]], 1)


def attend_back(fields, back, mixed, total, head, group):
    length = fields.shape[0]
    return pl.pallas_call(
        functools.partial(attend_back_kernel, head=head, group=group),
        out_shape=[
            jax.ShapeDtypeStruct((length, group * HEAD_DIM), jnp.float32),
            jax.ShapeDtypeStruct((length, 2 * HEAD_DIM), jnp.float32),
        ],
        in_specs=[pl.BlockSpec(memory_space=pltpu.VMEM)] * 4,
        out_specs=[pl.BlockSpec(memory_space=pltpu.VMEM)] * 2,
        scratch_shapes=[
            pltpu.VMEM((group, length, HEAD_DIM), jnp.bfloat16),
            pltpu.VMEM((group, length, HEAD_DIM), jnp.bfloat16),
            pltpu.VMEM((8, length), jnp.float32),
            pltpu.VMEM((group, 8, length), jnp.float32),
            pltpu.VMEM((group, length, HEAD_DIM), jnp.float32),
            pltpu.VMEM((length, HEAD_DIM), jnp.float32),
            pltpu.VMEM((length, HEAD_DIM), jnp.float32),
        ],
        compiler_params=pltpu.CompilerParams(vmem_limit_bytes=VMEM_LIMIT),
        cost_estimate=LIGHT,
        name="attend_back",
    )(fields, back, mixed, total)


def partner_of(tile):
    lane = lax.broadcasted_iota(jnp.int32, tile.shape, 1)
    half = HEAD_DIM // 2
    return jnp.where(
        lane % HEAD_DIM < half, pltpu.roll(tile, LANES - half, 1), pltpu.roll(tile, half, 1)
    )


def normed_rows(tokens_ref, gains_ref):
    resid = tokens_ref[...].astype(jnp.float32)
    inv_rms = lax.rsqrt(jnp.mean(resid * resid, 1, keepdims=True) + EPS)
    return resid, inv_rms, (resid * inv_rms * gains_ref[0:1, :]).astype(jnp.bfloat16)


def project_kernel(tokens_ref, gains_ref, wide_ref, cosine_ref, sine_ref, fields_ref, normed):
    _, _, normed[...] = normed_rows(tokens_ref, gains_ref)
    first_key = tiles_of(HEADS * HEAD_DIM)
    first_value = first_key + tiles_of(KV_HEADS * HEAD_DIM)
    count = fields_ref.shape[1] // LANES
    for start in range(0, count, 2):
        stop = min(start + 2, count)
        pair = dot_nn(normed[...], wide_ref[:, start * LANES : stop * LANES])
        for at in range(start, stop):
            tile = pair[:, (at - start) * LANES : (at - start + 1) * LANES]
            if at < first_value:
                tile = tile * cosine_ref[...] - partner_of(tile) * sine_ref[...]
            tile = tile.astype(jnp.bfloat16)
            if at < first_key:
                tile = (tile.astype(jnp.float32) * HEAD_DIM ** (-0.5)).astype(jnp.bfloat16)
            fields_ref[:, at * LANES : (at + 1) * LANES] = tile


def vmem_call(kernel, out_shape, scratch_shapes, name, *args):
    single = not isinstance(out_shape, list)
    return pl.pallas_call(
        kernel,
        out_shape=out_shape,
        in_specs=[pl.BlockSpec(memory_space=pltpu.VMEM)] * len(args),
        out_specs=pl.BlockSpec(memory_space=pltpu.VMEM)
        if single
        else [pl.BlockSpec(memory_space=pltpu.VMEM)] * len(out_shape),
        scratch_shapes=scratch_shapes,
        compiler_params=pltpu.CompilerParams(vmem_limit_bytes=VMEM_LIMIT),
        cost_estimate=LIGHT,
        name=name,
    )(*args)


def project(tokens, gains, wide, cosine, sine):
    return vmem_call(
        project_kernel,
        jax.ShapeDtypeStruct((tokens.shape[0], wide.shape[1]), jnp.bfloat16),
        [pltpu.VMEM(tokens.shape, jnp.bfloat16)],
        "project",
        tokens, gains, wide, cosine, sine,
    )


def finish_kernel(
    tokens_ref, gains_ref, wide_ref, cosine_ref, sine_ref, mid_back_ref, *refs, heads
):
    backs = refs[: 2 * heads]
    input_grad_ref, tiled_ref, gain_ref, fields, normed_t = refs[2 * heads :]
    half = HEAD_DIM
    group = HEADS // heads
    wide_heads = [(backs[2 * (at // group)], at % group * half) for at in range(HEADS)]
    wide_heads += [None] * (HEADS % 2)
    for offset in (0, half):
        wide_heads += [(backs[2 * at + 1], offset) for at in range(heads)] + [None] * (heads % 2)
    turned = tiles_of(HEADS * HEAD_DIM) + tiles_of(heads * HEAD_DIM)
    for at in range(len(wide_heads) // 2):
        cols = []
        for item in wide_heads[2 * at : 2 * at + 2]:
            if item is None:
                cols.append(jnp.zeros((fields.shape[0], half), jnp.float32))
            else:
                cols.append(item[0][:, item[1] : item[1] + half])
        tile = jnp.concatenate(cols, 1)
        if at < turned:
            tile = tile * cosine_ref[...] + partner_of(tile) * sine_ref[...]
        fields[:, at * LANES : (at + 1) * LANES] = tile.astype(jnp.bfloat16)
    resid, inv_rms, normed = normed_rows(tokens_ref, gains_ref)
    normed_t[...] = normed.T
    count = fields.shape[1] // LANES
    for start in range(0, count, 2):
        stop = min(start + 2, count)
        pair = dot_nn(normed_t[...], fields[:, start * LANES : stop * LANES])
        for at in range(start, stop):
            tiled_ref[at] = pair[:, (at - start) * LANES : (at - start + 1) * LANES]
    one_back = dot_nt(fields[...], wide_ref[...])
    weighted = one_back * gains_ref[0:1, :]
    cubed = inv_rms * inv_rms * inv_rms
    scaled = resid * inv_rms
    gain_ref[...] = jnp.sum(one_back * scaled, 0, keepdims=True)
    mean = jnp.mean(weighted * resid, 1, keepdims=True)
    grad = mid_back_ref[...] + inv_rms * weighted - resid * (cubed * mean)
    input_grad_ref[...] = grad.astype(jnp.bfloat16)


def finish(tokens, gains, wide, cosine, sine, mid_back, backs):
    heads = len(backs)
    rows, width = tokens.shape
    return vmem_call(
        functools.partial(finish_kernel, heads=heads),
        [
            jax.ShapeDtypeStruct(tokens.shape, jnp.bfloat16),
            jax.ShapeDtypeStruct((wide.shape[1] // LANES, width, LANES), jnp.float32),
            jax.ShapeDtypeStruct((1, width), jnp.float32),
        ],
        [
            pltpu.VMEM((rows, wide.shape[1]), jnp.bfloat16),
            pltpu.VMEM((width, rows), jnp.bfloat16),
        ],
        "finish",
        tokens, gains, wide, cosine, sine, mid_back, *[part for back in backs for part in back],
    )


def rotary_tables(length, head_dim):
    half_dim = head_dim // 2
    frequency = THETA ** (-(jnp.arange(half_dim, dtype=jnp.float32) * 2.0 / head_dim))
    angles = jnp.arange(length, dtype=jnp.float32)[:, None] * frequency[None, :]
    return (jnp.cos(angles), jnp.sin(angles))


def rotate_heads(field, cosine, sine):
    half_dim = field.shape[-1] // 2
    first_half = field[..., :half_dim]
    second_half = field[..., half_dim:]
    cosine = cosine[None, :, None, :]
    sine = sine[None, :, None, :]
    return jnp.concatenate(
        [first_half * cosine - second_half * sine, second_half * cosine + first_half * sine], -1
    )


def normalize(hidden, gain):
    inv_rms = lax.rsqrt(jnp.mean(hidden * hidden, -1, keepdims=True) + EPS)
    return (hidden * inv_rms * gain, inv_rms)


def normalize_back(grad, hidden, inv_rms, gain):
    weighted = grad * gain
    cubed = inv_rms * inv_rms * inv_rms
    hidden_grad = inv_rms * weighted - hidden * cubed * jnp.mean(
        weighted * hidden, -1, keepdims=True
    )
    gain_part = jnp.sum(grad * hidden * inv_rms, 0)
    return (hidden_grad, gain_part)


def outer_prod(left, right):
    return lax.dot_general(
        left, right, (((0,), (0,)), ((), ())), preferred_element_type=jnp.float32
    )


def times_transposed(left, matrix):
    return lax.dot_general(
        left, matrix, (((1,), (1,)), ((), ())), preferred_element_type=jnp.float32
    )


def whole_rows(shapes, devices):
    return (devices & (devices - 1)) == 0 and all(
        rows % (8 * devices // 4) == 0 and rows * wide % (devices * LANES) == 0
        for rows, wide in shapes
    )


def place_of():
    return lax.axis_index("dp").astype(jnp.int32).reshape(1)


class WeightGather:
    def __init__(self, shards, shapes, devices):
        self.shards, self.shapes, self.devices = shards, shapes, devices
        self.stages = whole_rows(shapes, devices)
        if self.stages:
            held = jnp.concatenate([shard.reshape(-1, LANES) for shard in shards])
            self.held = jnp.pad(held, ((0, -held.shape[0] % 16), (0, 0)))

    def line_stage(self, other):
        if not self.stages:
            return other
        _, line = masks_of(self.devices)
        self.held, other = tied(self.held, other)
        self.arrived = [self.held] + [swap(self.held, mask, self.devices) for mask in line[1:]]
        return other

    def plane_stage(self, other):
        if not self.stages:
            return other
        plane, _ = masks_of(self.devices)
        self.held, other = tied(jnp.stack(self.arrived), other)
        self.arrived = [self.held] + [swap(self.held, mask, self.devices) for mask in plane[1:]]
        self.origins = [(0, at, 0) for at in range(len(plane))]
        return other

    def first_half_stage(self, other):
        if not self.stages:
            return other
        plane, _ = masks_of(self.devices)
        cut = self.arrived[0].shape[0] // 2
        halves = [
            jnp.stack([field[at : at + cut] for field in self.arrived]) for at in (0, cut)
        ]
        halves, other = tied(halves, other)
        self.arrived = [
            [half, swap(half, mask, self.devices)] for half, mask in zip(halves, plane[1:3])
        ]
        return other

    def second_half_stage(self, other):
        if not self.stages:
            return other
        plane, _ = masks_of(self.devices)
        pairs, other = tied(self.arrived, other)
        cut = pairs[0][0].shape[1]
        self.arrived, self.origins = [], []
        for at, pair in enumerate(pairs):
            near, far = (1, 2) if at == 0 else (2, 1)
            self.arrived += pair + [swap(field, plane[far], self.devices) for field in pair]
            self.origins += [(0, where, at * cut) for where in (0, near, far, 3)]
        return other

    def core_stage(self, other, joined):
        if not self.stages:
            return other
        self.arrived, other = tied(self.arrived, other)
        if joined:
            self.arrived, self.origins = [jnp.concatenate(self.arrived)], [(0, 0, 0)]
        self.origins += [(1, where, offset) for _, where, offset in self.origins]
        self.got = [swap(field, CORE_MASK, self.devices) for field in self.arrived]
        return other

    def result(self, joined):
        if not self.stages:
            mats = [
                lax.all_gather(shard, "dp", axis=0, tiled=True).reshape(shape)
                for shard, shape in zip(self.shards, self.shapes)
            ]
            if not joined:
                return mats
            pads = [((0, 0), (0, tiles_of(mat.shape[1]) * LANES - mat.shape[1])) for mat in mats]
            return [jnp.concatenate([jnp.pad(mat, pad) for mat, pad in zip(mats, pads)], 1)]
        pieces = self.arrived + self.got
        return unpack_pieces(
            place_of(), pieces, tuple(self.origins), self.shapes, self.devices, joined
        )


def tied(first, second):
    return lax.optimization_barrier((first, second))


class GradSum:
    def __init__(self, grads, shapes, devices, extra=None):
        self.grads, self.shapes, self.devices, self.extra = grads, shapes, devices, extra
        self.stages = whole_rows(shapes, devices)
        if self.stages:
            self.kept, self.sent = pack_grads(place_of(), grads, shapes, devices, extra)

    def core_stage(self, other):
        if not self.stages:
            return other
        (self.kept, self.sent), other = tied((self.kept, self.sent), other)
        self.got = swap(self.sent, CORE_MASK, self.devices)
        return other

    def plane_stage(self, other):
        if not self.stages:
            return other
        plane, _ = masks_of(self.devices)
        block = self.kept.shape[0] // len(plane)
        cuts = [slice(at * block, (at + 1) * block) for at in range(len(plane))]
        parts = [(widen(self.kept[cut]) + widen(self.got[cut])).astype(jnp.bfloat16) for cut in cuts]
        self.parts, other = tied(parts, other)
        self.arrived = [
            swap(part, mask, self.devices) for part, mask in zip(self.parts[1:], plane[1:])
        ]
        return other

    def line_stage(self, other):
        if not self.stages:
            return other
        _, line = masks_of(self.devices)
        terms = [self.parts[0]] + self.arrived
        parts = [
            tree_sum([widen(term[at]) for term in terms]).astype(jnp.bfloat16)
            for at in range(len(line))
        ]
        self.parts, other = tied(parts, other)
        self.arrived = [
            swap(part, mask, self.devices) for part, mask in zip(self.parts[1:], line[1:])
        ]
        return other

    def result(self):
        if not self.stages:
            grads = [
                grad.swapaxes(0, 1).reshape(rows, -1)[:, :wide] if grad.ndim == 3 else grad
                for grad, (rows, wide) in zip(self.grads, self.shapes)
            ]
            sums = [
                lax.psum_scatter(grad.reshape(-1), "dp", scatter_dimension=0, tiled=True)
                for grad in grads
            ]
            return sums if self.extra is None else sums + [lax.psum(self.extra, "dp")]
        pieces = tree_sum([widen(term) for term in [self.parts[0]] + self.arrived])
        sums, start = [], 0
        for rows, wide in self.shapes:
            count = rows * wide // (self.devices * LANES)
            sums.append(pieces[start : start + count].reshape(-1))
            start += count
        if self.extra is not None:
            count = self.extra.size // LANES
            sums.append(pieces[start : start + count].reshape(self.extra.shape))
        return sums


def body(tokens, cotangent, w_query, w_key, w_value, w_out, w_gate, w_up, w_down, norm_gains):
    model_width = tokens.shape[1]
    seq_count = tokens.shape[0] // LENGTH
    group_size = HEADS // KV_HEADS
    scale_factor = HEAD_DIM ** (-0.5)
    gain_f = norm_gains.astype(jnp.float32)
    shards = (w_query, w_key, w_value, w_out, w_gate, w_up, w_down)
    devices = lax.axis_size("dp")
    widths = [shards[at].shape[0] * devices // model_width for at in range(6)]
    shapes = [(model_width, wide) for wide in widths] + [
        (shards[6].shape[0] * devices // model_width, model_width)
    ]
    first = WeightGather(shards[:3], shapes[:3], devices)
    rest = (4, 5, 6, 3)
    second = WeightGather(
        [shards[at] for at in rest], [shapes[at] for at in rest], devices
    )
    tokens = first.line_stage(tokens)
    if first.stages:
        first.arrived[1] = second.line_stage(first.arrived[1])
    tokens = first.plane_stage(tokens)
    tokens = first.core_stage(tokens, True)
    if first.stages:
        first.got = second.first_half_stage(first.got)
    (wide_mat,) = first.result(True)
    resid_in = tokens.astype(jnp.float32)
    cosine, sine = rotary_tables(LENGTH, HEAD_DIM)
    pairs = LANES // HEAD_DIM
    cosine = jnp.tile(cosine, (seq_count, 2 * pairs))
    sine = jnp.tile(jnp.concatenate([sine, -sine], 1), (seq_count, pairs))
    fields = project(tokens, gain_f, wide_mat, cosine, sine)
    fields = second.second_half_stage(fields)
    attended = [attend(fields, head, group_size) for head in range(2)]
    fields, attended = second.core_stage((fields, attended), False)
    attended.append(attend(fields, 2, group_size))
    wg_mat, wu_mat, wd_mat, wo_mat = second.result(False)
    mixed = jnp.concatenate([part for part, _ in attended], 1)
    attn_out = jnp.dot(mixed, wo_mat, preferred_element_type=jnp.float32)
    middle = resid_in + attn_out
    normed_two, rms_two = normalize(middle, gain_f[1])
    normed_two = normed_two.astype(jnp.bfloat16)
    gate = jnp.dot(normed_two, wg_mat, preferred_element_type=jnp.float32)
    upward = jnp.dot(normed_two, wu_mat, preferred_element_type=jnp.float32)
    sigmoid_g = jax.nn.sigmoid(gate)
    activated = gate * sigmoid_g
    hidden = (activated * upward).astype(jnp.bfloat16)
    ffn_out = jnp.dot(hidden, wd_mat, preferred_element_type=jnp.float32)
    output = (middle + ffn_out).astype(jnp.bfloat16)
    grad_down = outer_prod(hidden, cotangent)
    hidden_back = times_transposed(cotangent, wd_mat)
    gate_back = (hidden_back * upward * sigmoid_g * (1.0 + gate * (1.0 - sigmoid_g))).astype(
        jnp.bfloat16
    )
    up_back = (hidden_back * activated).astype(jnp.bfloat16)
    grad_gate = outer_prod(normed_two, gate_back)
    grad_up = outer_prod(normed_two, up_back)
    two_back = times_transposed(gate_back, wg_mat) + times_transposed(up_back, wu_mat)
    norm_two_back, gain_two = normalize_back(two_back, middle, rms_two, gain_f[1])
    mid_back = cotangent.astype(jnp.float32) + norm_two_back
    mid_low = mid_back.astype(jnp.bfloat16)
    grad_out = outer_prod(mixed, mid_low)
    mixed_back = times_transposed(mid_low, wo_mat).astype(jnp.bfloat16)
    feed_sum = GradSum(
        (grad_gate, grad_up, grad_down, grad_out), [shapes[at] for at in rest], devices
    )

    def back_of(head, field):
        part, total = attended[head]
        return attend_back(fields, field, part, total, head, group_size)

    mixed_back = feed_sum.core_stage(mixed_back)
    backs = [back_of(0, mixed_back)]
    mixed_back, _ = tied(mixed_back, backs[0])
    mixed_back = feed_sum.plane_stage(mixed_back)
    backs += [back_of(head, mixed_back) for head in range(1, KV_HEADS)]
    input_grad, tiled, gain_one = finish(tokens, gain_f, wide_mat, cosine, sine, mid_back, backs)
    input_grad, tiled = feed_sum.line_stage((input_grad, tiled))
    gains_back = jnp.concatenate([gain_one, gain_two[None]], 0)
    cuts = [0]
    for _, wide in shapes[:3]:
        cuts.append(cuts[-1] + tiles_of(wide))
    grads = tuple(tiled[start:stop] for start, stop in zip(cuts, cuts[1:]))
    mix_sum = GradSum(grads, shapes[:3], devices, gains_back)
    input_grad = mix_sum.core_stage(input_grad)
    input_grad = mix_sum.plane_stage(input_grad)
    if feed_sum.stages:
        feed_sum.arrived = mix_sum.line_stage(feed_sum.arrived)
    mix_parts = mix_sum.result()
    gate_part, up_part, down_part, out_part = feed_sum.result()
    all_parts = mix_parts[:3] + [out_part, gate_part, up_part, down_part]
    gain_grad = mix_parts[3]
    return (output, input_grad) + tuple(all_parts) + (gain_grad,)


def solution(mesh):
    return jax.shard_map(
        body,
        mesh=mesh,
        in_specs=(
            P("dp", None),
            P("dp", None),
            P("dp"),
            P("dp"),
            P("dp"),
            P("dp"),
            P("dp"),
            P("dp"),
            P("dp"),
            P(),
        ),
        out_specs=(
            P("dp", None),
            P("dp", None),
            P("dp"),
            P("dp"),
            P("dp"),
            P("dp"),
            P("dp"),
            P("dp"),
            P("dp"),
            P(),
        ),
        check_vma=False,
    )
```

profile of v0, /device:TPU:0, one launch (start us, length us, event | category | flops | bytes accessed | tf_op | source)
XLA Modules:
  0.0 253.2 jit_solution(16702547486606102415)
XLA Ops:
  1.4 3.1 %collective-permute-start = (bf16[144,128]{1,0:T(8,128)(2,1)S(1)}, bf16[144,128]{1,0:T(8,128)(2,1)S(1)}, u32[]{:S(2)}, u32[]{:S(2)}) collective-permute-start(bf16[144,128]{1,0:T(8,128)(2,1)S(1)} %fusion.31), channel_id=1, source_target_pairs={{0,8},{1,9},{2,10},{3,11},{4,12},{5,13},{6,14},{7,15},{8,0},{9,1},... | collective-permute-start | bytes 110600 | tf_op jit(solution)/shard_map/ppermute | solution.py:32
  4.5 2.5 collective-permute-start.2
  8.0 2.7 %collective-permute-done.2 = bf16[144,128]{1,0:T(8,128)(2,1)S(1)} collective-permute-done((bf16[144,128]{1,0:T(8,128)(2,1)S(1)}, bf16[144,128]{1,0:T(8,128)(2,1)S(1)}, u32[]{:S(2)}, u32[]{:S(2)}) %collective-permute-start.2) | collective-permute-done | bytes 36896 | tf_op jit(solution)/shard_map/ppermute | solution.py:32
  10.8 1.5 collective-permute-done.1
  12.3 1.6 collective-permute-start.3
  13.8 1.5 collective-permute-start.4
  16.2 1.6 collective-permute-start.7
  17.9 1.2 collective-permute-done.3
  19.0 1.3 collective-permute-start.8
  20.3 1.5 collective-permute-done.4
  22.0 1.1 collective-permute-done.6
  23.1 8.1 %collective-permute-done.7 = bf16[736,128]{1,0:T(8,128)(2,1)S(1)} collective-permute-done((bf16[736,128]{1,0:T(8,128)(2,1)S(1)}, bf16[736,128]{1,0:T(8,128)(2,1)S(1)}, u32[]{:S(2)}, u32[]{:S(2)}) %collective-permute-start.7) | collective-permute-done | bytes 188448 | tf_op jit(solution)/shard_map/ppermute | solution.py:32
  32.3 1.5 collective-permute-start.10
  33.8 1.5 collective-permute-start.11
  38.0 1.3 convert_element_type.307.gains_ref
  39.3 1.4 copy.33.tokens_ref
  40.7 3.4 %unpack.2.wide_ref = bf16[576,1152]{1,0:T(8,128)(2,1)} custom-call(s32[1]{0:T(128)} %bitcast.19.place_ref, bf16[16,144,128]{2,1,0:T(8,128)(2,1)} %copy-done.9, bf16[16,144,128]{2,1,0:T(8,128)(2,1)} %copy-done.10), custom_call_target="tpu_custom_call" | custom-call | flops 100000000 | bytes 1000000 | tf_op jit(solution)/shard_map/unpack/pallas_call | solution.py:144
  44.2 6.2 %project.1.fields_ref = bf16[1024,1152]{1,0:T(8,128)(2,1)} custom-call(bf16[1024,576]{1,0:T(8,128)(2,1)} %copy.33.tokens_ref, f32[2,576]{1,0:T(2,128)} %convert_element_type.307.gains_ref, bf16[576,1152]{1,0:T(8,128)(2,1)} %unpack.2.wide_ref, f32[1024,128]{1,0:T(8,128)} %copy.35.cosine_ref, f32[1024,128]{1,0:T(8,128)} %copy.36.sine_ref), custom_call_target="tpu_custom_call" | custom-call | flops 100000000 | bytes 1000000 | tf_op jit(solution)/shard_map/project/pallas_call | solution.py:456
  51.0 1.5 collective-permute-start.13
  53.0 1.5 collective-permute-start.15
  54.5 7.2 %attend.3 = (bf16[1024,192]{1,0:T(8,128)(2,1)}, f32[1024,128]{1,0:T(8,128)}) custom-call(bf16[1024,1152]{1,0:T(8,128)(2,1)} %project.1.fields_ref), custom_call_target="tpu_custom_call" | custom-call | flops 100000000 | bytes 1000000 | tf_op jit(solution)/shard_map/attend/pallas_call | solution.py:323
  61.7 7.6 %attend.4 = (bf16[1024,192]{1,0:T(8,128)(2,1)}, f32[1024,128]{1,0:T(8,128)}) custom-call(bf16[1024,1152]{1,0:T(8,128)(2,1)} %project.1.fields_ref), custom_call_target="tpu_custom_call" | custom-call | flops 100000000 | bytes 1000000 | tf_op jit(solution)/shard_map/attend/pallas_call | solution.py:323
  71.8 1.5 collective-permute-done.18.refs_10_
  75.5 7.2 %attend.5 = (bf16[1024,192]{1,0:T(8,128)(2,1)}, f32[1024,128]{1,0:T(8,128)}) custom-call(bf16[1024,1152]{1,0:T(8,128)(2,1)} %project.1.fields_ref), custom_call_target="tpu_custom_call" | custom-call | flops 100000000 | bytes 1000000 | tf_op jit(solution)/shard_map/attend/pallas_call | solution.py:323
  82.7 7.1 %unpack.3 = (bf16[576,1536]{1,0:T(8,128)(2,1)}, bf16[576,1536]{1,0:T(8,128)(2,1)}, bf16[1536,576]{1,0:T(8,128)(2,1)}, bf16[576,576]{1,0:T(8,128)(2,1)}) custom-call(s32[1]{0:T(128)} %bitcast.19.place_ref, bf16[4,368,128]{2,1,0:T(8,128)(2,1)} %copy-done.4, bf16[4,368,128]{2,1,0:T(8,128)(2,1)} %copy-done.14, bf16[4,368,128]{2,1,0:T(8,128)(2,1)} %copy-done.15, ...), custom_call_target="tpu_custom_call" | custom-call | flops 100000000 | bytes 1000000 | tf_op jit(solution)/shard_map/unpack/pallas_call | solution.py:144
  89.9 2.5 %multiply_reduce_fusion.2 = (f32[1024]{0:T(1024)S(1)}, f32[1024,576]{1,0:T(8,128)S(1)}) fusion(bf16[576,576]{1,0:T(8,128)(2,1)} %get-tuple-element.130, bf16[1024,192]{1,0:T(8,128)(2,1)S(1)} %copy-done.13, bf16[1024,192]{1,0:T(8,128)(2,1)S(1)} %copy-done.11, bf16[1024,192]{1,0:T(8,128)(2,1)S(1)} %copy-done.12, bf16[1024,576]{1,0:T(8,128)(2,1)S(1)} %copy-done), kind=kOutput, calls=%fused_computation.14 | convolution fusion | flops 685374464 | bytes 5386240 | tf_op jit(solution)/shard_map/dot_general | solution.py:780
  92.8 1.1 copy-done.24
  93.9 4.5 %fusion.36 = f32[1024,1536]{1,0:T(8,128)} fusion(bf16[1024,576]{1,0:T(8,128)(2,1)S(1)} %multiply_convert_fusion.1, bf16[576,1536]{1,0:T(8,128)(2,1)S(1)} %copy-done.24), kind=kOutput, calls=%fused_computation.100 | convolution fusion | flops 1811939328 | bytes 9240576 | tf_op jit(solution)/shard_map/dot_general | solution.py:785
  98.4 4.5 %fusion.35 = f32[1024,1536]{1,0:T(8,128)} fusion(bf16[1024,576]{1,0:T(8,128)(2,1)S(1)} %multiply_convert_fusion.1, bf16[576,1536]{1,0:T(8,128)(2,1)S(1)} %copy-done.23), kind=kOutput, calls=%fused_computation.99 | convolution fusion | flops 1811939328 | bytes 9240576 | tf_op jit(solution)/shard_map/dot_general | solution.py:784
  103.0 9.7 %fusion.3 = (bf16[1024,1536]{1,0:T(8,128)(2,1)S(1)}, bf16[1024,1536]{1,0:T(8,128)(2,1)S(1)}, bf16[1024,1536]{1,0:T(8,128)(2,1)}) fusion(f32[1024,1536]{1,0:T(8,128)} %fusion.35, f32[1024,1536]{1,0:T(8,128)} %fusion.36, bf16[1536,576]{1,0:T(8,128)(2,1)S(1)} %copy-done.21, bf16[1024,576]{0,1:T(8,128)(2,1)S(1)} %copy-done.8), kind=kOutput, calls=%fused_computation.5 | convolution fusion | flops 1835532288 | bytes 24969216 | tf_op jit(solution)/shard_map/dot_general | solution.py:580
  112.7 2.6 %fusion.40 = f32[1024,576]{1,0:T(8,128)S(1)} fusion(bf16[1024,1536]{1,0:T(8,128)(2,1)S(1)} %get-tuple-element.202, bf16[576,1536]{1,0:T(8,128)(2,1)S(1)} %copy-done.24), kind=kOutput, calls=%fused_computation.104 | convolution fusion | flops 1811939328 | bytes 7274496 | tf_op jit(solution)/shard_map/dot_general | solution.py:580
  115.3 3.0 %multiply_reduce_fusion = (f32[576]{0:T(1024)S(1)}, f32[1024]{0:T(1024)S(1)}, f32[1024,576]{1,0:T(8,128)S(1)}) fusion(f32[1024,576]{1,0:T(8,128)S(1)} %get-tuple-element.242, f32[1024]{0:T(1024)S(1)} %get-tuple-element.237, f32[576]{0:T(1024)S(1)} %copy-done.20, f32[1024,576]{1,0:T(8,128)S(1)} %fusion.40, bf16[1024,1536]{1,0:T(8,128)(2,1)S(1)} %get-tuple-element.203, ...), kind=kOutput, calls=%fused_computation.9 | convolution fusion | flops 1816066560 | bytes 12005888 | tf_op jit(solution)/shard_map/dot_general | solution.py:580
  118.4 1.1 subtract_add_fusion.mid_back_ref
  119.5 2.4 convolution_convert_fusion.back_ref
  121.9 2.5 fusion.6.refs_3_
  124.4 3.8 %fusion.38.refs_1_ = f32[576,1536]{1,0:T(8,128)} fusion(bf16[1024,576]{1,0:T(8,128)(2,1)S(1)} %multiply_convert_fusion.1, bf16[1024,1536]{1,0:T(8,128)(2,1)S(1)} %get-tuple-element.202), kind=kOutput, calls=%fused_computation.102 | convolution fusion | flops 1811939328 | bytes 7864320 | tf_op jit(solution)/shard_map/dot_general | solution.py:574
  128.3 3.9 %fusion.37.refs_0_ = f32[576,1536]{1,0:T(8,128)} fusion(bf16[1024,576]{1,0:T(8,128)(2,1)S(1)} %multiply_convert_fusion.1, bf16[1024,1536]{1,0:T(8,128)(2,1)S(1)} %get-tuple-element.203), kind=kOutput, calls=%fused_computation.101 | convolution fusion | flops 1811939328 | bytes 7864320 | tf_op jit(solution)/shard_map/dot_general | solution.py:574
  132.1 4.6 %fusion.39.refs_2_ = f32[1536,576]{1,0:T(8,128)} fusion(bf16[1024,1536]{1,0:T(8,128)(2,1)S(1)} %copy-done.26, bf16[1024,576]{0,1:T(8,128)(2,1)S(1)} %copy-done.8), kind=kOutput, calls=%fused_computation.103 | convolution fusion | flops 1811939328 | bytes 7864320 | tf_op jit(solution)/shard_map/dot_general | solution.py:574
  136.8 10.3 %pack.2 = (bf16[16,736,128]{2,1,0:T(8,128)(2,1)}, bf16[16,736,128]{2,1,0:T(8,128)(2,1)}) custom-call(s32[1]{0:T(128)} %bitcast.19.place_ref, f32[576,1536]{1,0:T(8,128)} %fusion.37.refs_0_, f32[576,1536]{1,0:T(8,128)} %fusion.38.refs_1_, f32[1536,576]{1,0:T(8,128)} %fusion.39.refs_2_, f32[576,576]{1,0:T(8,128)} %fusion.6.refs_3_), custom_call_target="tpu_custom_call" | custom-call | flops 100000000 | bytes 1000000 | tf_op jit(solution)/shard_map/pack/pallas_call | solution.py:243
  147.5 10.8 %attend_back.3 = (f32[1024,192]{1,0:T(8,128)}, f32[1024,128]{1,0:T(8,128)}) custom-call(bf16[1024,1152]{1,0:T(8,128)(2,1)} %project.1.fields_ref, bf16[1024,576]{1,0:T(8,128)(2,1)} %convolution_convert_fusion.back_ref, bf16[1024,192]{1,0:T(8,128)(2,1)} %get-tuple-element.118.mixed_ref, f32[1024,128]{1,0:T(8,128)} %get-tuple-element.139.total_ref), custom_call_target="tpu_custom_call" | custom-call | flops 100000000 | bytes 1000000 | tf_op jit(solution)/shard_map/attend_back/pallas_call | solution.py:399
  158.3 3.5 %add_convert_fusion.1 = (bf16[4,736,128]{2,1,0:T(8,128)(2,1)S(1)}, bf16[4,736,128]{2,1,0:T(8,128)(2,1)S(1)}, bf16[4,736,128]{2,1,0:T(8,128)(2,1)}, bf16[4,736,128]{2,1,0:T(8,128)(2,1)S(1)}) fusion(bf16[16,736,128]{2,1,0:T(8,128)(2,1)} %collective-permute-done.24, bf16[16,736,128]{2,1,0:T(8,128)(2,1)S(1)} %copy-done.2), kind=kLoop, calls=%fused_computation.18 | loop fusion | flops 6029312 | bytes 9043968 | tf_op jit(solution)/shard_map/convert_element_type | solution.py:698
  162.9 2.5 collective-permute-start.27
  165.3 11.1 %attend_back.5 = (f32[1024,192]{1,0:T(8,128)}, f32[1024,128]{1,0:T(8,128)}) custom-call(bf16[1024,1152]{1,0:T(8,128)(2,1)} %project.1.fields_ref, bf16[1024,576]{1,0:T(8,128)(2,1)} %convolution_convert_fusion.back_ref, bf16[1024,192]{1,0:T(8,128)(2,1)} %get-tuple-element.121.mixed_ref, f32[1024,128]{1,0:T(8,128)} %get-tuple-element.151.total_ref), custom_call_target="tpu_custom_call" | custom-call | flops 100000000 | bytes 1000000 | tf_op jit(solution)/shard_map/attend_back/pallas_call | solution.py:399
  176.4 10.7 %attend_back.4 = (f32[1024,192]{1,0:T(8,128)}, f32[1024,128]{1,0:T(8,128)}) custom-call(bf16[1024,1152]{1,0:T(8,128)(2,1)} %project.1.fields_ref, bf16[1024,576]{1,0:T(8,128)(2,1)} %convolution_convert_fusion.back_ref, bf16[1024,192]{1,0:T(8,128)(2,1)} %get-tuple-element.119.mixed_ref, f32[1024,128]{1,0:T(8,128)} %get-tuple-element.148.total_ref), custom_call_target="tpu_custom_call" | custom-call | flops 100000000 | bytes 1000000 | tf_op jit(solution)/shard_map/attend_back/pallas_call | solution.py:399
  187.2 12.8 %finish.1 = (bf16[1024,576]{1,0:T(8,128)(2,1)}, f32[9,576,128]{2,1,0:T(8,128)}, f32[1,576]{1,0:T(1,128)}) custom-call(bf16[1024,576]{1,0:T(8,128)(2,1)} %copy.33.tokens_ref, f32[2,576]{1,0:T(2,128)} %convert_element_type.307.gains_ref, bf16[576,1152]{1,0:T(8,128)(2,1)} %unpack.2.wide_ref, f32[1024,128]{1,0:T(8,128)} %copy.35.cosine_ref, ...), custom_call_target="tpu_custom_call" | custom-call | flops 100000000 | bytes 1000000 | tf_op jit(solution)/shard_map/finish/pallas_call | solution.py:456
  200.0 1.4 pad_maximum_fusion.9.refs_3_
  201.8 1.2 slice.238.refs_0_
  203.1 1.1 fusion.34
  204.2 4.1 %pack.3 = (bf16[16,144,128]{2,1,0:T(8,128)(2,1)}, bf16[16,144,128]{2,1,0:T(8,128)(2,1)}) custom-call(s32[1]{0:T(128)} %bitcast.19.place_ref, f32[5,576,128]{2,1,0:T(8,128)} %slice.238.refs_0_, f32[2,576,128]{2,1,0:T(8,128)} %get-tuple-element.214.refs_1_, f32[2,576,128]{2,1,0:T(8,128)} %get-tuple-element.213.refs_2_, f32[2,576]{1,0:T(2,128)} %pad_maximum_fusion.9.refs_3_), custom_call_target="tpu_custom_call" | custom-call | flops 100000000 | bytes 1000000 | tf_op jit(solution)/shard_map/pack/pallas_call | solution.py:243
  208.2 2.2 collective-permute-done.28
  210.4 2.0 add_convert_fusion.9
  213.4 2.5 collective-permute-start.31
  215.9 4.5 %add_convert_fusion = bf16[1024,576]{1,0:T(8,128)(2,1)S(1)} fusion(f32[1024,576]{1,0:T(8,128)S(1)} %get-tuple-element.242, bf16[1024,1536]{1,0:T(8,128)(2,1)} %get-tuple-element.204, bf16[1536,576]{1,0:T(8,128)(2,1)S(1)} %copy-done.22), kind=kOutput, calls=%fused_computation.12 | convolution fusion | flops 1813118976 | bytes 8454144 | tf_op jit(solution)/shard_map/dot_general | solution.py:789
  220.4 1.4 copy.48
  221.8 2.5 %collective-permute-start.32 = (bf16[736,128]{1,0:T(8,128)(2,1)S(1)}, bf16[736,128]{1,0:T(8,128)(2,1)S(1)}, u32[]{:S(2)}, u32[]{:S(2)}) collective-permute-start(bf16[736,128]{1,0:T(8,128)(2,1)S(1)} %get-tuple-element.169), channel_id=1, source_target_pairs={{0,8},{1,9},{2,10},{3,11},{4,12},{5,13},{6,14},{7,15},{8,0},{9,1},... | collective-permute-start | bytes 565256 | tf_op jit(solution)/shard_map/ppermute | solution.py:32
  225.2 1.4 copy.49
  226.6 1.6 collective-permute-start.34
  228.2 1.1 fusion.29
  229.2 1.9 collective-permute-done.32
  231.2 9.8 %collective-permute-done.33 = bf16[736,128]{1,0:T(8,128)(2,1)S(1)} collective-permute-done((bf16[736,128]{1,0:T(8,128)(2,1)S(1)}, bf16[736,128]{1,0:T(8,128)(2,1)S(1)}, u32[]{:S(2)}, u32[]{:S(2)}) %collective-permute-start.33) | collective-permute-done | bytes 188448 | tf_op jit(solution)/shard_map/ppermute | solution.py:32
  241.8 2.7 %collective-permute-start.35 = (bf16[144,128]{1,0:T(8,128)(2,1)S(1)}, bf16[144,128]{1,0:T(8,128)(2,1)S(1)}, u32[]{:S(2)}, u32[]{:S(2)}) collective-permute-start(bf16[144,128]{1,0:T(8,128)(2,1)S(1)} %get-tuple-element.173), channel_id=1, source_target_pairs={{0,8},{1,9},{2,10},{3,11},{4,12},{5,13},{6,14},{7,15},{8,0},{9,1},... | collective-permute-start | bytes 110600 | tf_op jit(solution)/shard_map/ppermute | solution.py:32
  245.3 1.6 collective-permute-start.37
  247.5 2.0 collective-permute-done.36
  249.5 1.6 collective-permute-done.37
  (135 shorter events, 20.5 us)
Async XLA Ops:
  1.4 6.6 %collective-permute-start = (bf16[144,128]{1,0:T(8,128)(2,1)S(1)}, bf16[144,128]{1,0:T(8,128)(2,1)S(1)}, u32[]{:S(2)}, u32[]{:S(2)}) collective-permute-start(bf16[144,128]{1,0:T(8,128)(2,1)S(1)} %fusion.31), channel_id=1, source_target_pairs={{0,8},{1,9},{2,10},{3,11},{4,12},{5,13},{6,14},{7,15},{8,0},{9,1},... | collective-permute-start | bytes 110600 | tf_op jit(solution)/shard_map/ppermute | solution.py:32
  4.5 6.2 %collective-permute-start.2 = (bf16[144,128]{1,0:T(8,128)(2,1)S(1)}, bf16[144,128]{1,0:T(8,128)(2,1)S(1)}, u32[]{:S(2)}, u32[]{:S(2)}) collective-permute-start(bf16[144,128]{1,0:T(8,128)(2,1)S(1)} %fusion.31), channel_id=1, source_target_pairs={{0,24},{1,25},{2,26},{3,27},{4,28},{5,29},{6,30},{7,31},{8,16},{9,... | collective-permute-start | bytes 110600 | tf_op jit(solution)/shard_map/ppermute | solution.py:32
  7.0 5.3 %collective-permute-start.1 = (bf16[144,128]{1,0:T(8,128)(2,1)S(1)}, bf16[144,128]{1,0:T(8,128)(2,1)S(1)}, u32[]{:S(2)}, u32[]{:S(2)}) collective-permute-start(bf16[144,128]{1,0:T(8,128)(2,1)S(1)} %fusion.31), channel_id=1, source_target_pairs={{0,16},{1,17},{2,18},{3,19},{4,20},{5,21},{6,22},{7,23},{8,24},{9,... | collective-permute-start | bytes 110600 | tf_op jit(solution)/shard_map/ppermute | solution.py:32
  12.3 6.7 %collective-permute-start.3 = (bf16[4,144,128]{2,1,0:T(8,128)(2,1)S(1)}, bf16[4,144,128]{2,1,0:T(8,128)(2,1)S(1)}, u32[]{:S(2)}, u32[]{:S(2)}) collective-permute-start(bf16[4,144,128]{2,1,0:T(8,128)(2,1)S(1)} %pad_maximum_fusion.8), channel_id=1, source_target_pairs={{0,2},{1,3},{2,0},{3,1},{4,6},{5,7},{6,4},{7,5},{8,10},{9,11},{10,... | collective-permute-start | bytes 442376 | tf_op jit(solution)/shard_map/ppermute | solution.py:32
  13.8 8.0 %collective-permute-start.4 = (bf16[4,144,128]{2,1,0:T(8,128)(2,1)S(1)}, bf16[4,144,128]{2,1,0:T(8,128)(2,1)S(1)}, u32[]{:S(2)}, u32[]{:S(2)}) collective-permute-start(bf16[4,144,128]{2,1,0:T(8,128)(2,1)S(1)} %pad_maximum_fusion.8), channel_id=1, source_target_pairs={{0,4},{1,5},{2,6},{3,7},{4,0},{5,1},{6,2},{7,3},{8,12},{9,13},{10,... | collective-permute-start | bytes 442376 | tf_op jit(solution)/shard_map/ppermute | solution.py:32
  15.3 6.5 %collective-permute-start.5 = (bf16[4,144,128]{2,1,0:T(8,128)(2,1)S(1)}, bf16[4,144,128]{2,1,0:T(8,128)(2,1)S(1)}, u32[]{:S(2)}, u32[]{:S(2)}) collective-permute-start(bf16[4,144,128]{2,1,0:T(8,128)(2,1)S(1)} %pad_maximum_fusion.8), channel_id=1, source_target_pairs={{0,6},{1,7},{2,4},{3,5},{4,2},{5,3},{6,0},{7,1},{8,14},{9,15},{10,... | collective-permute-start | bytes 442376 | tf_op jit(solution)/shard_map/ppermute | solution.py:32
  15.8 7.3 %collective-permute-start.6 = (bf16[736,128]{1,0:T(8,128)(2,1)S(1)}, bf16[736,128]{1,0:T(8,128)(2,1)S(1)}, u32[]{:S(2)}, u32[]{:S(2)}) collective-permute-start(bf16[736,128]{1,0:T(8,128)(2,1)S(1)} %fusion.19), channel_id=1, source_target_pairs={{0,8},{1,9},{2,10},{3,11},{4,12},{5,13},{6,14},{7,15},{8,0},{9,1},... | collective-permute-start | bytes 565256 | tf_op jit(solution)/shard_map/ppermute | solution.py:32
  16.2 15.1 %collective-permute-start.7 = (bf16[736,128]{1,0:T(8,128)(2,1)S(1)}, bf16[736,128]{1,0:T(8,128)(2,1)S(1)}, u32[]{:S(2)}, u32[]{:S(2)}) collective-permute-start(bf16[736,128]{1,0:T(8,128)(2,1)S(1)} %fusion.19), channel_id=1, source_target_pairs={{0,16},{1,17},{2,18},{3,19},{4,20},{5,21},{6,22},{7,23},{8,24},{9,... | collective-permute-start | bytes 565256 | tf_op jit(solution)/shard_map/ppermute | solution.py:32
  19.0 12.3 %collective-permute-start.8 = (bf16[736,128]{1,0:T(8,128)(2,1)S(1)}, bf16[736,128]{1,0:T(8,128)(2,1)S(1)}, u32[]{:S(2)}, u32[]{:S(2)}) collective-permute-start(bf16[736,128]{1,0:T(8,128)(2,1)S(1)} %fusion.19), channel_id=1, source_target_pairs={{0,24},{1,25},{2,26},{3,27},{4,28},{5,29},{6,30},{7,31},{8,16},{9,... | collective-permute-start | bytes 565256 | tf_op jit(solution)/shard_map/ppermute | solution.py:32
  21.9 15.0 %copy-start.9 = (bf16[16,144,128]{2,1,0:T(8,128)(2,1)}, bf16[16,144,128]{2,1,0:T(8,128)(2,1)S(1)}, u32[]{:S(2)}) copy-start(bf16[16,144,128]{2,1,0:T(8,128)(2,1)S(1)} %constant_dynamic-update-slice_fusion.refs_0_) | copy-start | bytes 1769476
  21.9 9.5 %collective-permute-start.9 = (bf16[16,144,128]{2,1,0:T(8,128)(2,1)S(1)}, bf16[16,144,128]{2,1,0:T(8,128)(2,1)S(1)}, u32[]{:S(2)}, u32[]{:S(2)}) collective-permute-start(bf16[16,144,128]{2,1,0:T(8,128)(2,1)S(1)} %constant_dynamic-update-slice_fusion.refs_0_), channel_id=1, source_target_pairs={{0,1},{1,0},{2,3},{3,2},{4,5},{5,4},{6,7},{7,6},{8,9},{9,8},{10,11... | collective-permute-start | bytes 1769480 | tf_op jit(solution)/shard_map/ppermute | solution.py:32
  31.3 8.0 %copy-start.7 = (bf16[1024,576]{0,1:T(8,128)(2,1)S(1)}, bf16[1024,576]{0,1:T(8,128)(2,1)}, u32[]{:S(2)}) copy-start(bf16[1024,576]{0,1:T(8,128)(2,1)} %param.10) | copy-start | bytes 3538948
  31.4 37.9 %copy-start.4 = (bf16[4,368,128]{2,1,0:T(8,128)(2,1)}, bf16[4,368,128]{2,1,0:T(8,128)(2,1)S(1)}, u32[]{:S(2)}) copy-start(bf16[4,368,128]{2,1,0:T(8,128)(2,1)S(1)} %get-tuple-element.122.refs_0_) | copy-start | bytes 1130500
  31.5 38.9 %copy-start.5 = (bf16[4,368,128]{2,1,0:T(8,128)(2,1)}, bf16[4,368,128]{2,1,0:T(8,128)(2,1)S(1)}, u32[]{:S(2)}) copy-start(bf16[4,368,128]{2,1,0:T(8,128)(2,1)S(1)} %get-tuple-element.126.refs_4_) | copy-start | bytes 1130500
  31.5 0.8 copy-start.10
  32.3 18.1 %collective-permute-start.10 = (bf16[4,368,128]{2,1,0:T(8,128)(2,1)S(1)}, bf16[4,368,128]{2,1,0:T(8,128)(2,1)S(1)}, u32[]{:S(2)}, u32[]{:S(2)}) collective-permute-start(bf16[4,368,128]{2,1,0:T(8,128)(2,1)S(1)} %get-tuple-element.122.refs_0_), channel_id=1, source_target_pairs={{0,2},{1,3},{2,0},{3,1},{4,6},{5,7},{6,4},{7,5},{8,10},{9,11},{10,... | collective-permute-start | bytes 1130504 | tf_op jit(solution)/shard_map/ppermute | solution.py:32
  33.8 16.6 %collective-permute-start.11 = (bf16[4,368,128]{2,1,0:T(8,128)(2,1)S(1)}, bf16[4,368,128]{2,1,0:T(8,128)(2,1)}, u32[]{:S(2)}, u32[]{:S(2)}) collective-permute-start(bf16[4,368,128]{2,1,0:T(8,128)(2,1)S(1)} %get-tuple-element.126.refs_4_), channel_id=1, source_target_pairs={{0,4},{1,5},{2,6},{3,7},{4,0},{5,1},{6,2},{7,3},{8,12},{9,13},{10,... | collective-permute-start | bytes 1130504 | tf_op jit(solution)/shard_map/ppermute | solution.py:32
  50.4 23.8 %copy-start.8 = (bf16[1024,576]{0,1:T(8,128)(2,1)S(1)}, bf16[1024,576]{0,1:T(8,128)(2,1)}, u32[]{:S(2)}) copy-start(bf16[1024,576]{0,1:T(8,128)(2,1)} %param.11) | copy-start | bytes 3538948
  50.4 24.5 %copy-start.14 = (bf16[4,368,128]{2,1,0:T(8,128)(2,1)}, bf16[4,368,128]{2,1,0:T(8,128)(2,1)S(1)}, u32[]{:S(2)}) copy-start(bf16[4,368,128]{2,1,0:T(8,128)(2,1)S(1)} %collective-permute-done.10.refs_1_) | copy-start | bytes 1130500
  50.4 18.9 %collective-permute-start.12 = (bf16[4,368,128]{2,1,0:T(8,128)(2,1)S(1)}, bf16[4,368,128]{2,1,0:T(8,128)(2,1)S(1)}, u32[]{:S(2)}, u32[]{:S(2)}) collective-permute-start(bf16[4,368,128]{2,1,0:T(8,128)(2,1)S(1)} %get-tuple-element.122.refs_0_), channel_id=1, source_target_pairs={{0,4},{1,5},{2,6},{3,7},{4,0},{5,1},{6,2},{7,3},{8,12},{9,13},{10,... | collective-permute-start | bytes 1130504 | tf_op jit(solution)/shard_map/ppermute | solution.py:32
  51.0 18.3 %collective-permute-start.13 = (bf16[4,368,128]{2,1,0:T(8,128)(2,1)S(1)}, bf16[4,368,128]{2,1,0:T(8,128)(2,1)}, u32[]{:S(2)}, u32[]{:S(2)}) collective-permute-start(bf16[4,368,128]{2,1,0:T(8,128)(2,1)S(1)} %collective-permute-done.10.refs_1_), channel_id=1, source_target_pairs={{0,4},{1,5},{2,6},{3,7},{4,0},{5,1},{6,2},{7,3},{8,12},{9,13},{10,... | collective-permute-start | bytes 1130504 | tf_op jit(solution)/shard_map/ppermute | solution.py:32
  52.5 16.8 %collective-permute-start.14 = (bf16[4,368,128]{2,1,0:T(8,128)(2,1)S(1)}, bf16[4,368,128]{2,1,0:T(8,128)(2,1)}, u32[]{:S(2)}, u32[]{:S(2)}) collective-permute-start(bf16[4,368,128]{2,1,0:T(8,128)(2,1)S(1)} %get-tuple-element.126.refs_4_), channel_id=1, source_target_pairs={{0,2},{1,3},{2,0},{3,1},{4,6},{5,7},{6,4},{7,5},{8,10},{9,11},{10,... | collective-permute-start | bytes 1130504 | tf_op jit(solution)/shard_map/ppermute | solution.py:32
  53.0 16.3 %collective-permute-start.15 = (bf16[4,368,128]{2,1,0:T(8,128)(2,1)}, bf16[4,368,128]{2,1,0:T(8,128)(2,1)}, u32[]{:S(2)}, u32[]{:S(2)}) collective-permute-start(bf16[4,368,128]{2,1,0:T(8,128)(2,1)} %collective-permute-done.11.refs_5_), channel_id=1, source_target_pairs={{0,2},{1,3},{2,0},{3,1},{4,6},{5,7},{6,4},{7,5},{8,10},{9,11},{10,... | collective-permute-start | bytes 1130504 | tf_op jit(solution)/shard_map/ppermute | solution.py:32
  61.7 13.1 %copy-start.19 = (f32[2,576]{1,0:T(2,128)S(1)}, f32[2,576]{1,0:T(2,128)}, u32[]{:S(2)}) copy-start(f32[2,576]{1,0:T(2,128)} %convert_element_type.307.gains_ref) | copy-start | bytes 13828
  69.3 4.0 %copy-start.15 = (bf16[4,368,128]{2,1,0:T(8,128)(2,1)}, bf16[4,368,128]{2,1,0:T(8,128)(2,1)S(1)}, u32[]{:S(2)}) copy-start(bf16[4,368,128]{2,1,0:T(8,128)(2,1)S(1)} %collective-permute-done.12.refs_2_) | copy-start | bytes 1130500
  69.3 1.8 collective-permute-start.16
  69.4 2.2 collective-permute-start.17
  69.9 3.3 %collective-permute-start.18 = (bf16[4,368,128]{2,1,0:T(8,128)(2,1)S(1)}, bf16[4,368,128]{2,1,0:T(8,128)(2,1)S(1)}, u32[]{:S(2)}, u32[]{:S(2)}) collective-permute-start(bf16[4,368,128]{2,1,0:T(8,128)(2,1)S(1)} %collective-permute-done.12.refs_2_), channel_id=1, source_target_pairs={{0,1},{1,0},{2,3},{3,2},{4,5},{5,4},{6,7},{7,6},{8,9},{9,8},{10,11... | collective-permute-start | bytes 1130504 | tf_op jit(solution)/shard_map/ppermute | solution.py:32
  70.0 12.7 %collective-permute-start.19 = (bf16[4,368,128]{2,1,0:T(8,128)(2,1)}, bf16[4,368,128]{2,1,0:T(8,128)(2,1)}, u32[]{:S(2)}, u32[]{:S(2)}) collective-permute-start(bf16[4,368,128]{2,1,0:T(8,128)(2,1)} %collective-permute-done.13.refs_3_), channel_id=1, source_target_pairs={{0,1},{1,0},{2,3},{3,2},{4,5},{5,4},{6,7},{7,6},{8,9},{9,8},{10,11... | collective-permute-start | bytes 1130504 | tf_op jit(solution)/shard_map/ppermute | solution.py:32
  70.4 12.3 %collective-permute-start.20 = (bf16[4,368,128]{2,1,0:T(8,128)(2,1)S(1)}, bf16[4,368,128]{2,1,0:T(8,128)(2,1)}, u32[]{:S(2)}, u32[]{:S(2)}) collective-permute-start(bf16[4,368,128]{2,1,0:T(8,128)(2,1)S(1)} %get-tuple-element.126.refs_4_), channel_id=1, source_target_pairs={{0,1},{1,0},{2,3},{3,2},{4,5},{5,4},{6,7},{7,6},{8,9},{9,8},{10,11... | collective-permute-start | bytes 1130504 | tf_op jit(solution)/shard_map/ppermute | solution.py:32
  71.1 2.2 copy-start.16
  71.1 11.6 %collective-permute-start.21 = (bf16[4,368,128]{2,1,0:T(8,128)(2,1)}, bf16[4,368,128]{2,1,0:T(8,128)(2,1)}, u32[]{:S(2)}, u32[]{:S(2)}) collective-permute-start(bf16[4,368,128]{2,1,0:T(8,128)(2,1)} %collective-permute-done.11.refs_5_), channel_id=1, source_target_pairs={{0,1},{1,0},{2,3},{3,2},{4,5},{5,4},{6,7},{7,6},{8,9},{9,8},{10,11... | collective-permute-start | bytes 1130504 | tf_op jit(solution)/shard_map/ppermute | solution.py:32
  71.6 1.6 copy-start.17
  71.6 11.1 %collective-permute-start.22 = (bf16[4,368,128]{2,1,0:T(8,128)(2,1)}, bf16[4,368,128]{2,1,0:T(8,128)(2,1)}, u32[]{:S(2)}, u32[]{:S(2)}) collective-permute-start(bf16[4,368,128]{2,1,0:T(8,128)(2,1)} %collective-permute-done.14.refs_6_), channel_id=1, source_target_pairs={{0,1},{1,0},{2,3},{3,2},{4,5},{5,4},{6,7},{7,6},{8,9},{9,8},{10,11... | collective-permute-start | bytes 1130504 | tf_op jit(solution)/shard_map/ppermute | solution.py:32
  74.0 8.7 %collective-permute-start.23 = (bf16[4,368,128]{2,1,0:T(8,128)(2,1)}, bf16[4,368,128]{2,1,0:T(8,128)(2,1)}, u32[]{:S(2)}, u32[]{:S(2)}) collective-permute-start(bf16[4,368,128]{2,1,0:T(8,128)(2,1)} %collective-permute-done.15.refs_7_), channel_id=1, source_target_pairs={{0,1},{1,0},{2,3},{3,2},{4,5},{5,4},{6,7},{7,6},{8,9},{9,8},{10,11... | collective-permute-start | bytes 1130504 | tf_op jit(solution)/shard_map/ppermute | solution.py:32
  82.7 7.2 %copy-start = (bf16[1024,576]{1,0:T(8,128)(2,1)S(1)}, bf16[1024,576]{1,0:T(8,128)(2,1)}, u32[]{:S(2)}) copy-start(bf16[1024,576]{1,0:T(8,128)(2,1)} %copy.33.tokens_ref) | copy-start | bytes 3538948
  82.7 7.2 %copy-start.11 = (bf16[1024,192]{1,0:T(8,128)(2,1)S(1)}, bf16[1024,192]{1,0:T(8,128)(2,1)}, u32[]{:S(2)}) copy-start(bf16[1024,192]{1,0:T(8,128)(2,1)} %get-tuple-element.119.mixed_ref) | copy-start | bytes 1179652
  82.7 7.2 %copy-start.12 = (bf16[1024,192]{1,0:T(8,128)(2,1)S(1)}, bf16[1024,192]{1,0:T(8,128)(2,1)}, u32[]{:S(2)}) copy-start(bf16[1024,192]{1,0:T(8,128)(2,1)} %get-tuple-element.118.mixed_ref) | copy-start | bytes 1179652
  82.7 7.2 %copy-start.13 = (bf16[1024,192]{1,0:T(8,128)(2,1)S(1)}, bf16[1024,192]{1,0:T(8,128)(2,1)}, u32[]{:S(2)}) copy-start(bf16[1024,192]{1,0:T(8,128)(2,1)} %get-tuple-element.121.mixed_ref) | copy-start | bytes 1179652
  89.9 2.6 %copy-start.20 = (f32[576]{0:T(1024)S(1)}, f32[576]{0:T(1024)}, u32[]{:S(2)}) copy-start(f32[576]{0:T(1024)} %slice_reduce_fusion) | copy-start | bytes 6916
  92.4 1.5 copy-start.24
  93.9 4.5 %copy-start.23 = (bf16[576,1536]{1,0:T(8,128)(2,1)S(1)}, bf16[576,1536]{1,0:T(8,128)(2,1)}, u32[]{:S(2)}) copy-start(bf16[576,1536]{1,0:T(8,128)(2,1)} %get-tuple-element.131) | copy-start | bytes 5308420
  98.4 4.6 %copy-start.21 = (bf16[1536,576]{1,0:T(8,128)(2,1)S(1)}, bf16[1536,576]{1,0:T(8,128)(2,1)}, u32[]{:S(2)}) copy-start(bf16[1536,576]{1,0:T(8,128)(2,1)} %get-tuple-element.133) | copy-start | bytes 5308420
  118.4 1.1 copy-start.25
  119.5 5.0 %copy-start.1 = (f32[1024,576]{1,0:T(8,128)}, f32[1024,576]{1,0:T(8,128)S(1)}, u32[]{:S(2)}) copy-start(f32[1024,576]{1,0:T(8,128)S(1)} %subtract_add_fusion.mid_back_ref) | copy-start | bytes 7077892
  128.3 3.9 %copy-start.26 = (bf16[1024,1536]{1,0:T(8,128)(2,1)S(1)}, bf16[1024,1536]{1,0:T(8,128)(2,1)}, u32[]{:S(2)}) copy-start(bf16[1024,1536]{1,0:T(8,128)(2,1)} %get-tuple-element.204) | copy-start | bytes 9437188
  147.1 11.2 %copy-start.2 = (bf16[16,736,128]{2,1,0:T(8,128)(2,1)S(1)}, bf16[16,736,128]{2,1,0:T(8,128)(2,1)}, u32[]{:S(2)}) copy-start(bf16[16,736,128]{2,1,0:T(8,128)(2,1)} %get-tuple-element.136) | copy-start | bytes 9043972
  147.1 11.2 %collective-permute-start.24 = (bf16[16,736,128]{2,1,0:T(8,128)(2,1)}, bf16[16,736,128]{2,1,0:T(8,128)(2,1)}, u32[]{:S(2)}, u32[]{:S(2)}) collective-permute-start(bf16[16,736,128]{2,1,0:T(8,128)(2,1)} %get-tuple-element.137), channel_id=1, source_target_pairs={{0,1},{1,0},{2,3},{3,2},{4,5},{5,4},{6,7},{7,6},{8,9},{9,8},{10,11... | collective-permute-start | bytes 9043976 | tf_op jit(solution)/shard_map/ppermute | solution.py:32
  161.8 39.6 %collective-permute-start.25 = (bf16[4,736,128]{2,1,0:T(8,128)(2,1)}, bf16[4,736,128]{2,1,0:T(8,128)(2,1)S(1)}, u32[]{:S(2)}, u32[]{:S(2)}) collective-permute-start(bf16[4,736,128]{2,1,0:T(8,128)(2,1)} %get-tuple-element.144), channel_id=1, source_target_pairs={{0,2},{1,3},{2,0},{3,1},{4,6},{5,7},{6,4},{7,5},{8,10},{9,11},{10,... | collective-permute-start | bytes 2261000 | tf_op jit(solution)/shard_map/ppermute | solution.py:32
  162.3 39.1 %collective-permute-start.26 = (bf16[4,736,128]{2,1,0:T(8,128)(2,1)S(1)}, bf16[4,736,128]{2,1,0:T(8,128)(2,1)S(1)}, u32[]{:S(2)}, u32[]{:S(2)}) collective-permute-start(bf16[4,736,128]{2,1,0:T(8,128)(2,1)S(1)} %get-tuple-element.145), channel_id=1, source_target_pairs={{0,4},{1,5},{2,6},{3,7},{4,0},{5,1},{6,2},{7,3},{8,12},{9,13},{10,... | collective-permute-start | bytes 2261000 | tf_op jit(solution)/shard_map/ppermute | solution.py:32
  162.9 38.6 %collective-permute-start.27 = (bf16[4,736,128]{2,1,0:T(8,128)(2,1)S(1)}, bf16[4,736,128]{2,1,0:T(8,128)(2,1)S(1)}, u32[]{:S(2)}, u32[]{:S(2)}) collective-permute-start(bf16[4,736,128]{2,1,0:T(8,128)(2,1)S(1)} %get-tuple-element.146), channel_id=1, source_target_pairs={{0,6},{1,7},{2,4},{3,5},{4,2},{5,3},{6,0},{7,1},{8,14},{9,15},{10,... | collective-permute-start | bytes 2261000 | tf_op jit(solution)/shard_map/ppermute | solution.py:32
  200.0 1.9 copy-start.3
  204.2 11.8 %copy-start.22 = (bf16[1536,576]{1,0:T(8,128)(2,1)S(1)}, bf16[1536,576]{1,0:T(8,128)(2,1)}, u32[]{:S(2)}) copy-start(bf16[1536,576]{1,0:T(8,128)(2,1)} %get-tuple-element.133) | copy-start | bytes 5308420
  208.2 2.2 collective-permute-start.28
  212.4 14.2 %collective-permute-start.29 = (bf16[4,144,128]{2,1,0:T(8,128)(2,1)}, bf16[4,144,128]{2,1,0:T(8,128)(2,1)}, u32[]{:S(2)}, u32[]{:S(2)}) collective-permute-start(bf16[4,144,128]{2,1,0:T(8,128)(2,1)} %get-tuple-element.166), channel_id=1, source_target_pairs={{0,2},{1,3},{2,0},{3,1},{4,6},{5,7},{6,4},{7,5},{8,10},{9,11},{10,... | collective-permute-start | bytes 442376 | tf_op jit(solution)/shard_map/ppermute | solution.py:32
  212.9 15.2 %collective-permute-start.30 = (bf16[4,144,128]{2,1,0:T(8,128)(2,1)}, bf16[4,144,128]{2,1,0:T(8,128)(2,1)}, u32[]{:S(2)}, u32[]{:S(2)}) collective-permute-start(bf16[4,144,128]{2,1,0:T(8,128)(2,1)} %get-tuple-element.167), channel_id=1, source_target_pairs={{0,4},{1,5},{2,6},{3,7},{4,0},{5,1},{6,2},{7,3},{8,12},{9,13},{10,... | collective-permute-start | bytes 442376 | tf_op jit(solution)/shard_map/ppermute | solution.py:32
  213.4 14.7 %collective-permute-start.31 = (bf16[4,144,128]{2,1,0:T(8,128)(2,1)}, bf16[4,144,128]{2,1,0:T(8,128)(2,1)}, u32[]{:S(2)}, u32[]{:S(2)}) collective-permute-start(bf16[4,144,128]{2,1,0:T(8,128)(2,1)} %get-tuple-element.168), channel_id=1, source_target_pairs={{0,6},{1,7},{2,4},{3,5},{4,2},{5,3},{6,0},{7,1},{8,14},{9,15},{10,... | collective-permute-start | bytes 442376 | tf_op jit(solution)/shard_map/ppermute | solution.py:32
  220.4 4.8 %copy-start.6 = (bf16[1024,576]{1,0:T(8,128)(2,1)S(1)}, bf16[1024,576]{1,0:T(8,128)(2,1)}, u32[]{:S(2)}) copy-start(bf16[1024,576]{1,0:T(8,128)(2,1)} %get-tuple-element.191) | copy-start | bytes 3538948
  221.8 9.3 %collective-permute-start.32 = (bf16[736,128]{1,0:T(8,128)(2,1)S(1)}, bf16[736,128]{1,0:T(8,128)(2,1)S(1)}, u32[]{:S(2)}, u32[]{:S(2)}) collective-permute-start(bf16[736,128]{1,0:T(8,128)(2,1)S(1)} %get-tuple-element.169), channel_id=1, source_target_pairs={{0,8},{1,9},{2,10},{3,11},{4,12},{5,13},{6,14},{7,15},{8,0},{9,1},... | collective-permute-start | bytes 565256 | tf_op jit(solution)/shard_map/ppermute | solution.py:32
  224.4 16.5 %collective-permute-start.33 = (bf16[736,128]{1,0:T(8,128)(2,1)S(1)}, bf16[736,128]{1,0:T(8,128)(2,1)S(1)}, u32[]{:S(2)}, u32[]{:S(2)}) collective-permute-start(bf16[736,128]{1,0:T(8,128)(2,1)S(1)} %get-tuple-element.170), channel_id=1, source_target_pairs={{0,16},{1,17},{2,18},{3,19},{4,20},{5,21},{6,22},{7,23},{8,24},{9,... | collective-permute-start | bytes 565256 | tf_op jit(solution)/shard_map/ppermute | solution.py:32
  226.6 14.3 %collective-permute-start.34 = (bf16[736,128]{1,0:T(8,128)(2,1)S(1)}, bf16[736,128]{1,0:T(8,128)(2,1)S(1)}, u32[]{:S(2)}, u32[]{:S(2)}) collective-permute-start(bf16[736,128]{1,0:T(8,128)(2,1)S(1)} %get-tuple-element.171), channel_id=1, source_target_pairs={{0,24},{1,25},{2,26},{3,27},{4,28},{5,29},{6,30},{7,31},{8,16},{9,... | collective-permute-start | bytes 565256 | tf_op jit(solution)/shard_map/ppermute | solution.py:32
  241.8 5.7 %collective-permute-start.35 = (bf16[144,128]{1,0:T(8,128)(2,1)S(1)}, bf16[144,128]{1,0:T(8,128)(2,1)S(1)}, u32[]{:S(2)}, u32[]{:S(2)}) collective-permute-start(bf16[144,128]{1,0:T(8,128)(2,1)S(1)} %get-tuple-element.173), channel_id=1, source_target_pairs={{0,8},{1,9},{2,10},{3,11},{4,12},{5,13},{6,14},{7,15},{8,0},{9,1},... | collective-permute-start | bytes 110600 | tf_op jit(solution)/shard_map/ppermute | solution.py:32
  244.5 5.0 %collective-permute-start.36 = (bf16[144,128]{1,0:T(8,128)(2,1)S(1)}, bf16[144,128]{1,0:T(8,128)(2,1)S(1)}, u32[]{:S(2)}, u32[]{:S(2)}) collective-permute-start(bf16[144,128]{1,0:T(8,128)(2,1)S(1)} %get-tuple-element.174), channel_id=1, source_target_pairs={{0,16},{1,17},{2,18},{3,19},{4,20},{5,21},{6,22},{7,23},{8,24},{9,... | collective-permute-start | bytes 110600 | tf_op jit(solution)/shard_map/ppermute | solution.py:32
  245.3 5.8 %collective-permute-start.37 = (bf16[144,128]{1,0:T(8,128)(2,1)S(1)}, bf16[144,128]{1,0:T(8,128)(2,1)S(1)}, u32[]{:S(2)}, u32[]{:S(2)}) collective-permute-start(bf16[144,128]{1,0:T(8,128)(2,1)S(1)} %get-tuple-element.175), channel_id=1, source_target_pairs={{0,24},{1,25},{2,26},{3,27},{4,28},{5,29},{6,30},{7,31},{8,16},{9,... | collective-permute-start | bytes 110600 | tf_op jit(solution)/shard_map/ppermute | solution.py:32
  (1 other events, 0.8 us)
where the time goes:
time: 256 us; the launch traced here: 253 us
  Pallas kernels  98.6 us (39%)
  matrix products  48.7 us (19%)
  starting transfers between devices  38.7 us (15%)
  waiting for transfers between devices  36.2 us (14%)
  local copies, waits for them, and re-layouts  16.2 us (6%)
  other arithmetic  13.5 us (5%)
    ppermute x38, starting transfers between devices, swap(): lax.ppermute(field, 'dp', [(place, place ^ mask) for place in range(devic...  38.7 us
    ppermute x38, waiting for transfers between devices, swap(): lax.ppermute(field, 'dp', [(place, place ^ mask) for place in range(devic...  36.2 us
    pallas_call x3, Pallas kernels, attend_back(): pl.pallas_call(functools.partial(attend_back_kernel, head=head, group=gro...  32.7 us
    pallas_call x3, Pallas kernels, attend(): pl.pallas_call(functools.partial(attend_kernel, head=head, group=group),...  21.9 us
    pallas_call x2, Pallas kernels, vmem_call(): pl.pallas_call(kernel, out_shape=out_shape, in_specs=[pl.BlockSpec(memory...  19 us
    dot_general x4, matrix products, times_transposed(): lax.dot_general(left, matrix, (((1,), (1,)), ((), ())), preferred_element...  17.8 us
    dot_general x4, matrix products, outer_prod(): lax.dot_general(left, right, (((0,), (0,)), ((), ())), preferred_element_...  14.9 us
    pallas_call x2, Pallas kernels, pack_grads(): pl.pallas_call(functools.partial(pack_kernel, devices=devices, shapes=sha...  14.4 us
  transfers between devices with their start and end apart: 38, of which 14 were waited for; matrix products, arithmetic and copies ran while one was open for 7% of the time, Pallas kernels for 30%

commit v1 on v0

--- a/solution.py
+++ b/solution.py
@@ -34,7 +34,8 @@
 
 def tree_sum(terms):
     while len(terms) > 1:
-        terms = [terms[at] + terms[at + 1] for at in range(0, len(terms), 2)]
+        odd = terms[len(terms) // 2 * 2 :]
+        terms = [terms[at] + terms[at + 1] for at in range(0, len(terms) - 1, 2)] + odd
     return terms[0]
 
 
@@ -427,13 +428,30 @@
     )
 
 
+def first_gain(gains_ref):
+    return gains_ref[...].astype(jnp.float32)[0:1]
+
+
 def normed_rows(tokens_ref, gains_ref):
     resid = tokens_ref[...].astype(jnp.float32)
     inv_rms = lax.rsqrt(jnp.mean(resid * resid, 1, keepdims=True) + EPS)
-    return resid, inv_rms, (resid * inv_rms * gains_ref[0:1, :]).astype(jnp.bfloat16)
-
-
-def project_kernel(tokens_ref, gains_ref, wide_ref, cosine_ref, sine_ref, fields_ref, normed):
+    return resid, inv_rms, (resid * inv_rms * first_gain(gains_ref)).astype(jnp.bfloat16)
+
+
+def project_kernel(
+    tokens_in, cosine_in, sine_in, gains_ref, wide_ref, fields_ref,
+    tokens_ref, cosine_ref, sine_ref, normed, arrival,
+):
+    copies = [
+        pltpu.make_async_copy(source, target, arrival.at[at])
+        for at, (source, target) in enumerate(
+            ((tokens_in, tokens_ref), (cosine_in, cosine_ref), (sine_in, sine_ref))
+        )
+    ]
+    for copy in copies:
+        copy.start()
+    for copy in copies:
+        copy.wait()
     _, _, normed[...] = normed_rows(tokens_ref, gains_ref)
     first_key = tiles_of(HEADS * HEAD_DIM)
     first_value = first_key + tiles_of(KV_HEADS * HEAD_DIM)
@@ -468,13 +486,23 @@
 
 
 def project(tokens, gains, wide, cosine, sine):
-    return vmem_call(
+    return pl.pallas_call(
         project_kernel,
-        jax.ShapeDtypeStruct((tokens.shape[0], wide.shape[1]), jnp.bfloat16),
-        [pltpu.VMEM(tokens.shape, jnp.bfloat16)],
-        "project",
-        tokens, gains, wide, cosine, sine,
-    )
+        out_shape=jax.ShapeDtypeStruct((tokens.shape[0], wide.shape[1]), jnp.bfloat16),
+        in_specs=[pl.BlockSpec(memory_space=pl.ANY)] * 3
+        + [pl.BlockSpec(memory_space=pltpu.VMEM)] * 2,
+        out_specs=pl.BlockSpec(memory_space=pltpu.VMEM),
+        scratch_shapes=[
+            pltpu.VMEM(tokens.shape, tokens.dtype),
+            pltpu.VMEM(cosine.shape, cosine.dtype),
+            pltpu.VMEM(sine.shape, sine.dtype),
+            pltpu.VMEM(tokens.shape, jnp.bfloat16),
+            pltpu.SemaphoreType.DMA((3,)),
+        ],
+        compiler_params=pltpu.CompilerParams(vmem_limit_bytes=VMEM_LIMIT),
+        cost_estimate=LIGHT,
+        name="project",
+    )(tokens, cosine, sine, gains, wide)
 
 
 def finish_kernel(
@@ -509,7 +537,7 @@
         for at in range(start, stop):
             tiled_ref[at] = pair[:, (at - start) * LANES : (at - start + 1) * LANES]
     one_back = dot_nt(fields[...], wide_ref[...])
-    weighted = one_back * gains_ref[0:1, :]
+    weighted = one_back * first_gain(gains_ref)
     cubed = inv_rms * inv_rms * inv_rms
     scaled = resid * inv_rms
     gain_ref[...] = jnp.sum(one_back * scaled, 0, keepdims=True)
@@ -697,8 +725,46 @@
         cuts = [slice(at * block, (at + 1) * block) for at in range(len(plane))]
         parts = [(widen(self.kept[cut]) + widen(self.got[cut])).astype(jnp.bfloat16) for cut in cuts]
         self.parts, other = tied(parts, other)
+        self.groups = [
+            [self.parts[0]]
+            + [swap(part, mask, self.devices) for part, mask in zip(self.parts[1:], plane[1:])]
+        ]
+        return other
+
+    def first_half_stage(self, other):
+        if not self.stages:
+            return other
+        plane, _ = masks_of(self.devices)
+        block, cut = self.kept.shape[0] // len(plane), self.kept.shape[1] // 2
+        parts = []
+        for half in range(2):
+            rows = slice(half * cut, (half + 1) * cut)
+            cuts = [slice(at * block, (at + 1) * block) for at in range(len(plane))]
+            parts.append(
+                [
+                    (widen(self.kept[at, rows]) + widen(self.got[at, rows])).astype(jnp.bfloat16)
+                    for at in cuts
+                ]
+            )
+        self.parts, other = tied(parts, other)
         self.arrived = [
-            swap(part, mask, self.devices) for part, mask in zip(self.parts[1:], plane[1:])
+            [swap(part[at], plane[near], self.devices) for at in (near, 3)]
+            for part, near in zip(self.parts, (1, 2))
+        ]
+        return other
+
+    def second_half_stage(self, other):
+        if not self.stages:
+            return other
+        plane, _ = masks_of(self.devices)
+        sends = [
+            (widen(part[far]) + widen(arrived[1])).astype(jnp.bfloat16)
+            for part, arrived, far in zip(self.parts, self.arrived, (2, 1))
+        ]
+        sends, other = tied(sends, other)
+        self.groups = [
+            [part[0], arrived[0], swap(send, plane[far], self.devices)]
+            for part, arrived, send, far in zip(self.parts, self.arrived, sends, (2, 1))
         ]
         return other
 
@@ -706,9 +772,13 @@
         if not self.stages:
             return other
         _, line = masks_of(self.devices)
-        terms = [self.parts[0]] + self.arrived
         parts = [
-            tree_sum([widen(term[at]) for term in terms]).astype(jnp.bfloat16)
+            jnp.concatenate(
+                [
+                    tree_sum([widen(term[at]) for term in terms]).astype(jnp.bfloat16)
+                    for terms in self.groups
+                ]
+            )
             for at in range(len(line))
         ]
         self.parts, other = tied(parts, other)
@@ -770,7 +840,7 @@
     pairs = LANES // HEAD_DIM
     cosine = jnp.tile(cosine, (seq_count, 2 * pairs))
     sine = jnp.tile(jnp.concatenate([sine, -sine], 1), (seq_count, pairs))
-    fields = project(tokens, gain_f, wide_mat, cosine, sine)
+    fields = project(tokens, norm_gains, wide_mat, cosine, sine)
     fields = second.second_half_stage(fields)
     attended = [attend(fields, head, group_size) for head in range(2)]
     fields, attended = second.core_stage((fields, attended), False)
@@ -813,20 +883,22 @@
     mixed_back = feed_sum.core_stage(mixed_back)
     backs = [back_of(0, mixed_back)]
     mixed_back, _ = tied(mixed_back, backs[0])
-    mixed_back = feed_sum.plane_stage(mixed_back)
-    backs += [back_of(head, mixed_back) for head in range(1, KV_HEADS)]
-    input_grad, tiled, gain_one = finish(tokens, gain_f, wide_mat, cosine, sine, mid_back, backs)
-    input_grad, tiled = feed_sum.line_stage((input_grad, tiled))
+    mixed_back = feed_sum.first_half_stage(mixed_back)
+    backs.append(back_of(1, mixed_back))
+    mixed_back, backs = feed_sum.second_half_stage((mixed_back, backs))
+    backs.append(back_of(2, mixed_back))
+    backs = feed_sum.line_stage(backs)
+    input_grad, tiled, gain_one = finish(tokens, norm_gains, wide_mat, cosine, sine, mid_back, backs)
     gains_back = jnp.concatenate([gain_one, gain_two[None]], 0)
     cuts = [0]
     for _, wide in shapes[:3]:
         cuts.append(cuts[-1] + tiles_of(wide))
     grads = tuple(tiled[start:stop] for start, stop in zip(cuts, cuts[1:]))
     mix_sum = GradSum(grads, shapes[:3], devices, gains_back)
-    input_grad = mix_sum.core_stage(input_grad)
+    if feed_sum.stages:
+        feed_sum.arrived = mix_sum.core_stage(feed_sum.arrived)
     input_grad = mix_sum.plane_stage(input_grad)
-    if feed_sum.stages:
-        feed_sum.arrived = mix_sum.line_stage(feed_sum.arrived)
+    input_grad = mix_sum.line_stage(input_grad)
     mix_parts = mix_sum.result()
     gate_part, up_part, down_part, out_part = feed_sum.result()
     all_parts = mix_parts[:3] + [out_part, gate_part, up_part, down_part]

time: 256 us -> 248 us (0.969)
  other arithmetic: 13.5 us -> 8.5 us
  waiting for transfers between devices: 36.2 us -> 31.5 us
  matrix products: 48.7 us -> 45.8 us
    pallas_call x0 -> x1, Pallas kernels: none -> 7.18 us  [project(): pl.pallas_call(project_kernel, out_shape=jax.ShapeDtypeStruct((tokens.sha...]
    pallas_call x2 -> x1, Pallas kernels: 19 us -> 12.8 us  [vmem_call(): pl.pallas_call(kernel, out_shape=out_shape, in_specs=[pl.BlockSpec(memory...]
    convert_element_type x2 -> x1, other arithmetic: 5.51 us -> 0.16 us  [plane_stage(): (widen(self.kept[cut]) + widen(self.got[cut])).astype(jnp.bfloat16)]
    dot_general x4, matrix products: 17.8 us -> 12.5 us  [times_transposed(): lax.dot_general(left, matrix, (((1,), (1,)), ((), ())), preferred_element...]
    ppermute x38 -> x41, waiting for transfers between devices: 36.2 us -> 31.5 us  [swap(): lax.ppermute(field, 'dp', [(place, place ^ mask) for place in range(devic...]
    dot_general x1, matrix products: 4.53 us -> 8.04 us  [body(): upward = jnp.dot(normed_two, wu_mat, preferred_element_type=jnp.float32)]
    slice x2, local copies, waits for them, and re-layouts: 2.3 us -> 4.93 us  [body(): grads = tuple((tiled[start:stop] for start, stop in zip(cuts, cuts[1:])))]
    ppermute x38 -> x41, starting transfers between devices: 38.7 us -> 40.4 us  [swap(): lax.ppermute(field, 'dp', [(place, place ^ mask) for place in range(devic...]
  transfers between devices with their start and end apart: 38 -> 41, of which waited for: 14 -> 14; matrix products, arithmetic and copies ran while one was open for 7% -> 9% of each run, Pallas kernels for 30% -> 33%
where the time goes in v1:
time: 248 us; the launch traced here: 245 us
  Pallas kernels  98.9 us (40%)
  matrix products  45.8 us (18%)
  starting transfers between devices  40.4 us (16%)
  waiting for transfers between devices  31.5 us (13%)
  local copies, waits for them, and re-layouts  18.5 us (7%)
  other arithmetic  8.5 us (3%)
    ppermute x41, starting transfers between devices, swap(): lax.ppermute(field, 'dp', [(place, place ^ mask) for place in range(devic...  40.4 us
    pallas_call x3, Pallas kernels, attend_back(): pl.pallas_call(functools.partial(attend_back_kernel, head=head, group=gro...  32.5 us
    ppermute x41, waiting for transfers between devices, swap(): lax.ppermute(field, 'dp', [(place, place ^ mask) for place in range(devic...  31.5 us
    pallas_call x3, Pallas kernels, attend(): pl.pallas_call(functools.partial(attend_kernel, head=head, group=group),...  21.7 us
    dot_general x4, matrix products, outer_prod(): lax.dot_general(left, right, (((0,), (0,)), ((), ())), preferred_element_...  14.7 us
    pallas_call x2, Pallas kernels, pack_grads(): pl.pallas_call(functools.partial(pack_kernel, devices=devices, shapes=sha...  14.2 us
    pallas_call x1, Pallas kernels, vmem_call(): pl.pallas_call(kernel, out_shape=out_shape, in_specs=[pl.BlockSpec(memory...  12.8 us
    dot_general x4, matrix products, times_transposed(): lax.dot_general(left, matrix, (((1,), (1,)), ((), ())), preferred_element...  12.5 us
  transfers between devices with their start and end apart: 41, of which 14 were waited for; matrix products, arithmetic and copies ran while one was open for 9% of the time, Pallas kernels for 33%

profile of v1, /device:TPU:0, one launch (start us, length us, event | category | flops | bytes accessed | tf_op | source)
XLA Modules:
  0.0 245.0 jit_solution(11762277604142192445)
XLA Ops:
  1.4 3.1 %collective-permute-start = (bf16[144,128]{1,0:T(8,128)(2,1)S(1)}, bf16[144,128]{1,0:T(8,128)(2,1)S(1)}, u32[]{:S(2)}, u32[]{:S(2)}) collective-permute-start(bf16[144,128]{1,0:T(8,128)(2,1)S(1)} %fusion.35), channel_id=1, source_target_pairs={{0,8},{1,9},{2,10},{3,11},{4,12},{5,13},{6,14},{7,15},{8,0},{9,1},... | collective-permute-start | bytes 110600 | tf_op jit(solution)/shard_map/ppermute | solution.py:32
  4.5 2.5 %collective-permute-start.2 = (bf16[144,128]{1,0:T(8,128)(2,1)S(1)}, bf16[144,128]{1,0:T(8,128)(2,1)S(1)}, u32[]{:S(2)}, u32[]{:S(2)}) collective-permute-start(bf16[144,128]{1,0:T(8,128)(2,1)S(1)} %fusion.35), channel_id=1, source_target_pairs={{0,24},{1,25},{2,26},{3,27},{4,28},{5,29},{6,30},{7,31},{8,16},{9,... | collective-permute-start | bytes 110600 | tf_op jit(solution)/shard_map/ppermute | solution.py:32
  8.0 2.7 %collective-permute-done.2 = bf16[144,128]{1,0:T(8,128)(2,1)S(1)} collective-permute-done((bf16[144,128]{1,0:T(8,128)(2,1)S(1)}, bf16[144,128]{1,0:T(8,128)(2,1)S(1)}, u32[]{:S(2)}, u32[]{:S(2)}) %collective-permute-start.2) | collective-permute-done | bytes 36896 | tf_op jit(solution)/shard_map/ppermute | solution.py:32
  10.8 1.5 collective-permute-done.1
  12.3 1.6 collective-permute-start.3
  13.8 1.5 collective-permute-start.4
  16.2 1.6 collective-permute-start.7
  17.9 1.2 collective-permute-done.3
  19.0 1.3 collective-permute-start.8
  20.3 1.5 collective-permute-done.4
  22.0 1.1 collective-permute-done.6
  23.1 8.1 %collective-permute-done.7 = bf16[736,128]{1,0:T(8,128)(2,1)S(1)} collective-permute-done((bf16[736,128]{1,0:T(8,128)(2,1)S(1)}, bf16[736,128]{1,0:T(8,128)(2,1)S(1)}, u32[]{:S(2)}, u32[]{:S(2)}) %collective-permute-start.7) | collective-permute-done | bytes 188448 | tf_op jit(solution)/shard_map/ppermute | solution.py:32
  32.3 1.5 collective-permute-start.10
  33.8 1.5 collective-permute-start.11
  36.0 1.0 copy.36.sine_in.sine_ref
  37.0 1.0 copy.35.cosine_in.cosine_ref
  38.0 1.5 copy.33.tokens_in.tokens_ref
  39.5 3.5 %unpack.2.wide_ref = bf16[576,1152]{1,0:T(8,128)(2,1)} custom-call(s32[1]{0:T(128)} %bitcast.21.place_ref, bf16[16,144,128]{2,1,0:T(8,128)(2,1)} %copy-done.8, bf16[16,144,128]{2,1,0:T(8,128)(2,1)} %copy-done.10), custom_call_target="tpu_custom_call" | custom-call | flops 100000000 | bytes 1000000 | tf_op jit(solution)/shard_map/unpack/pallas_call | solution.py:145
  42.9 7.2 %project.1.fields_ref = bf16[1024,1152]{1,0:T(8,128)(2,1)} custom-call(bf16[1024,576]{1,0:T(8,128)(2,1)} %copy.33.tokens_in.tokens_ref, f32[1024,128]{1,0:T(8,128)} %copy.35.cosine_in.cosine_ref, f32[1024,128]{1,0:T(8,128)} %copy.36.sine_in.sine_ref, bf16[2,576]{1,0:T(2,128)(2,1)} %gains_ref.3, bf16[576,1152]{1,0:T(8,128)(2,1)} %unpack.2.wide_ref), custom_call_target="tpu_custom_call" | custom-call | flops 100000000 | bytes 1000000 | tf_op jit(solution)/shard_map/project/pallas_call | solution.py:489
  50.8 1.5 collective-permute-start.13
  52.8 1.5 collective-permute-start.15
  54.3 7.2 %attend.3 = (bf16[1024,192]{1,0:T(8,128)(2,1)}, f32[1024,128]{1,0:T(8,128)}) custom-call(bf16[1024,1152]{1,0:T(8,128)(2,1)} %project.1.fields_ref), custom_call_target="tpu_custom_call" | custom-call | flops 100000000 | bytes 1000000 | tf_op jit(solution)/shard_map/attend/pallas_call | solution.py:324
  61.5 7.3 %attend.4 = (bf16[1024,192]{1,0:T(8,128)(2,1)}, f32[1024,128]{1,0:T(8,128)}) custom-call(bf16[1024,1152]{1,0:T(8,128)(2,1)} %project.1.fields_ref), custom_call_target="tpu_custom_call" | custom-call | flops 100000000 | bytes 1000000 | tf_op jit(solution)/shard_map/attend/pallas_call | solution.py:324
  71.7 1.5 collective-permute-done.18.refs_10_
  74.9 7.2 %attend.5 = (bf16[1024,192]{1,0:T(8,128)(2,1)}, f32[1024,128]{1,0:T(8,128)}) custom-call(bf16[1024,1152]{1,0:T(8,128)(2,1)} %project.1.fields_ref), custom_call_target="tpu_custom_call" | custom-call | flops 100000000 | bytes 1000000 | tf_op jit(solution)/shard_map/attend/pallas_call | solution.py:324
  82.1 7.1 %unpack.3 = (bf16[576,1536]{1,0:T(8,128)(2,1)}, bf16[576,1536]{1,0:T(8,128)(2,1)}, bf16[1536,576]{1,0:T(8,128)(2,1)}, bf16[576,576]{1,0:T(8,128)(2,1)}) custom-call(s32[1]{0:T(128)} %bitcast.21.place_ref, bf16[4,368,128]{2,1,0:T(8,128)(2,1)} %copy-done.3, bf16[4,368,128]{2,1,0:T(8,128)(2,1)} %copy-done.14, bf16[4,368,128]{2,1,0:T(8,128)(2,1)} %copy-done.15, ...), custom_call_target="tpu_custom_call" | custom-call | flops 100000000 | bytes 1000000 | tf_op jit(solution)/shard_map/unpack/pallas_call | solution.py:145
  89.3 2.8 %multiply_reduce_fusion.2 = (f32[1024]{0:T(1024)S(1)}, f32[1024,576]{1,0:T(8,128)S(1)}) fusion(bf16[576,576]{1,0:T(8,128)(2,1)} %get-tuple-element.145, bf16[1024,192]{1,0:T(8,128)(2,1)S(1)} %copy-done.12, bf16[1024,192]{1,0:T(8,128)(2,1)S(1)} %copy-done.11, bf16[1024,192]{1,0:T(8,128)(2,1)} %get-tuple-element.133.mixed_ref, bf16[1024,576]{1,0:T(8,128)(2,1)S(1)} %copy-done), kind=kOutput, calls=%fused_computation.14 | convolution fusion | flops 685374464 | bytes 5386240 | tf_op jit(solution)/shard_map/dot_general | solution.py:850
  92.1 4.7 %fusion.40 = f32[1536,1024]{0,1:T(8,128)} fusion(bf16[1536,576]{1,0:T(8,128)(2,1)S(1)} %copy-done.21, bf16[1024,576]{0,1:T(8,128)(2,1)S(1)} %copy-done.7), kind=kOutput, calls=%fused_computation.118 | convolution fusion | flops 1811939328 | bytes 9240576 | tf_op jit(solution)/shard_map/dot_general | solution.py:608
  97.1 1.2 copy-done.22
  98.3 2.6 %fusion.39 = f32[1024,1536]{1,0:T(8,128)S(1)} fusion(bf16[1024,576]{1,0:T(8,128)(2,1)S(1)} %multiply_convert_fusion.1, bf16[576,1536]{1,0:T(8,128)(2,1)S(1)} %copy-done.22), kind=kOutput, calls=%fused_computation.117 | convolution fusion | flops 1811939328 | bytes 9240576 | tf_op jit(solution)/shard_map/dot_general | solution.py:854
  100.9 8.0 %fusion.2 = (bf16[1024,1536]{1,0:T(8,128)(2,1)S(1)}, bf16[1024,1536]{1,0:T(8,128)(2,1)S(1)}, bf16[1024,1536]{1,0:T(8,128)(2,1)}) fusion(f32[1536,1024]{0,1:T(8,128)} %fusion.40, f32[1024,1536]{1,0:T(8,128)S(1)} %fusion.39, bf16[1024,576]{1,0:T(8,128)(2,1)S(1)} %multiply_convert_fusion.1, bf16[576,1536]{1,0:T(8,128)(2,1)S(1)} %copy-done.23), kind=kOutput, calls=%fused_computation.4 | convolution fusion | flops 1835532288 | bytes 24969216 | tf_op jit(solution)/shard_map/dot_general | solution.py:855
  108.9 2.6 %fusion.41 = f32[1024,576]{1,0:T(8,128)S(1)} fusion(bf16[1024,1536]{1,0:T(8,128)(2,1)S(1)} %get-tuple-element.233, bf16[576,1536]{1,0:T(8,128)(2,1)S(1)} %copy-done.23), kind=kOutput, calls=%fused_computation.119 | convolution fusion | flops 1811939328 | bytes 7274496 | tf_op jit(solution)/shard_map/dot_general | solution.py:608
  111.5 2.8 %multiply_reduce_fusion = (f32[576]{0:T(1024)S(1)}, f32[1024]{0:T(1024)S(1)}, f32[1024,576]{1,0:T(8,128)S(1)}) fusion(f32[1024,576]{1,0:T(8,128)S(1)} %get-tuple-element.280, f32[1024]{0:T(1024)S(1)} %get-tuple-element.275, f32[576]{0:T(1024)S(1)} %convert_reduce_fusion, f32[1024,576]{1,0:T(8,128)S(1)} %fusion.41, ...), kind=kOutput, calls=%fused_computation.9 | convolution fusion | flops 1816066560 | bytes 12005888 | tf_op jit(solution)/shard_map/dot_general | solution.py:608
  115.5 2.4 convolution_convert_fusion.back_ref
  117.9 2.5 %fusion.6.refs_3_ = f32[576,576]{1,0:T(8,128)} fusion(f32[1024,576]{1,0:T(8,128)S(1)} %subtract_add_fusion.mid_back_ref, bf16[1024,192]{1,0:T(8,128)(2,1)S(1)} %copy-done.12, bf16[1024,192]{1,0:T(8,128)(2,1)S(1)} %copy-done.11, bf16[1024,192]{1,0:T(8,128)(2,1)S(1)} %copy-done.13), kind=kOutput, calls=%fused_computation.30 | convolution fusion | flops 683606016 | bytes 4866048 | tf_op jit(solution)/shard_map/dot_general | solution.py:602
  120.4 3.8 %fusion.43.refs_1_ = f32[576,1536]{1,0:T(8,128)} fusion(bf16[1024,576]{1,0:T(8,128)(2,1)S(1)} %multiply_convert_fusion.1, bf16[1024,1536]{1,0:T(8,128)(2,1)S(1)} %get-tuple-element.233), kind=kOutput, calls=%fused_computation.121 | convolution fusion | flops 1811939328 | bytes 7864320 | tf_op jit(solution)/shard_map/dot_general | solution.py:602
  124.2 3.8 %fusion.42.refs_0_ = f32[576,1536]{1,0:T(8,128)} fusion(bf16[1024,576]{1,0:T(8,128)(2,1)S(1)} %multiply_convert_fusion.1, bf16[1024,1536]{1,0:T(8,128)(2,1)S(1)} %get-tuple-element.232), kind=kOutput, calls=%fused_computation.120 | convolution fusion | flops 1811939328 | bytes 7864320 | tf_op jit(solution)/shard_map/dot_general | solution.py:602
  128.0 4.6 %fusion.44.refs_2_ = f32[1536,576]{1,0:T(8,128)} fusion(bf16[1024,1536]{1,0:T(8,128)(2,1)S(1)} %copy-done.25, bf16[1024,576]{0,1:T(8,128)(2,1)S(1)} %copy-done.7), kind=kOutput, calls=%fused_computation.122 | convolution fusion | flops 1811939328 | bytes 7864320 | tf_op jit(solution)/shard_map/dot_general | solution.py:602
  132.6 10.2 %pack.2 = (bf16[16,736,128]{2,1,0:T(8,128)(2,1)}, bf16[16,736,128]{2,1,0:T(8,128)(2,1)}) custom-call(s32[1]{0:T(128)} %bitcast.21.place_ref, f32[576,1536]{1,0:T(8,128)} %fusion.42.refs_0_, f32[576,1536]{1,0:T(8,128)} %fusion.43.refs_1_, f32[1536,576]{1,0:T(8,128)} %fusion.44.refs_2_, f32[576,576]{1,0:T(8,128)} %fusion.6.refs_3_), custom_call_target="tpu_custom_call" | custom-call | flops 100000000 | bytes 1000000 | tf_op jit(solution)/shard_map/pack/pallas_call | solution.py:244
  143.2 10.8 %attend_back.3 = (f32[1024,192]{1,0:T(8,128)}, f32[1024,128]{1,0:T(8,128)}) custom-call(bf16[1024,1152]{1,0:T(8,128)(2,1)} %project.1.fields_ref, bf16[1024,576]{1,0:T(8,128)(2,1)} %convolution_convert_fusion.back_ref, bf16[1024,192]{1,0:T(8,128)(2,1)} %get-tuple-element.133.mixed_ref, f32[1024,128]{1,0:T(8,128)} %get-tuple-element.154.total_ref), custom_call_target="tpu_custom_call" | custom-call | flops 100000000 | bytes 1000000 | tf_op jit(solution)/shard_map/attend_back/pallas_call | solution.py:400
  154.1 3.4 %add_convert_fusion.3 = (bf16[4,368,128]{2,1,0:T(8,128)(2,1)}, bf16[4,368,128]{2,1,0:T(8,128)(2,1)S(1)}, bf16[4,368,128]{2,1,0:T(8,128)(2,1)S(1)}, bf16[4,368,12...) fusion(bf16[16,736,128]{2,1,0:T(8,128)(2,1)} %collective-permut, ...), kind=kLoop, calls=%fused_computation.21 | loop fusion | flops 6029312 | bytes 9043968 | tf_op jit(solution)/shard_map/convert_element_type | solution.py:745
  158.4 1.5 collective-permute-start.25
  160.0 11.0 %attend_back.4 = (f32[1024,192]{1,0:T(8,128)}, f32[1024,128]{1,0:T(8,128)}) custom-call(bf16[1024,1152]{1,0:T(8,128)(2,1)} %project.1.fields_ref, bf16[1024,576]{1,0:T(8,128)(2,1)} %convolution_convert_fusion.back_ref, bf16[1024,192]{1,0:T(8,128)(2,1)} %get-tuple-element.134.mixed_ref, f32[1024,128]{1,0:T(8,128)} %get-tuple-element.165.total_ref), custom_call_target="tpu_custom_call" | custom-call | flops 100000000 | bytes 1000000 | tf_op jit(solution)/shard_map/attend_back/pallas_call | solution.py:400
  171.2 1.6 collective-permute-start.28
  173.8 10.7 %attend_back.5 = (f32[1024,192]{1,0:T(8,128)}, f32[1024,128]{1,0:T(8,128)}) custom-call(bf16[1024,1152]{1,0:T(8,128)(2,1)} %project.1.fields_ref, bf16[1024,576]{1,0:T(8,128)(2,1)} %convolution_convert_fusion.back_ref, bf16[1024,192]{1,0:T(8,128)(2,1)} %get-tuple-element.136.mixed_ref, f32[1024,128]{1,0:T(8,128)} %get-tuple-element.177.total_ref), custom_call_target="tpu_custom_call" | custom-call | flops 100000000 | bytes 1000000 | tf_op jit(solution)/shard_map/attend_back/pallas_call | solution.py:400
  184.6 4.6 %collective-permute-done.29 = bf16[4,368,128]{2,1,0:T(8,128)(2,1)S(1)} collective-permute-done((bf16[4,368,128]{2,1,0:T(8,128)(2,1)S(1)}, bf16[4,368,128]{2,1,0:T(8,128)(2,1)S(1)}, u32[]{:S(2)}, u32[]{:S(2)}) %collective-permute-start.29) | collective-permute-done | bytes 376864 | tf_op jit(solution)/shard_map/ppermute | solution.py:32
  189.5 2.6 %collective-permute-start.31 = (bf16[736,128]{1,0:T(8,128)(2,1)S(1)}, bf16[736,128]{1,0:T(8,128)(2,1)S(1)}, u32[]{:S(2)}, u32[]{:S(2)}) collective-permute-start(bf16[736,128]{1,0:T(8,128)(2,1)S(1)} %pad_maximum_fusion.9), channel_id=1, source_target_pairs={{0,8},{1,9},{2,10},{3,11},{4,12},{5,13},{6,14},{7,15},{8,0},{9,1},... | collective-permute-start | bytes 565256 | tf_op jit(solution)/shard_map/ppermute | solution.py:32
  192.9 1.6 collective-permute-start.33
  194.5 12.8 %finish.1 = (bf16[1024,576]{1,0:T(8,128)(2,1)}, f32[9,576,128]{2,1,0:T(8,128)}, f32[1,576]{1,0:T(1,128)}) custom-call(bf16[1024,576]{1,0:T(8,128)(2,1)} %copy.33.tokens_in.tokens_ref, bf16[2,576]{1,0:T(2,128)(2,1)} %gains_ref.3, bf16[576,1152]{1,0:T(8,128)(2,1)} %unpack.2.wide_ref, f32[1024,128]{1,0:T(8,128)} %copy.35.cosine_in.cosine_ref, ...), custom_call_target="tpu_custom_call" | custom-call | flops 100000000 | bytes 1000000 | tf_op jit(solution)/shard_map/finish/pallas_call | solution.py:474
  207.3 2.3 fusion.38
  209.6 2.6 %slice.303.refs_0_ = f32[5,576,128]{2,1,0:T(8,128)} slice(f32[9,576,128]{2,1,0:T(8,128)} %get-tuple-element.186), slice={[0:5], [0:576], [0:128]} | slice | bytes 2949120 | tf_op jit(solution)/shard_map/slice | solution.py:896
  212.8 3.9 %pack.3 = (bf16[16,144,128]{2,1,0:T(8,128)(2,1)}, bf16[16,144,128]{2,1,0:T(8,128)(2,1)}) custom-call(s32[1]{0:T(128)} %bitcast.21.place_ref, f32[5,576,128]{2,1,0:T(8,128)} %slice.303.refs_0_, f32[2,576,128]{2,1,0:T(8,128)} %get-tuple-element.244.refs_1_, f32[2,576,128]{2,1,0:T(8,128)} %get-tuple-element.243.refs_2_, f32[2,576]{1,0:T(2,128)} %pad_maximum_fusion.13.refs_3_), custom_call_target="tpu_custom_call" | custom-call | flops 100000000 | bytes 1000000 | tf_op jit(solution)/shard_map/pack/pallas_call | solution.py:244
  216.9 5.1 %add_convert_fusion = bf16[1024,576]{1,0:T(8,128)(2,1)S(1)} fusion(f32[1024,576]{1,0:T(8,128)S(1)} %get-tuple-element.280, bf16[1024,1536]{1,0:T(8,128)(2,1)} %get-tuple-element.234, bf16[1536,576]{1,0:T(8,128)(2,1)} %get-tuple-element.148), kind=kOutput, calls=%fused_computation.12 | convolution fusion | flops 1813118976 | bytes 8454144 | tf_op jit(solution)/shard_map/dot_general | solution.py:859
  222.0 1.4 copy.48
  224.3 1.5 collective-permute-start.36
  225.8 1.4 collective-permute-start.37
  228.0 2.4 collective-permute-done.35
  230.4 2.1 collective-permute-done.36
  232.5 1.6 collective-permute-done.37
  234.2 1.1 collective-permute-start.38
  235.3 1.8 collective-permute-start.39
  237.1 1.6 collective-permute-start.40
  239.3 1.4 copy.49
  240.7 2.2 collective-permute-done.40
  (145 shorter events, 20.3 us)
Async XLA Ops:
  1.4 6.6 %collective-permute-start = (bf16[144,128]{1,0:T(8,128)(2,1)S(1)}, bf16[144,128]{1,0:T(8,128)(2,1)S(1)}, u32[]{:S(2)}, u32[]{:S(2)}) collective-permute-start(bf16[144,128]{1,0:T(8,128)(2,1)S(1)} %fusion.35), channel_id=1, source_target_pairs={{0,8},{1,9},{2,10},{3,11},{4,12},{5,13},{6,14},{7,15},{8,0},{9,1},... | collective-permute-start | bytes 110600 | tf_op jit(solution)/shard_map/ppermute | solution.py:32
  4.5 6.2 %collective-permute-start.2 = (bf16[144,128]{1,0:T(8,128)(2,1)S(1)}, bf16[144,128]{1,0:T(8,128)(2,1)S(1)}, u32[]{:S(2)}, u32[]{:S(2)}) collective-permute-start(bf16[144,128]{1,0:T(8,128)(2,1)S(1)} %fusion.35), channel_id=1, source_target_pairs={{0,24},{1,25},{2,26},{3,27},{4,28},{5,29},{6,30},{7,31},{8,16},{9,... | collective-permute-start | bytes 110600 | tf_op jit(solution)/shard_map/ppermute | solution.py:32
  7.0 5.3 %collective-permute-start.1 = (bf16[144,128]{1,0:T(8,128)(2,1)S(1)}, bf16[144,128]{1,0:T(8,128)(2,1)S(1)}, u32[]{:S(2)}, u32[]{:S(2)}) collective-permute-start(bf16[144,128]{1,0:T(8,128)(2,1)S(1)} %fusion.35), channel_id=1, source_target_pairs={{0,16},{1,17},{2,18},{3,19},{4,20},{5,21},{6,22},{7,23},{8,24},{9,... | collective-permute-start | bytes 110600 | tf_op jit(solution)/shard_map/ppermute | solution.py:32
  12.3 6.7 %collective-permute-start.3 = (bf16[4,144,128]{2,1,0:T(8,128)(2,1)S(1)}, bf16[4,144,128]{2,1,0:T(8,128)(2,1)S(1)}, u32[]{:S(2)}, u32[]{:S(2)}) collective-permute-start(bf16[4,144,128]{2,1,0:T(8,128)(2,1)S(1)} %pad_maximum_fusion.12), channel_id=1, source_target_pairs={{0,2},{1,3},{2,0},{3,1},{4,6},{5,7},{6,4},{7,5},{8,10},{9,11},{10,... | collective-permute-start | bytes 442376 | tf_op jit(solution)/shard_map/ppermute | solution.py:32
  13.8 8.0 %collective-permute-start.4 = (bf16[4,144,128]{2,1,0:T(8,128)(2,1)S(1)}, bf16[4,144,128]{2,1,0:T(8,128)(2,1)S(1)}, u32[]{:S(2)}, u32[]{:S(2)}) collective-permute-start(bf16[4,144,128]{2,1,0:T(8,128)(2,1)S(1)} %pad_maximum_fusion.12), channel_id=1, source_target_pairs={{0,4},{1,5},{2,6},{3,7},{4,0},{5,1},{6,2},{7,3},{8,12},{9,13},{10,... | collective-permute-start | bytes 442376 | tf_op jit(solution)/shard_map/ppermute | solution.py:32
  15.3 6.5 %collective-permute-start.5 = (bf16[4,144,128]{2,1,0:T(8,128)(2,1)S(1)}, bf16[4,144,128]{2,1,0:T(8,128)(2,1)S(1)}, u32[]{:S(2)}, u32[]{:S(2)}) collective-permute-start(bf16[4,144,128]{2,1,0:T(8,128)(2,1)S(1)} %pad_maximum_fusion.12), channel_id=1, source_target_pairs={{0,6},{1,7},{2,4},{3,5},{4,2},{5,3},{6,0},{7,1},{8,14},{9,15},{10,... | collective-permute-start | bytes 442376 | tf_op jit(solution)/shard_map/ppermute | solution.py:32
  15.8 7.3 %collective-permute-start.6 = (bf16[736,128]{1,0:T(8,128)(2,1)S(1)}, bf16[736,128]{1,0:T(8,128)(2,1)S(1)}, u32[]{:S(2)}, u32[]{:S(2)}) collective-permute-start(bf16[736,128]{1,0:T(8,128)(2,1)S(1)} %fusion.15), channel_id=1, source_target_pairs={{0,8},{1,9},{2,10},{3,11},{4,12},{5,13},{6,14},{7,15},{8,0},{9,1},... | collective-permute-start | bytes 565256 | tf_op jit(solution)/shard_map/ppermute | solution.py:32
  16.2 15.1 %collective-permute-start.7 = (bf16[736,128]{1,0:T(8,128)(2,1)S(1)}, bf16[736,128]{1,0:T(8,128)(2,1)S(1)}, u32[]{:S(2)}, u32[]{:S(2)}) collective-permute-start(bf16[736,128]{1,0:T(8,128)(2,1)S(1)} %fusion.15), channel_id=1, source_target_pairs={{0,16},{1,17},{2,18},{3,19},{4,20},{5,21},{6,22},{7,23},{8,24},{9,... | collective-permute-start | bytes 565256 | tf_op jit(solution)/shard_map/ppermute | solution.py:32
  19.0 12.3 %collective-permute-start.8 = (bf16[736,128]{1,0:T(8,128)(2,1)S(1)}, bf16[736,128]{1,0:T(8,128)(2,1)S(1)}, u32[]{:S(2)}, u32[]{:S(2)}) collective-permute-start(bf16[736,128]{1,0:T(8,128)(2,1)S(1)} %fusion.15), channel_id=1, source_target_pairs={{0,24},{1,25},{2,26},{3,27},{4,28},{5,29},{6,30},{7,31},{8,16},{9,... | collective-permute-start | bytes 565256 | tf_op jit(solution)/shard_map/ppermute | solution.py:32
  21.9 15.0 %copy-start.8 = (bf16[16,144,128]{2,1,0:T(8,128)(2,1)}, bf16[16,144,128]{2,1,0:T(8,128)(2,1)S(1)}, u32[]{:S(2)}) copy-start(bf16[16,144,128]{2,1,0:T(8,128)(2,1)S(1)} %constant_dynamic-update-slice_fusion.refs_0_) | copy-start | bytes 1769476
  21.9 9.5 %collective-permute-start.9 = (bf16[16,144,128]{2,1,0:T(8,128)(2,1)S(1)}, bf16[16,144,128]{2,1,0:T(8,128)(2,1)S(1)}, u32[]{:S(2)}, u32[]{:S(2)}) collective-permute-start(bf16[16,144,128]{2,1,0:T(8,128)(2,1)S(1)} %constant_dynamic-update-slice_fusion.refs_0_), channel_id=1, source_target_pairs={{0,1},{1,0},{2,3},{3,2},{4,5},{5,4},{6,7},{7,6},{8,9},{9,8},{10,11... | collective-permute-start | bytes 1769480 | tf_op jit(solution)/shard_map/ppermute | solution.py:32
  31.3 6.7 %copy-start.6 = (bf16[1024,576]{0,1:T(8,128)(2,1)S(1)}, bf16[1024,576]{0,1:T(8,128)(2,1)}, u32[]{:S(2)}) copy-start(bf16[1024,576]{0,1:T(8,128)(2,1)} %param.10) | copy-start | bytes 3538948
  31.4 37.4 %copy-start.3 = (bf16[4,368,128]{2,1,0:T(8,128)(2,1)}, bf16[4,368,128]{2,1,0:T(8,128)(2,1)S(1)}, u32[]{:S(2)}) copy-start(bf16[4,368,128]{2,1,0:T(8,128)(2,1)S(1)} %get-tuple-element.137.refs_0_) | copy-start | bytes 1130500
  31.5 38.9 %copy-start.4 = (bf16[4,368,128]{2,1,0:T(8,128)(2,1)}, bf16[4,368,128]{2,1,0:T(8,128)(2,1)S(1)}, u32[]{:S(2)}) copy-start(bf16[4,368,128]{2,1,0:T(8,128)(2,1)S(1)} %get-tuple-element.141.refs_4_) | copy-start | bytes 1130500
  32.3 17.9 %collective-permute-start.10 = (bf16[4,368,128]{2,1,0:T(8,128)(2,1)S(1)}, bf16[4,368,128]{2,1,0:T(8,128)(2,1)S(1)}, u32[]{:S(2)}, u32[]{:S(2)}) collective-permute-start(bf16[4,368,128]{2,1,0:T(8,128)(2,1)S(1)} %get-tuple-element.137.refs_0_), channel_id=1, source_target_pairs={{0,2},{1,3},{2,0},{3,1},{4,6},{5,7},{6,4},{7,5},{8,10},{9,11},{10,... | collective-permute-start | bytes 1130504 | tf_op jit(solution)/shard_map/ppermute | solution.py:32
  33.8 16.4 %collective-permute-start.11 = (bf16[4,368,128]{2,1,0:T(8,128)(2,1)S(1)}, bf16[4,368,128]{2,1,0:T(8,128)(2,1)}, u32[]{:S(2)}, u32[]{:S(2)}) collective-permute-start(bf16[4,368,128]{2,1,0:T(8,128)(2,1)S(1)} %get-tuple-element.141.refs_4_), channel_id=1, source_target_pairs={{0,4},{1,5},{2,6},{3,7},{4,0},{5,1},{6,2},{7,3},{8,12},{9,13},{10,... | collective-permute-start | bytes 1130504 | tf_op jit(solution)/shard_map/ppermute | solution.py:32
  50.1 24.0 %copy-start.7 = (bf16[1024,576]{0,1:T(8,128)(2,1)S(1)}, bf16[1024,576]{0,1:T(8,128)(2,1)}, u32[]{:S(2)}) copy-start(bf16[1024,576]{0,1:T(8,128)(2,1)} %param.11) | copy-start | bytes 3538948
  50.2 24.7 %copy-start.14 = (bf16[4,368,128]{2,1,0:T(8,128)(2,1)}, bf16[4,368,128]{2,1,0:T(8,128)(2,1)S(1)}, u32[]{:S(2)}) copy-start(bf16[4,368,128]{2,1,0:T(8,128)(2,1)S(1)} %collective-permute-done.10.refs_1_) | copy-start | bytes 1130500
  50.2 18.7 %collective-permute-start.12 = (bf16[4,368,128]{2,1,0:T(8,128)(2,1)S(1)}, bf16[4,368,128]{2,1,0:T(8,128)(2,1)S(1)}, u32[]{:S(2)}, u32[]{:S(2)}) collective-permute-start(bf16[4,368,128]{2,1,0:T(8,128)(2,1)S(1)} %get-tuple-element.137.refs_0_), channel_id=1, source_target_pairs={{0,4},{1,5},{2,6},{3,7},{4,0},{5,1},{6,2},{7,3},{8,12},{9,13},{10,... | collective-permute-start | bytes 1130504 | tf_op jit(solution)/shard_map/ppermute | solution.py:32
  50.8 18.1 %collective-permute-start.13 = (bf16[4,368,128]{2,1,0:T(8,128)(2,1)S(1)}, bf16[4,368,128]{2,1,0:T(8,128)(2,1)}, u32[]{:S(2)}, u32[]{:S(2)}) collective-permute-start(bf16[4,368,128]{2,1,0:T(8,128)(2,1)S(1)} %collective-permute-done.10.refs_1_), channel_id=1, source_target_pairs={{0,4},{1,5},{2,6},{3,7},{4,0},{5,1},{6,2},{7,3},{8,12},{9,13},{10,... | collective-permute-start | bytes 1130504 | tf_op jit(solution)/shard_map/ppermute | solution.py:32
  52.3 16.6 %collective-permute-start.14 = (bf16[4,368,128]{2,1,0:T(8,128)(2,1)S(1)}, bf16[4,368,128]{2,1,0:T(8,128)(2,1)}, u32[]{:S(2)}, u32[]{:S(2)}) collective-permute-start(bf16[4,368,128]{2,1,0:T(8,128)(2,1)S(1)} %get-tuple-element.141.refs_4_), channel_id=1, source_target_pairs={{0,2},{1,3},{2,0},{3,1},{4,6},{5,7},{6,4},{7,5},{8,10},{9,11},{10,... | collective-permute-start | bytes 1130504 | tf_op jit(solution)/shard_map/ppermute | solution.py:32
  52.8 16.1 %collective-permute-start.15 = (bf16[4,368,128]{2,1,0:T(8,128)(2,1)}, bf16[4,368,128]{2,1,0:T(8,128)(2,1)}, u32[]{:S(2)}, u32[]{:S(2)}) collective-permute-start(bf16[4,368,128]{2,1,0:T(8,128)(2,1)} %collective-permute-done.11.refs_5_), channel_id=1, source_target_pairs={{0,2},{1,3},{2,0},{3,1},{4,6},{5,7},{6,4},{7,5},{8,10},{9,11},{10,... | collective-permute-start | bytes 1130504 | tf_op jit(solution)/shard_map/ppermute | solution.py:32
  61.5 13.3 %copy-start.19 = (bf16[2,576]{1,0:T(2,128)(2,1)S(1)}, bf16[2,576]{1,0:T(2,128)(2,1)}, u32[]{:S(2)}) copy-start(bf16[2,576]{1,0:T(2,128)(2,1)} %gains_ref.3) | copy-start | bytes 6916
  68.8 4.4 %copy-start.15 = (bf16[4,368,128]{2,1,0:T(8,128)(2,1)}, bf16[4,368,128]{2,1,0:T(8,128)(2,1)S(1)}, u32[]{:S(2)}) copy-start(bf16[4,368,128]{2,1,0:T(8,128)(2,1)S(1)} %collective-permute-done.12.refs_2_) | copy-start | bytes 1130500
  68.9 2.2 collective-permute-start.16
  69.4 2.2 collective-permute-start.17
  69.9 3.3 %collective-permute-start.18 = (bf16[4,368,128]{2,1,0:T(8,128)(2,1)S(1)}, bf16[4,368,128]{2,1,0:T(8,128)(2,1)S(1)}, u32[]{:S(2)}, u32[]{:S(2)}) collective-permute-start(bf16[4,368,128]{2,1,0:T(8,128)(2,1)S(1)} %collective-permute-done.12.refs_2_), channel_id=1, source_target_pairs={{0,1},{1,0},{2,3},{3,2},{4,5},{5,4},{6,7},{7,6},{8,9},{9,8},{10,11... | collective-permute-start | bytes 1130504 | tf_op jit(solution)/shard_map/ppermute | solution.py:32
  69.9 12.1 %collective-permute-start.19 = (bf16[4,368,128]{2,1,0:T(8,128)(2,1)}, bf16[4,368,128]{2,1,0:T(8,128)(2,1)}, u32[]{:S(2)}, u32[]{:S(2)}) collective-permute-start(bf16[4,368,128]{2,1,0:T(8,128)(2,1)} %collective-permute-done.13.refs_3_), channel_id=1, source_target_pairs={{0,1},{1,0},{2,3},{3,2},{4,5},{5,4},{6,7},{7,6},{8,9},{9,8},{10,11... | collective-permute-start | bytes 1130504 | tf_op jit(solution)/shard_map/ppermute | solution.py:32
  70.4 11.7 %collective-permute-start.20 = (bf16[4,368,128]{2,1,0:T(8,128)(2,1)S(1)}, bf16[4,368,128]{2,1,0:T(8,128)(2,1)}, u32[]{:S(2)}, u32[]{:S(2)}) collective-permute-start(bf16[4,368,128]{2,1,0:T(8,128)(2,1)S(1)} %get-tuple-element.141.refs_4_), channel_id=1, source_target_pairs={{0,1},{1,0},{2,3},{3,2},{4,5},{5,4},{6,7},{7,6},{8,9},{9,8},{10,11... | collective-permute-start | bytes 1130504 | tf_op jit(solution)/shard_map/ppermute | solution.py:32
  71.1 2.2 copy-start.16
  71.1 11.0 %collective-permute-start.21 = (bf16[4,368,128]{2,1,0:T(8,128)(2,1)}, bf16[4,368,128]{2,1,0:T(8,128)(2,1)}, u32[]{:S(2)}, u32[]{:S(2)}) collective-permute-start(bf16[4,368,128]{2,1,0:T(8,128)(2,1)} %collective-permute-done.11.refs_5_), channel_id=1, source_target_pairs={{0,1},{1,0},{2,3},{3,2},{4,5},{5,4},{6,7},{7,6},{8,9},{9,8},{10,11... | collective-permute-start | bytes 1130504 | tf_op jit(solution)/shard_map/ppermute | solution.py:32
  71.6 1.6 copy-start.17
  71.6 10.5 %collective-permute-start.22 = (bf16[4,368,128]{2,1,0:T(8,128)(2,1)}, bf16[4,368,128]{2,1,0:T(8,128)(2,1)}, u32[]{:S(2)}, u32[]{:S(2)}) collective-permute-start(bf16[4,368,128]{2,1,0:T(8,128)(2,1)} %collective-permute-done.14.refs_6_), channel_id=1, source_target_pairs={{0,1},{1,0},{2,3},{3,2},{4,5},{5,4},{6,7},{7,6},{8,9},{9,8},{10,11... | collective-permute-start | bytes 1130504 | tf_op jit(solution)/shard_map/ppermute | solution.py:32
  74.0 8.1 %collective-permute-start.23 = (bf16[4,368,128]{2,1,0:T(8,128)(2,1)}, bf16[4,368,128]{2,1,0:T(8,128)(2,1)}, u32[]{:S(2)}, u32[]{:S(2)}) collective-permute-start(bf16[4,368,128]{2,1,0:T(8,128)(2,1)} %collective-permute-done.15.refs_7_), channel_id=1, source_target_pairs={{0,1},{1,0},{2,3},{3,2},{4,5},{5,4},{6,7},{7,6},{8,9},{9,8},{10,11... | collective-permute-start | bytes 1130504 | tf_op jit(solution)/shard_map/ppermute | solution.py:32
  82.1 7.2 %copy-start = (bf16[1024,576]{1,0:T(8,128)(2,1)S(1)}, bf16[1024,576]{1,0:T(8,128)(2,1)}, u32[]{:S(2)}) copy-start(bf16[1024,576]{1,0:T(8,128)(2,1)} %copy.33.tokens_in.tokens_ref) | copy-start | bytes 3538948
  82.1 7.2 %copy-start.11 = (bf16[1024,192]{1,0:T(8,128)(2,1)S(1)}, bf16[1024,192]{1,0:T(8,128)(2,1)}, u32[]{:S(2)}) copy-start(bf16[1024,192]{1,0:T(8,128)(2,1)} %get-tuple-element.134.mixed_ref) | copy-start | bytes 1179652
  82.1 7.2 %copy-start.12 = (bf16[1024,192]{1,0:T(8,128)(2,1)S(1)}, bf16[1024,192]{1,0:T(8,128)(2,1)}, u32[]{:S(2)}) copy-start(bf16[1024,192]{1,0:T(8,128)(2,1)} %get-tuple-element.136.mixed_ref) | copy-start | bytes 1179652
  89.3 2.9 %copy-start.21 = (bf16[1536,576]{1,0:T(8,128)(2,1)S(1)}, bf16[1536,576]{1,0:T(8,128)(2,1)}, u32[]{:S(2)}) copy-start(bf16[1536,576]{1,0:T(8,128)(2,1)} %get-tuple-element.148) | copy-start | bytes 5308420
  96.8 1.5 copy-start.22
  98.3 2.6 %copy-start.23 = (bf16[576,1536]{1,0:T(8,128)(2,1)S(1)}, bf16[576,1536]{1,0:T(8,128)(2,1)}, u32[]{:S(2)}) copy-start(bf16[576,1536]{1,0:T(8,128)(2,1)} %get-tuple-element.147) | copy-start | bytes 5308420
  115.5 4.9 %copy-start.1 = (f32[1024,576]{1,0:T(8,128)}, f32[1024,576]{1,0:T(8,128)S(1)}, u32[]{:S(2)}) copy-start(f32[1024,576]{1,0:T(8,128)S(1)} %subtract_add_fusion.mid_back_ref) | copy-start | bytes 7077892
  115.5 2.4 copy-start.13
  124.2 3.9 %copy-start.25 = (bf16[1024,1536]{1,0:T(8,128)(2,1)S(1)}, bf16[1024,1536]{1,0:T(8,128)(2,1)}, u32[]{:S(2)}) copy-start(bf16[1024,1536]{1,0:T(8,128)(2,1)} %get-tuple-element.234) | copy-start | bytes 9437188
  142.9 11.2 %copy-start.2 = (bf16[16,736,128]{2,1,0:T(8,128)(2,1)S(1)}, bf16[16,736,128]{2,1,0:T(8,128)(2,1)}, u32[]{:S(2)}) copy-start(bf16[16,736,128]{2,1,0:T(8,128)(2,1)} %get-tuple-element.151) | copy-start | bytes 9043972
  142.9 11.2 %collective-permute-start.24 = (bf16[16,736,128]{2,1,0:T(8,128)(2,1)}, bf16[16,736,128]{2,1,0:T(8,128)(2,1)}, u32[]{:S(2)}, u32[]{:S(2)}) collective-permute-start(bf16[16,736,128]{2,1,0:T(8,128)(2,1)} %get-tuple-element.152), channel_id=1, source_target_pairs={{0,1},{1,0},{2,3},{3,2},{4,5},{5,4},{6,7},{7,6},{8,9},{9,8},{10,11... | collective-permute-start | bytes 9043976 | tf_op jit(solution)/shard_map/ppermute | solution.py:32
  157.4 13.5 %collective-permute-start.27 = (bf16[4,368,128]{2,1,0:T(8,128)(2,1)}, bf16[4,368,128]{2,1,0:T(8,128)(2,1)S(1)}, u32[]{:S(2)}, u32[]{:S(2)}) collective-permute-start(bf16[4,368,128]{2,1,0:T(8,128)(2,1)} %get-tuple-element.163), channel_id=1, source_target_pairs={{0,4},{1,5},{2,6},{3,7},{4,0},{5,1},{6,2},{7,3},{8,12},{9,13},{10,... | collective-permute-start | bytes 1130504 | tf_op jit(solution)/shard_map/ppermute | solution.py:32
  157.9 13.1 %collective-permute-start.26 = (bf16[4,368,128]{2,1,0:T(8,128)(2,1)S(1)}, bf16[4,368,128]{2,1,0:T(8,128)(2,1)S(1)}, u32[]{:S(2)}, u32[]{:S(2)}) collective-permute-start(bf16[4,368,128]{2,1,0:T(8,128)(2,1)S(1)} %get-tuple-element.161), channel_id=1, source_target_pairs={{0,2},{1,3},{2,0},{3,1},{4,6},{5,7},{6,4},{7,5},{8,10},{9,11},{10,... | collective-permute-start | bytes 1130504 | tf_op jit(solution)/shard_map/ppermute | solution.py:32
  158.4 26.0 %collective-permute-start.25 = (bf16[4,368,128]{2,1,0:T(8,128)(2,1)S(1)}, bf16[4,368,128]{2,1,0:T(8,128)(2,1)S(1)}, u32[]{:S(2)}, u32[]{:S(2)}) collective-permute-start(bf16[4,368,128]{2,1,0:T(8,128)(2,1)S(1)} %get-tuple-element.159), channel_id=1, source_target_pairs={{0,2},{1,3},{2,0},{3,1},{4,6},{5,7},{6,4},{7,5},{8,10},{9,11},{10,... | collective-permute-start | bytes 1130504 | tf_op jit(solution)/shard_map/ppermute | solution.py:32
  171.2 13.3 %collective-permute-start.28 = (bf16[4,368,128]{2,1,0:T(8,128)(2,1)S(1)}, bf16[4,368,128]{2,1,0:T(8,128)(2,1)S(1)}, u32[]{:S(2)}, u32[]{:S(2)}) collective-permute-start(bf16[4,368,128]{2,1,0:T(8,128)(2,1)S(1)} %add_convert_fusion.2), channel_id=1, source_target_pairs={{0,4},{1,5},{2,6},{3,7},{4,0},{5,1},{6,2},{7,3},{8,12},{9,13},{10,... | collective-permute-start | bytes 1130504 | tf_op jit(solution)/shard_map/ppermute | solution.py:32
  172.7 16.5 %collective-permute-start.29 = (bf16[4,368,128]{2,1,0:T(8,128)(2,1)S(1)}, bf16[4,368,128]{2,1,0:T(8,128)(2,1)S(1)}, u32[]{:S(2)}, u32[]{:S(2)}) collective-permute-start(bf16[4,368,128]{2,1,0:T(8,128)(2,1)S(1)} %get-tuple-element.170), channel_id=1, source_target_pairs={{0,4},{1,5},{2,6},{3,7},{4,0},{5,1},{6,2},{7,3},{8,12},{9,13},{10,... | collective-permute-start | bytes 1130504 | tf_op jit(solution)/shard_map/ppermute | solution.py:32
  173.3 16.0 %collective-permute-start.30 = (bf16[4,368,128]{2,1,0:T(8,128)(2,1)S(1)}, bf16[4,368,128]{2,1,0:T(8,128)(2,1)S(1)}, u32[]{:S(2)}, u32[]{:S(2)}) collective-permute-start(bf16[4,368,128]{2,1,0:T(8,128)(2,1)S(1)} %add_convert_fusion.1), channel_id=1, source_target_pairs={{0,2},{1,3},{2,0},{3,1},{4,6},{5,7},{6,4},{7,5},{8,10},{9,11},{10,... | collective-permute-start | bytes 1130504 | tf_op jit(solution)/shard_map/ppermute | solution.py:32
  189.5 27.3 %collective-permute-start.31 = (bf16[736,128]{1,0:T(8,128)(2,1)S(1)}, bf16[736,128]{1,0:T(8,128)(2,1)S(1)}, u32[]{:S(2)}, u32[]{:S(2)}) collective-permute-start(bf16[736,128]{1,0:T(8,128)(2,1)S(1)} %pad_maximum_fusion.9), channel_id=1, source_target_pairs={{0,8},{1,9},{2,10},{3,11},{4,12},{5,13},{6,14},{7,15},{8,0},{9,1},... | collective-permute-start | bytes 565256 | tf_op jit(solution)/shard_map/ppermute | solution.py:32
  192.1 24.7 %collective-permute-start.32 = (bf16[736,128]{1,0:T(8,128)(2,1)S(1)}, bf16[736,128]{1,0:T(8,128)(2,1)S(1)}, u32[]{:S(2)}, u32[]{:S(2)}) collective-permute-start(bf16[736,128]{1,0:T(8,128)(2,1)S(1)} %pad_maximum_fusion.10), channel_id=1, source_target_pairs={{0,16},{1,17},{2,18},{3,19},{4,20},{5,21},{6,22},{7,23},{8,24},{9,... | collective-permute-start | bytes 565256 | tf_op jit(solution)/shard_map/ppermute | solution.py:32
  192.9 23.8 %collective-permute-start.33 = (bf16[736,128]{1,0:T(8,128)(2,1)S(1)}, bf16[736,128]{1,0:T(8,128)(2,1)S(1)}, u32[]{:S(2)}, u32[]{:S(2)}) collective-permute-start(bf16[736,128]{1,0:T(8,128)(2,1)S(1)} %pad_maximum_fusion.11), channel_id=1, source_target_pairs={{0,24},{1,25},{2,26},{3,27},{4,28},{5,29},{6,30},{7,31},{8,16},{9,... | collective-permute-start | bytes 565256 | tf_op jit(solution)/shard_map/ppermute | solution.py:32
  207.3 4.9 %copy-start.20 = (f32[1,576]{1,0:T(1,128)S(1)}, f32[1,576]{1,0:T(1,128)}, u32[]{:S(2)}) copy-start(f32[1,576]{1,0:T(1,128)} %get-tuple-element.187) | copy-start | bytes 6916
  216.8 6.7 %collective-permute-start.34 = (bf16[16,144,128]{2,1,0:T(8,128)(2,1)}, bf16[16,144,128]{2,1,0:T(8,128)(2,1)S(1)}, u32[]{:S(2)}, u32[]{:S(2)}) collective-permute-start(bf16[16,144,128]{2,1,0:T(8,128)(2,1)} %get-tuple-element.194), channel_id=1, source_target_pairs={{0,1},{1,0},{2,3},{3,2},{4,5},{5,4},{6,7},{7,6},{8,9},{9,8},{10,11... | collective-permute-start | bytes 1769480 | tf_op jit(solution)/shard_map/ppermute | solution.py:32
  222.0 1.5 copy-start.9
  223.4 15.9 %copy-start.5 = (bf16[1024,576]{1,0:T(8,128)(2,1)S(1)}, bf16[1024,576]{1,0:T(8,128)(2,1)}, u32[]{:S(2)}) copy-start(bf16[1024,576]{1,0:T(8,128)(2,1)} %get-tuple-element.221) | copy-start | bytes 3538948
  223.7 6.7 %collective-permute-start.35 = (bf16[4,144,128]{2,1,0:T(8,128)(2,1)S(1)}, bf16[4,144,128]{2,1,0:T(8,128)(2,1)S(1)}, u32[]{:S(2)}, u32[]{:S(2)}) collective-permute-start(bf16[4,144,128]{2,1,0:T(8,128)(2,1)S(1)} %get-tuple-element.197), channel_id=1, source_target_pairs={{0,2},{1,3},{2,0},{3,1},{4,6},{5,7},{6,4},{7,5},{8,10},{9,11},{10,... | collective-permute-start | bytes 442376 | tf_op jit(solution)/shard_map/ppermute | solution.py:32
  224.3 8.2 %collective-permute-start.36 = (bf16[4,144,128]{2,1,0:T(8,128)(2,1)S(1)}, bf16[4,144,128]{2,1,0:T(8,128)(2,1)S(1)}, u32[]{:S(2)}, u32[]{:S(2)}) collective-permute-start(bf16[4,144,128]{2,1,0:T(8,128)(2,1)S(1)} %get-tuple-element.198), channel_id=1, source_target_pairs={{0,4},{1,5},{2,6},{3,7},{4,0},{5,1},{6,2},{7,3},{8,12},{9,13},{10,... | collective-permute-start | bytes 442376 | tf_op jit(solution)/shard_map/ppermute | solution.py:32
  225.8 8.3 %collective-permute-start.37 = (bf16[4,144,128]{2,1,0:T(8,128)(2,1)S(1)}, bf16[4,144,128]{2,1,0:T(8,128)(2,1)S(1)}, u32[]{:S(2)}, u32[]{:S(2)}) collective-permute-start(bf16[4,144,128]{2,1,0:T(8,128)(2,1)S(1)} %get-tuple-element.199), channel_id=1, source_target_pairs={{0,6},{1,7},{2,4},{3,5},{4,2},{5,3},{6,0},{7,1},{8,14},{9,15},{10,... | collective-permute-start | bytes 442376 | tf_op jit(solution)/shard_map/ppermute | solution.py:32
  234.2 6.5 %collective-permute-start.38 = (bf16[144,128]{1,0:T(8,128)(2,1)S(1)}, bf16[144,128]{1,0:T(8,128)(2,1)S(1)}, u32[]{:S(2)}, u32[]{:S(2)}) collective-permute-start(bf16[144,128]{1,0:T(8,128)(2,1)S(1)} %get-tuple-element.203), channel_id=1, source_target_pairs={{0,8},{1,9},{2,10},{3,11},{4,12},{5,13},{6,14},{7,15},{8,0},{9,1},... | collective-permute-start | bytes 110600 | tf_op jit(solution)/shard_map/ppermute | solution.py:32
  235.3 5.4 %collective-permute-start.39 = (bf16[144,128]{1,0:T(8,128)(2,1)S(1)}, bf16[144,128]{1,0:T(8,128)(2,1)S(1)}, u32[]{:S(2)}, u32[]{:S(2)}) collective-permute-start(bf16[144,128]{1,0:T(8,128)(2,1)S(1)} %get-tuple-element.204), channel_id=1, source_target_pairs={{0,16},{1,17},{2,18},{3,19},{4,20},{5,21},{6,22},{7,23},{8,24},{9,... | collective-permute-start | bytes 110600 | tf_op jit(solution)/shard_map/ppermute | solution.py:32
  237.1 5.8 %collective-permute-start.40 = (bf16[144,128]{1,0:T(8,128)(2,1)S(1)}, bf16[144,128]{1,0:T(8,128)(2,1)S(1)}, u32[]{:S(2)}, u32[]{:S(2)}) collective-permute-start(bf16[144,128]{1,0:T(8,128)(2,1)S(1)} %get-tuple-element.205), channel_id=1, source_target_pairs={{0,24},{1,25},{2,26},{3,27},{4,28},{5,29},{6,30},{7,31},{8,16},{9,... | collective-permute-start | bytes 110600 | tf_op jit(solution)/shard_map/ppermute | solution.py:32
  (3 other events, 2.7 us)

commit v2 on v1

--- a/solution.py
+++ b/solution.py
@@ -509,7 +509,8 @@
     tokens_ref, gains_ref, wide_ref, cosine_ref, sine_ref, mid_back_ref, *refs, heads
 ):
     backs = refs[: 2 * heads]
-    input_grad_ref, tiled_ref, gain_ref, fields, normed_t = refs[2 * heads :]
+    input_grad_ref, gain_ref, *tiled_refs, fields, normed_t = refs[2 * heads :]
+    places = [(ref, at) for ref in tiled_refs for at in range(ref.shape[0])]
     half = HEAD_DIM
     group = HEADS // heads
     wide_heads = [(backs[2 * (at // group)], at % group * half) for at in range(HEADS)]
@@ -535,7 +536,8 @@
         stop = min(start + 2, count)
         pair = dot_nn(normed_t[...], fields[:, start * LANES : stop * LANES])
         for at in range(start, stop):
-            tiled_ref[at] = pair[:, (at - start) * LANES : (at - start + 1) * LANES]
+            ref, inner = places[at]
+            ref[inner] = pair[:, (at - start) * LANES : (at - start + 1) * LANES]
     one_back = dot_nt(fields[...], wide_ref[...])
     weighted = one_back * first_gain(gains_ref)
     cubed = inv_rms * inv_rms * inv_rms
@@ -553,8 +555,11 @@
         functools.partial(finish_kernel, heads=heads),
         [
             jax.ShapeDtypeStruct(tokens.shape, jnp.bfloat16),
-            jax.ShapeDtypeStruct((wide.shape[1] // LANES, width, LANES), jnp.float32),
             jax.ShapeDtypeStruct((1, width), jnp.float32),
+        ]
+        + [
+            jax.ShapeDtypeStruct((tiles_of(count * HEAD_DIM), width, LANES), jnp.float32)
+            for count in (HEADS, heads, heads)
         ],
         [
             pltpu.VMEM((rows, wide.shape[1]), jnp.bfloat16),
@@ -887,14 +892,10 @@
     backs.append(back_of(1, mixed_back))
     mixed_back, backs = feed_sum.second_half_stage((mixed_back, backs))
     backs.append(back_of(2, mixed_back))
-    backs = feed_sum.line_stage(backs)
-    input_grad, tiled, gain_one = finish(tokens, norm_gains, wide_mat, cosine, sine, mid_back, backs)
+    backs, output = feed_sum.line_stage((backs, output))
+    input_grad, gain_one, *tiled = finish(tokens, norm_gains, wide_mat, cosine, sine, mid_back, backs)
     gains_back = jnp.concatenate([gain_one, gain_two[None]], 0)
-    cuts = [0]
-    for _, wide in shapes[:3]:
-        cuts.append(cuts[-1] + tiles_of(wide))
-    grads = tuple(tiled[start:stop] for start, stop in zip(cuts, cuts[1:]))
-    mix_sum = GradSum(grads, shapes[:3], devices, gains_back)
+    mix_sum = GradSum(tuple(tiled), shapes[:3], devices, gains_back)
     if feed_sum.stages:
         feed_sum.arrived = mix_sum.core_stage(feed_sum.arrived)
     input_grad = mix_sum.plane_stage(input_grad)

time: 248 us -> 245 us (0.988)
  local copies, waits for them, and re-layouts: 18.5 us -> 13.3 us
  matrix products: 45.8 us -> 50.8 us
  waiting for transfers between devices: 31.5 us -> 27.6 us
    slice x2 -> x0, local copies, waits for them, and re-layouts: 4.93 us -> none  [body(): grads = tuple((tiled[start:stop] for start, stop in zip(cuts, cuts[1:])))]
    ppermute x41, waiting for transfers between devices: 31.5 us -> 27.6 us  [swap(): lax.ppermute(field, 'dp', [(place, place ^ mask) for place in range(devic...]
  transfers between devices with their start and end apart: 41 -> 41, of which waited for: 14 -> 13; matrix products, arithmetic and copies ran while one was open for 9% -> 7% of each run, Pallas kernels for 33% -> 34%
where the time goes in v2:
time: 245 us; the launch traced here: 242 us
  Pallas kernels  99.5 us (41%)
  matrix products  50.8 us (21%)
  starting transfers between devices  39.6 us (16%)
  waiting for transfers between devices  27.6 us (11%)
  local copies, waits for them, and re-layouts  13.3 us (5%)
  other arithmetic  9.39 us (4%)
    ppermute x41, starting transfers between devices, swap(): lax.ppermute(field, 'dp', [(place, place ^ mask) for place in range(devic...  39.6 us
    pallas_call x3, Pallas kernels, attend_back(): pl.pallas_call(functools.partial(attend_back_kernel, head=head, group=gro...  32.9 us
    ppermute x41, waiting for transfers between devices, swap(): lax.ppermute(field, 'dp', [(place, place ^ mask) for place in range(devic...  27.6 us
    pallas_call x3, Pallas kernels, attend(): pl.pallas_call(functools.partial(attend_kernel, head=head, group=group),...  21.7 us
    dot_general x4, matrix products, outer_prod(): lax.dot_general(left, right, (((0,), (0,)), ((), ())), preferred_element_...  15.5 us
    pallas_call x2, Pallas kernels, pack_grads(): pl.pallas_call(functools.partial(pack_kernel, devices=devices, shapes=sha...  14.2 us
    pallas_call x1, Pallas kernels, vmem_call(): pl.pallas_call(kernel, out_shape=out_shape, in_specs=[pl.BlockSpec(memory...  13.1 us
    dot_general x4, matrix products, times_transposed(): lax.dot_general(left, matrix, (((1,), (1,)), ((), ())), preferred_element...  13 us
  transfers between devices with their start and end apart: 41, of which 13 were waited for; matrix products, arithmetic and copies ran while one was open for 7% of the time, Pallas kernels for 34%

profile of v2, /device:TPU:0, one launch (start us, length us, event | category | flops | bytes accessed | tf_op | source)
XLA Modules:
  0.0 241.7 jit_solution(18211847980160659845)
XLA Ops:
  1.4 3.1 %collective-permute-start = (bf16[144,128]{1,0:T(8,128)(2,1)S(1)}, bf16[144,128]{1,0:T(8,128)(2,1)S(1)}, u32[]{:S(2)}, u32[]{:S(2)}) collective-permute-start(bf16[144,128]{1,0:T(8,128)(2,1)S(1)} %fusion.35), channel_id=1, source_target_pairs={{0,8},{1,9},{2,10},{3,11},{4,12},{5,13},{6,14},{7,15},{8,0},{9,1},... | collective-permute-start | bytes 110600 | tf_op jit(solution)/shard_map/ppermute | solution.py:32
  4.5 2.6 %collective-permute-start.1 = (bf16[144,128]{1,0:T(8,128)(2,1)S(1)}, bf16[144,128]{1,0:T(8,128)(2,1)S(1)}, u32[]{:S(2)}, u32[]{:S(2)}) collective-permute-start(bf16[144,128]{1,0:T(8,128)(2,1)S(1)} %fusion.35), channel_id=1, source_target_pairs={{0,16},{1,17},{2,18},{3,19},{4,20},{5,21},{6,22},{7,23},{8,24},{9,... | collective-permute-start | bytes 110600 | tf_op jit(solution)/shard_map/ppermute | solution.py:32
  7.1 0.9 fusion.15
  8.0 2.0 collective-permute-done.1
  10.0 2.8 %collective-permute-done.2 = bf16[144,128]{1,0:T(8,128)(2,1)S(1)} collective-permute-done((bf16[144,128]{1,0:T(8,128)(2,1)S(1)}, bf16[144,128]{1,0:T(8,128)(2,1)S(1)}, u32[]{:S(2)}, u32[]{:S(2)}) %collective-permute-start.2) | collective-permute-done | bytes 36896 | tf_op jit(solution)/shard_map/ppermute | solution.py:32
  12.9 1.6 collective-permute-start.3
  14.4 1.5 collective-permute-start.4
  16.4 1.1 collective-permute-start.7
  17.5 1.8 collective-permute-done.3
  19.3 1.6 collective-permute-start.8
  20.9 1.2 collective-permute-done.4
  22.3 1.6 collective-permute-done.6
  24.0 7.5 %collective-permute-done.7 = bf16[736,128]{1,0:T(8,128)(2,1)S(1)} collective-permute-done((bf16[736,128]{1,0:T(8,128)(2,1)S(1)}, bf16[736,128]{1,0:T(8,128)(2,1)S(1)}, u32[]{:S(2)}, u32[]{:S(2)}) %collective-permute-start.7) | collective-permute-done | bytes 188448 | tf_op jit(solution)/shard_map/ppermute | solution.py:32
  31.7 0.8 copy-done.10
  32.5 1.5 collective-permute-start.10
  34.0 1.5 collective-permute-start.11
  36.2 1.0 copy.40.sine_in.sine_ref
  37.3 1.0 copy.39.cosine_in.cosine_ref
  38.2 1.5 copy.37.tokens_in.tokens_ref
  39.7 3.5 %unpack.2.wide_ref = bf16[576,1152]{1,0:T(8,128)(2,1)} custom-call(s32[1]{0:T(128)} %bitcast.place_ref, bf16[16,144,128]{2,1,0:T(8,128)(2,1)} %copy-done.8, bf16[16,144,128]{2,1,0:T(8,128)(2,1)} %copy-done.10), custom_call_target="tpu_custom_call" | custom-call | flops 100000000 | bytes 1000000 | tf_op jit(solution)/shard_map/unpack/pallas_call | solution.py:145
  43.2 7.2 %project.1.fields_ref = bf16[1024,1152]{1,0:T(8,128)(2,1)} custom-call(bf16[1024,576]{1,0:T(8,128)(2,1)} %copy.37.tokens_in.tokens_ref, f32[1024,128]{1,0:T(8,128)} %copy.39.cosine_in.cosine_ref, f32[1024,128]{1,0:T(8,128)} %copy.40.sine_in.sine_ref, bf16[2,576]{1,0:T(2,128)(2,1)} %gains_ref.3, bf16[576,1152]{1,0:T(8,128)(2,1)} %unpack.2.wide_ref), custom_call_target="tpu_custom_call" | custom-call | flops 100000000 | bytes 1000000 | tf_op jit(solution)/shard_map/project/pallas_call | solution.py:489
  51.0 1.5 collective-permute-start.13
  53.1 1.5 collective-permute-start.15
  54.5 7.2 %attend.3 = (bf16[1024,192]{1,0:T(8,128)(2,1)}, f32[1024,128]{1,0:T(8,128)}) custom-call(bf16[1024,1152]{1,0:T(8,128)(2,1)} %project.1.fields_ref), custom_call_target="tpu_custom_call" | custom-call | flops 100000000 | bytes 1000000 | tf_op jit(solution)/shard_map/attend/pallas_call | solution.py:324
  61.7 7.3 %attend.4 = (bf16[1024,192]{1,0:T(8,128)(2,1)}, f32[1024,128]{1,0:T(8,128)}) custom-call(bf16[1024,1152]{1,0:T(8,128)(2,1)} %project.1.fields_ref), custom_call_target="tpu_custom_call" | custom-call | flops 100000000 | bytes 1000000 | tf_op jit(solution)/shard_map/attend/pallas_call | solution.py:324
  71.8 1.5 collective-permute-done.18.refs_10_
  75.0 7.2 %attend.5 = (bf16[1024,192]{1,0:T(8,128)(2,1)}, f32[1024,128]{1,0:T(8,128)}) custom-call(bf16[1024,1152]{1,0:T(8,128)(2,1)} %project.1.fields_ref), custom_call_target="tpu_custom_call" | custom-call | flops 100000000 | bytes 1000000 | tf_op jit(solution)/shard_map/attend/pallas_call | solution.py:324
  82.2 7.0 %unpack.3 = (bf16[576,1536]{1,0:T(8,128)(2,1)}, bf16[576,1536]{1,0:T(8,128)(2,1)}, bf16[1536,576]{1,0:T(8,128)(2,1)}, bf16[576,576]{1,0:T(8,128)(2,1)}) custom-call(s32[1]{0:T(128)} %bitcast.place_ref, bf16[4,368,128]{2,1,0:T(8,128)(2,1)} %copy-done.3, bf16[4,368,128]{2,1,0:T(8,128)(2,1)} %copy-done.14, bf16[4,368,128]{2,1,0:T(8,128)(2,1)} %copy-done.15, ...), custom_call_target="tpu_custom_call" | custom-call | flops 100000000 | bytes 1000000 | tf_op jit(solution)/shard_map/unpack/pallas_call | solution.py:145
  89.3 2.8 %multiply_reduce_fusion.2 = (f32[1024]{0:T(1024)S(1)}, f32[1024,576]{1,0:T(8,128)S(1)}) fusion(bf16[576,576]{1,0:T(8,128)(2,1)} %get-tuple-element.148, bf16[1024,192]{1,0:T(8,128)(2,1)S(1)} %copy-done.12, bf16[1024,192]{1,0:T(8,128)(2,1)S(1)} %copy-done.11, bf16[1024,192]{1,0:T(8,128)(2,1)} %get-tuple-element.136.mixed_ref, bf16[1024,576]{1,0:T(8,128)(2,1)S(1)} %copy-done), kind=kOutput, calls=%fused_computation.14 | convolution fusion | flops 685374464 | bytes 5386240 | tf_op jit(solution)/shard_map/dot_general | solution.py:855
  92.1 2.7 %fusion.38 = f32[1536,1024]{1,0:T(8,128)S(1)} fusion(bf16[1536,576]{1,0:T(8,128)(2,1)S(1)} %copy-done.20, bf16[1024,576]{0,1:T(8,128)(2,1)S(1)} %copy-done.7), kind=kOutput, calls=%fused_computation.116 | convolution fusion | flops 1811939328 | bytes 9240576 | tf_op jit(solution)/shard_map/dot_general | solution.py:613
  95.2 1.2 copy-done.21
  96.3 5.1 %fusion.39 = f32[1024,1536]{0,1:T(8,128)} fusion(bf16[1024,576]{1,0:T(8,128)(2,1)S(1)} %multiply_convert_fusion.1, bf16[576,1536]{1,0:T(8,128)(2,1)S(1)} %copy-done.21), kind=kOutput, calls=%fused_computation.117 | convolution fusion | flops 1811939328 | bytes 9240576 | tf_op jit(solution)/shard_map/dot_general | solution.py:859
  101.4 9.2 %multiply_convert_fusion = (bf16[1024,1536]{0,1:T(8,128)(2,1)}, bf16[1024,1536]{0,1:T(8,128)(2,1)S(1)}, bf16[1024,1536]{0,1:T(8,128)(2,1)}) fusion(f32[1024,1536]{0,1:T(8,128)} %fusion.39, f32[1536,1024]{1,0:T(8,128)S(1)} %fusion.38, bf16[1024,576]{1,0:T(8,128)(2,1)S(1)} %multiply_convert_fusion.1, bf16[576,1536]{1,0:T(8,128)(2,1)S(1)} %copy-done.22), kind=kOutput, calls=%fused_computation.6 | convolution fusion | flops 1835532288 | bytes 24969216 | tf_op jit(solution)/shard_map/dot_general | solution.py:860
  110.6 4.6 %fusion.43 = f32[1024,576]{1,0:T(8,128)S(1)} fusion(bf16[1024,1536]{0,1:T(8,128)(2,1)} %get-tuple-element.240, bf16[576,1536]{1,0:T(8,128)(2,1)S(1)} %copy-done.22), kind=kOutput, calls=%fused_computation.121 | convolution fusion | flops 1811939328 | bytes 7274496 | tf_op jit(solution)/shard_map/dot_general | solution.py:613
  115.2 3.4 %multiply_reduce_fusion = (f32[576]{0:T(1024)S(1)}, f32[1024]{0:T(1024)S(1)}, f32[1024,576]{1,0:T(8,128)S(1)}) fusion(f32[1024,576]{1,0:T(8,128)S(1)} %get-tuple-element.284, f32[1024]{0:T(1024)S(1)} %get-tuple-element.279, f32[576]{0:T(1024)S(1)} %convert_reduce_fusion, f32[1024,576]{1,0:T(8,128)S(1)} %fusion.43, ...), kind=kOutput, calls=%fused_computation.9 | convolution fusion | flops 1816066560 | bytes 12005888 | tf_op jit(solution)/shard_map/dot_general | solution.py:613
  118.6 1.1 subtract_add_fusion.mid_back_ref
  119.7 2.4 %convolution_convert_fusion.back_ref = bf16[1024,576]{1,0:T(8,128)(2,1)} fusion(bf16[576,576]{1,0:T(8,128)(2,1)S(1)} %copy-done.23, f32[1024,576]{1,0:T(8,128)S(1)} %subtract_add_fusion.mid_back_ref), kind=kOutput, calls=%fused_computation.17 | convolution fusion | flops 680656896 | bytes 4202496 | tf_op jit(solution)/shard_map/dot_general | solution.py:613
  122.1 2.5 %fusion.6.refs_3_ = f32[576,576]{1,0:T(8,128)} fusion(f32[1024,576]{1,0:T(8,128)S(1)} %subtract_add_fusion.mid_back_ref, bf16[1024,192]{1,0:T(8,128)(2,1)S(1)} %copy-done.12, bf16[1024,192]{1,0:T(8,128)(2,1)S(1)} %copy-done.11, bf16[1024,192]{1,0:T(8,128)(2,1)S(1)} %copy-done.13), kind=kOutput, calls=%fused_computation.30 | convolution fusion | flops 683606016 | bytes 4866048 | tf_op jit(solution)/shard_map/dot_general | solution.py:607
  124.6 4.2 %fusion.41.refs_1_ = f32[576,1536]{1,0:T(8,128)} fusion(bf16[1024,576]{1,0:T(8,128)(2,1)S(1)} %multiply_convert_fusion.1, bf16[1024,1536]{0,1:T(8,128)(2,1)S(1)} %copy-done.25), kind=kOutput, calls=%fused_computation.119 | convolution fusion | flops 1811939328 | bytes 7864320 | tf_op jit(solution)/shard_map/dot_general | solution.py:607
  128.8 4.2 %fusion.40.refs_0_ = f32[576,1536]{1,0:T(8,128)} fusion(bf16[1024,576]{1,0:T(8,128)(2,1)S(1)} %multiply_convert_fusion.1, bf16[1024,1536]{0,1:T(8,128)(2,1)S(1)} %get-tuple-element.239), kind=kOutput, calls=%fused_computation.118 | convolution fusion | flops 1811939328 | bytes 7864320 | tf_op jit(solution)/shard_map/dot_general | solution.py:607
  133.0 4.6 %fusion.42.refs_2_ = f32[1536,576]{1,0:T(8,128)} fusion(bf16[1024,1536]{0,1:T(8,128)(2,1)S(1)} %copy-done.24, bf16[1024,576]{0,1:T(8,128)(2,1)S(1)} %copy-done.7), kind=kOutput, calls=%fused_computation.120 | convolution fusion | flops 1811939328 | bytes 7864320 | tf_op jit(solution)/shard_map/dot_general | solution.py:607
  137.6 10.2 %pack.2 = (bf16[16,736,128]{2,1,0:T(8,128)(2,1)}, bf16[16,736,128]{2,1,0:T(8,128)(2,1)}) custom-call(s32[1]{0:T(128)} %bitcast.place_ref, f32[576,1536]{1,0:T(8,128)} %fusion.40.refs_0_, f32[576,1536]{1,0:T(8,128)} %fusion.41.refs_1_, f32[1536,576]{1,0:T(8,128)} %fusion.42.refs_2_, f32[576,576]{1,0:T(8,128)} %fusion.6.refs_3_), custom_call_target="tpu_custom_call" | custom-call | flops 100000000 | bytes 1000000 | tf_op jit(solution)/shard_map/pack/pallas_call | solution.py:244
  148.2 10.8 %attend_back.3 = (f32[1024,192]{1,0:T(8,128)}, f32[1024,128]{1,0:T(8,128)}) custom-call(bf16[1024,1152]{1,0:T(8,128)(2,1)} %project.1.fields_ref, bf16[1024,576]{1,0:T(8,128)(2,1)} %convolution_convert_fusion.back_ref, bf16[1024,192]{1,0:T(8,128)(2,1)} %get-tuple-element.136.mixed_ref, f32[1024,128]{1,0:T(8,128)} %get-tuple-element.157.total_ref), custom_call_target="tpu_custom_call" | custom-call | flops 100000000 | bytes 1000000 | tf_op jit(solution)/shard_map/attend_back/pallas_call | solution.py:400
  159.0 3.4 %add_convert_fusion.3 = (bf16[4,368,128]{2,1,0:T(8,128)(2,1)}, bf16[4,368,128]{2,1,0:T(8,128)(2,1)S(1)}, bf16[4,368,128]{2,1,0:T(8,128)(2,1)S(1)}, bf16[4,368,12...) fusion(bf16[16,736,128]{2,1,0:T(8,128)(2,1)} %collective-permut, ...), kind=kLoop, calls=%fused_computation.21 | loop fusion | flops 6029312 | bytes 9043968 | tf_op jit(solution)/shard_map/convert_element_type | solution.py:750
  163.5 1.5 collective-permute-start.25
  165.0 1.5 collective-permute-start.29
  166.5 11.2 %attend_back.4 = (f32[1024,192]{1,0:T(8,128)}, f32[1024,128]{1,0:T(8,128)}) custom-call(bf16[1024,1152]{1,0:T(8,128)(2,1)} %project.1.fields_ref, bf16[1024,576]{1,0:T(8,128)(2,1)} %convolution_convert_fusion.back_ref, bf16[1024,192]{1,0:T(8,128)(2,1)} %get-tuple-element.137.mixed_ref, f32[1024,128]{1,0:T(8,128)} %get-tuple-element.168.total_ref), custom_call_target="tpu_custom_call" | custom-call | flops 100000000 | bytes 1000000 | tf_op jit(solution)/shard_map/attend_back/pallas_call | solution.py:400
  179.0 5.1 %add_convert_fusion = bf16[1024,576]{1,0:T(8,128)(2,1)S(1)} fusion(f32[1024,576]{1,0:T(8,128)S(1)} %get-tuple-element.284, bf16[1024,1536]{0,1:T(8,128)(2,1)} %get-tuple-element.238, bf16[1536,576]{1,0:T(8,128)(2,1)} %get-tuple-element.149), kind=kOutput, calls=%fused_computation.10 | convolution fusion | flops 1813118976 | bytes 8454144 | tf_op jit(solution)/shard_map/dot_general | solution.py:864
  184.2 10.9 %attend_back.5 = (f32[1024,192]{1,0:T(8,128)}, f32[1024,128]{1,0:T(8,128)}) custom-call(bf16[1024,1152]{1,0:T(8,128)(2,1)} %project.1.fields_ref, bf16[1024,576]{1,0:T(8,128)(2,1)} %convolution_convert_fusion.back_ref, bf16[1024,192]{1,0:T(8,128)(2,1)} %get-tuple-element.139.mixed_ref, f32[1024,128]{1,0:T(8,128)} %get-tuple-element.180.total_ref), custom_call_target="tpu_custom_call" | custom-call | flops 100000000 | bytes 1000000 | tf_op jit(solution)/shard_map/attend_back/pallas_call | solution.py:400
  195.5 2.6 %collective-permute-start.31 = (bf16[736,128]{1,0:T(8,128)(2,1)S(1)}, bf16[736,128]{1,0:T(8,128)(2,1)S(1)}, u32[]{:S(2)}, u32[]{:S(2)}) collective-permute-start(bf16[736,128]{1,0:T(8,128)(2,1)S(1)} %pad_maximum_fusion.9), channel_id=1, source_target_pairs={{0,8},{1,9},{2,10},{3,11},{4,12},{5,13},{6,14},{7,15},{8,0},{9,1},... | collective-permute-start | bytes 565256 | tf_op jit(solution)/shard_map/ppermute | solution.py:32
  198.2 2.3 collective-permute-start.33
  200.5 13.1 %finish.1 = (bf16[1024,576]{1,0:T(8,128)(2,1)}, f32[1,576]{1,0:T(1,128)}, f32[5,576,128]{2,1,0:T(8,128)}, f32[2,576,128]{2,1,0:T(8,128)}, f32[2,576,128]{2,1,0:T(8,128)}) custom-call(bf16[1024,576]{1,0:T(8,128)(2,1)} %copy.37.tokens_in.tokens_ref, bf16[2,576]{1,0:T(2,128)(2,1)} %gains_ref.3, bf16[576,1152]{1,0:T(8,128)(2,1)} %unpack.2.wide_ref, ...), custom_call_target="tpu_custom_call" | custom-call | flops 100000000 | bytes 1000000 | tf_op jit(solution)/shard_map/finish/pallas_call | solution.py:474
  213.6 1.3 pad_maximum_fusion.13.refs_3_
  214.9 3.9 %pack.3 = (bf16[16,144,128]{2,1,0:T(8,128)(2,1)}, bf16[16,144,128]{2,1,0:T(8,128)(2,1)}) custom-call(s32[1]{0:T(128)} %bitcast.place_ref, f32[5,576,128]{2,1,0:T(8,128)} %get-tuple-element.190.refs_0_, f32[2,576,128]{2,1,0:T(8,128)} %get-tuple-element.191.refs_1_, f32[2,576,128]{2,1,0:T(8,128)} %get-tuple-element.192.refs_2_, ...), custom_call_target="tpu_custom_call" | custom-call | flops 100000000 | bytes 1000000 | tf_op jit(solution)/shard_map/pack/pallas_call | solution.py:244
  218.9 1.4 copy.56
  221.3 1.6 collective-permute-start.35
  222.8 1.6 collective-permute-start.36
  225.5 2.4 collective-permute-done.35
  227.9 3.7 %collective-permute-done.36 = bf16[4,144,128]{2,1,0:T(8,128)(2,1)S(1)} collective-permute-done((bf16[4,144,128]{2,1,0:T(8,128)(2,1)S(1)}, bf16[4,144,128]{2,1,0:T(8,128)(2,1)S(1)}, u32[]{:S(2)}, u32[]{:S(2)}) %collective-permute-start.36) | collective-permute-done | bytes 147488 | tf_op jit(solution)/shard_map/ppermute | solution.py:32
  231.7 1.1 collective-permute-start.38
  232.8 1.0 collective-permute-start.39
  233.8 2.4 collective-permute-start.40
  236.8 1.4 copy.57
  238.2 1.4 collective-permute-done.40
  (143 shorter events, 16.2 us)
Async XLA Ops:
  1.4 6.6 %collective-permute-start = (bf16[144,128]{1,0:T(8,128)(2,1)S(1)}, bf16[144,128]{1,0:T(8,128)(2,1)S(1)}, u32[]{:S(2)}, u32[]{:S(2)}) collective-permute-start(bf16[144,128]{1,0:T(8,128)(2,1)S(1)} %fusion.35), channel_id=1, source_target_pairs={{0,8},{1,9},{2,10},{3,11},{4,12},{5,13},{6,14},{7,15},{8,0},{9,1},... | collective-permute-start | bytes 110600 | tf_op jit(solution)/shard_map/ppermute | solution.py:32
  4.5 5.5 %collective-permute-start.1 = (bf16[144,128]{1,0:T(8,128)(2,1)S(1)}, bf16[144,128]{1,0:T(8,128)(2,1)S(1)}, u32[]{:S(2)}, u32[]{:S(2)}) collective-permute-start(bf16[144,128]{1,0:T(8,128)(2,1)S(1)} %fusion.35), channel_id=1, source_target_pairs={{0,16},{1,17},{2,18},{3,19},{4,20},{5,21},{6,22},{7,23},{8,24},{9,... | collective-permute-start | bytes 110600 | tf_op jit(solution)/shard_map/ppermute | solution.py:32
  7.1 5.8 %collective-permute-start.2 = (bf16[144,128]{1,0:T(8,128)(2,1)S(1)}, bf16[144,128]{1,0:T(8,128)(2,1)S(1)}, u32[]{:S(2)}, u32[]{:S(2)}) collective-permute-start(bf16[144,128]{1,0:T(8,128)(2,1)S(1)} %fusion.35), channel_id=1, source_target_pairs={{0,24},{1,25},{2,26},{3,27},{4,28},{5,29},{6,30},{7,31},{8,16},{9,... | collective-permute-start | bytes 110600 | tf_op jit(solution)/shard_map/ppermute | solution.py:32
  12.9 6.4 %collective-permute-start.3 = (bf16[4,144,128]{2,1,0:T(8,128)(2,1)S(1)}, bf16[4,144,128]{2,1,0:T(8,128)(2,1)S(1)}, u32[]{:S(2)}, u32[]{:S(2)}) collective-permute-start(bf16[4,144,128]{2,1,0:T(8,128)(2,1)S(1)} %pad_maximum_fusion.12), channel_id=1, source_target_pairs={{0,2},{1,3},{2,0},{3,1},{4,6},{5,7},{6,4},{7,5},{8,10},{9,11},{10,... | collective-permute-start | bytes 442376 | tf_op jit(solution)/shard_map/ppermute | solution.py:32
  14.4 7.7 %collective-permute-start.4 = (bf16[4,144,128]{2,1,0:T(8,128)(2,1)S(1)}, bf16[4,144,128]{2,1,0:T(8,128)(2,1)S(1)}, u32[]{:S(2)}, u32[]{:S(2)}) collective-permute-start(bf16[4,144,128]{2,1,0:T(8,128)(2,1)S(1)} %pad_maximum_fusion.12), channel_id=1, source_target_pairs={{0,4},{1,5},{2,6},{3,7},{4,0},{5,1},{6,2},{7,3},{8,12},{9,13},{10,... | collective-permute-start | bytes 442376 | tf_op jit(solution)/shard_map/ppermute | solution.py:32
  16.0 6.2 %collective-permute-start.5 = (bf16[4,144,128]{2,1,0:T(8,128)(2,1)S(1)}, bf16[4,144,128]{2,1,0:T(8,128)(2,1)S(1)}, u32[]{:S(2)}, u32[]{:S(2)}) collective-permute-start(bf16[4,144,128]{2,1,0:T(8,128)(2,1)S(1)} %pad_maximum_fusion.12), channel_id=1, source_target_pairs={{0,6},{1,7},{2,4},{3,5},{4,2},{5,3},{6,0},{7,1},{8,14},{9,15},{10,... | collective-permute-start | bytes 442376 | tf_op jit(solution)/shard_map/ppermute | solution.py:32
  16.4 7.5 %collective-permute-start.6 = (bf16[736,128]{1,0:T(8,128)(2,1)S(1)}, bf16[736,128]{1,0:T(8,128)(2,1)S(1)}, u32[]{:S(2)}, u32[]{:S(2)}) collective-permute-start(bf16[736,128]{1,0:T(8,128)(2,1)S(1)} %fusion.15), channel_id=1, source_target_pairs={{0,8},{1,9},{2,10},{3,11},{4,12},{5,13},{6,14},{7,15},{8,0},{9,1},... | collective-permute-start | bytes 565256 | tf_op jit(solution)/shard_map/ppermute | solution.py:32
  16.4 15.1 %collective-permute-start.7 = (bf16[736,128]{1,0:T(8,128)(2,1)S(1)}, bf16[736,128]{1,0:T(8,128)(2,1)S(1)}, u32[]{:S(2)}, u32[]{:S(2)}) collective-permute-start(bf16[736,128]{1,0:T(8,128)(2,1)S(1)} %fusion.15), channel_id=1, source_target_pairs={{0,16},{1,17},{2,18},{3,19},{4,20},{5,21},{6,22},{7,23},{8,24},{9,... | collective-permute-start | bytes 565256 | tf_op jit(solution)/shard_map/ppermute | solution.py:32
  19.3 12.2 %collective-permute-start.8 = (bf16[736,128]{1,0:T(8,128)(2,1)S(1)}, bf16[736,128]{1,0:T(8,128)(2,1)S(1)}, u32[]{:S(2)}, u32[]{:S(2)}) collective-permute-start(bf16[736,128]{1,0:T(8,128)(2,1)S(1)} %fusion.15), channel_id=1, source_target_pairs={{0,24},{1,25},{2,26},{3,27},{4,28},{5,29},{6,30},{7,31},{8,16},{9,... | collective-permute-start | bytes 565256 | tf_op jit(solution)/shard_map/ppermute | solution.py:32
  22.2 15.0 %copy-start.8 = (bf16[16,144,128]{2,1,0:T(8,128)(2,1)}, bf16[16,144,128]{2,1,0:T(8,128)(2,1)S(1)}, u32[]{:S(2)}) copy-start(bf16[16,144,128]{2,1,0:T(8,128)(2,1)S(1)} %constant_dynamic-update-slice_fusion.refs_0_) | copy-start | bytes 1769476
  22.3 9.4 %collective-permute-start.9 = (bf16[16,144,128]{2,1,0:T(8,128)(2,1)S(1)}, bf16[16,144,128]{2,1,0:T(8,128)(2,1)S(1)}, u32[]{:S(2)}, u32[]{:S(2)}) collective-permute-start(bf16[16,144,128]{2,1,0:T(8,128)(2,1)S(1)} %constant_dynamic-update-slice_fusion.refs_0_), channel_id=1, source_target_pairs={{0,1},{1,0},{2,3},{3,2},{4,5},{5,4},{6,7},{7,6},{8,9},{9,8},{10,11... | collective-permute-start | bytes 1769480 | tf_op jit(solution)/shard_map/ppermute | solution.py:32
  31.6 6.7 %copy-start.6 = (bf16[1024,576]{0,1:T(8,128)(2,1)S(1)}, bf16[1024,576]{0,1:T(8,128)(2,1)}, u32[]{:S(2)}) copy-start(bf16[1024,576]{0,1:T(8,128)(2,1)} %param.10) | copy-start | bytes 3538948
  31.7 37.4 %copy-start.3 = (bf16[4,368,128]{2,1,0:T(8,128)(2,1)}, bf16[4,368,128]{2,1,0:T(8,128)(2,1)S(1)}, u32[]{:S(2)}) copy-start(bf16[4,368,128]{2,1,0:T(8,128)(2,1)S(1)} %get-tuple-element.140.refs_0_) | copy-start | bytes 1130500
  31.7 38.8 %copy-start.4 = (bf16[4,368,128]{2,1,0:T(8,128)(2,1)}, bf16[4,368,128]{2,1,0:T(8,128)(2,1)S(1)}, u32[]{:S(2)}) copy-start(bf16[4,368,128]{2,1,0:T(8,128)(2,1)S(1)} %get-tuple-element.144.refs_4_) | copy-start | bytes 1130500
  32.5 17.9 %collective-permute-start.10 = (bf16[4,368,128]{2,1,0:T(8,128)(2,1)S(1)}, bf16[4,368,128]{2,1,0:T(8,128)(2,1)S(1)}, u32[]{:S(2)}, u32[]{:S(2)}) collective-permute-start(bf16[4,368,128]{2,1,0:T(8,128)(2,1)S(1)} %get-tuple-element.140.refs_0_), channel_id=1, source_target_pairs={{0,2},{1,3},{2,0},{3,1},{4,6},{5,7},{6,4},{7,5},{8,10},{9,11},{10,... | collective-permute-start | bytes 1130504 | tf_op jit(solution)/shard_map/ppermute | solution.py:32
  34.0 16.4 %collective-permute-start.11 = (bf16[4,368,128]{2,1,0:T(8,128)(2,1)S(1)}, bf16[4,368,128]{2,1,0:T(8,128)(2,1)}, u32[]{:S(2)}, u32[]{:S(2)}) collective-permute-start(bf16[4,368,128]{2,1,0:T(8,128)(2,1)S(1)} %get-tuple-element.144.refs_4_), channel_id=1, source_target_pairs={{0,4},{1,5},{2,6},{3,7},{4,0},{5,1},{6,2},{7,3},{8,12},{9,13},{10,... | collective-permute-start | bytes 1130504 | tf_op jit(solution)/shard_map/ppermute | solution.py:32
  50.4 23.8 %copy-start.7 = (bf16[1024,576]{0,1:T(8,128)(2,1)S(1)}, bf16[1024,576]{0,1:T(8,128)(2,1)}, u32[]{:S(2)}) copy-start(bf16[1024,576]{0,1:T(8,128)(2,1)} %param.11) | copy-start | bytes 3538948
  50.4 24.5 %copy-start.14 = (bf16[4,368,128]{2,1,0:T(8,128)(2,1)}, bf16[4,368,128]{2,1,0:T(8,128)(2,1)S(1)}, u32[]{:S(2)}) copy-start(bf16[4,368,128]{2,1,0:T(8,128)(2,1)S(1)} %collective-permute-done.10.refs_1_) | copy-start | bytes 1130500
  50.4 18.7 %collective-permute-start.12 = (bf16[4,368,128]{2,1,0:T(8,128)(2,1)S(1)}, bf16[4,368,128]{2,1,0:T(8,128)(2,1)S(1)}, u32[]{:S(2)}, u32[]{:S(2)}) collective-permute-start(bf16[4,368,128]{2,1,0:T(8,128)(2,1)S(1)} %get-tuple-element.140.refs_0_), channel_id=1, source_target_pairs={{0,4},{1,5},{2,6},{3,7},{4,0},{5,1},{6,2},{7,3},{8,12},{9,13},{10,... | collective-permute-start | bytes 1130504 | tf_op jit(solution)/shard_map/ppermute | solution.py:32
  51.0 18.1 %collective-permute-start.13 = (bf16[4,368,128]{2,1,0:T(8,128)(2,1)S(1)}, bf16[4,368,128]{2,1,0:T(8,128)(2,1)}, u32[]{:S(2)}, u32[]{:S(2)}) collective-permute-start(bf16[4,368,128]{2,1,0:T(8,128)(2,1)S(1)} %collective-permute-done.10.refs_1_), channel_id=1, source_target_pairs={{0,4},{1,5},{2,6},{3,7},{4,0},{5,1},{6,2},{7,3},{8,12},{9,13},{10,... | collective-permute-start | bytes 1130504 | tf_op jit(solution)/shard_map/ppermute | solution.py:32
  52.5 16.6 %collective-permute-start.14 = (bf16[4,368,128]{2,1,0:T(8,128)(2,1)S(1)}, bf16[4,368,128]{2,1,0:T(8,128)(2,1)}, u32[]{:S(2)}, u32[]{:S(2)}) collective-permute-start(bf16[4,368,128]{2,1,0:T(8,128)(2,1)S(1)} %get-tuple-element.144.refs_4_), channel_id=1, source_target_pairs={{0,2},{1,3},{2,0},{3,1},{4,6},{5,7},{6,4},{7,5},{8,10},{9,11},{10,... | collective-permute-start | bytes 1130504 | tf_op jit(solution)/shard_map/ppermute | solution.py:32
  53.1 16.1 %collective-permute-start.15 = (bf16[4,368,128]{2,1,0:T(8,128)(2,1)}, bf16[4,368,128]{2,1,0:T(8,128)(2,1)}, u32[]{:S(2)}, u32[]{:S(2)}) collective-permute-start(bf16[4,368,128]{2,1,0:T(8,128)(2,1)} %collective-permute-done.11.refs_5_), channel_id=1, source_target_pairs={{0,2},{1,3},{2,0},{3,1},{4,6},{5,7},{6,4},{7,5},{8,10},{9,11},{10,... | collective-permute-start | bytes 1130504 | tf_op jit(solution)/shard_map/ppermute | solution.py:32
  61.7 13.2 %copy-start.19 = (bf16[2,576]{1,0:T(2,128)(2,1)S(1)}, bf16[2,576]{1,0:T(2,128)(2,1)}, u32[]{:S(2)}) copy-start(bf16[2,576]{1,0:T(2,128)(2,1)} %gains_ref.3) | copy-start | bytes 6916
  69.1 4.2 %copy-start.15 = (bf16[4,368,128]{2,1,0:T(8,128)(2,1)}, bf16[4,368,128]{2,1,0:T(8,128)(2,1)S(1)}, u32[]{:S(2)}) copy-start(bf16[4,368,128]{2,1,0:T(8,128)(2,1)S(1)} %collective-permute-done.12.refs_2_) | copy-start | bytes 1130500
  69.1 2.0 collective-permute-start.16
  69.5 2.2 collective-permute-start.17
  70.0 3.3 %collective-permute-start.18 = (bf16[4,368,128]{2,1,0:T(8,128)(2,1)S(1)}, bf16[4,368,128]{2,1,0:T(8,128)(2,1)S(1)}, u32[]{:S(2)}, u32[]{:S(2)}) collective-permute-start(bf16[4,368,128]{2,1,0:T(8,128)(2,1)S(1)} %collective-permute-done.12.refs_2_), channel_id=1, source_target_pairs={{0,1},{1,0},{2,3},{3,2},{4,5},{5,4},{6,7},{7,6},{8,9},{9,8},{10,11... | collective-permute-start | bytes 1130504 | tf_op jit(solution)/shard_map/ppermute | solution.py:32
  70.0 12.1 %collective-permute-start.19 = (bf16[4,368,128]{2,1,0:T(8,128)(2,1)}, bf16[4,368,128]{2,1,0:T(8,128)(2,1)}, u32[]{:S(2)}, u32[]{:S(2)}) collective-permute-start(bf16[4,368,128]{2,1,0:T(8,128)(2,1)} %collective-permute-done.13.refs_3_), channel_id=1, source_target_pairs={{0,1},{1,0},{2,3},{3,2},{4,5},{5,4},{6,7},{7,6},{8,9},{9,8},{10,11... | collective-permute-start | bytes 1130504 | tf_op jit(solution)/shard_map/ppermute | solution.py:32
  70.5 11.7 %collective-permute-start.20 = (bf16[4,368,128]{2,1,0:T(8,128)(2,1)S(1)}, bf16[4,368,128]{2,1,0:T(8,128)(2,1)}, u32[]{:S(2)}, u32[]{:S(2)}) collective-permute-start(bf16[4,368,128]{2,1,0:T(8,128)(2,1)S(1)} %get-tuple-element.144.refs_4_), channel_id=1, source_target_pairs={{0,1},{1,0},{2,3},{3,2},{4,5},{5,4},{6,7},{7,6},{8,9},{9,8},{10,11... | collective-permute-start | bytes 1130504 | tf_op jit(solution)/shard_map/ppermute | solution.py:32
  71.2 2.2 copy-start.16
  71.2 11.0 %collective-permute-start.21 = (bf16[4,368,128]{2,1,0:T(8,128)(2,1)}, bf16[4,368,128]{2,1,0:T(8,128)(2,1)}, u32[]{:S(2)}, u32[]{:S(2)}) collective-permute-start(bf16[4,368,128]{2,1,0:T(8,128)(2,1)} %collective-permute-done.11.refs_5_), channel_id=1, source_target_pairs={{0,1},{1,0},{2,3},{3,2},{4,5},{5,4},{6,7},{7,6},{8,9},{9,8},{10,11... | collective-permute-start | bytes 1130504 | tf_op jit(solution)/shard_map/ppermute | solution.py:32
  71.7 1.6 copy-start.17
  71.7 10.5 %collective-permute-start.22 = (bf16[4,368,128]{2,1,0:T(8,128)(2,1)}, bf16[4,368,128]{2,1,0:T(8,128)(2,1)}, u32[]{:S(2)}, u32[]{:S(2)}) collective-permute-start(bf16[4,368,128]{2,1,0:T(8,128)(2,1)} %collective-permute-done.14.refs_6_), channel_id=1, source_target_pairs={{0,1},{1,0},{2,3},{3,2},{4,5},{5,4},{6,7},{7,6},{8,9},{9,8},{10,11... | collective-permute-start | bytes 1130504 | tf_op jit(solution)/shard_map/ppermute | solution.py:32
  74.1 8.1 %collective-permute-start.23 = (bf16[4,368,128]{2,1,0:T(8,128)(2,1)}, bf16[4,368,128]{2,1,0:T(8,128)(2,1)}, u32[]{:S(2)}, u32[]{:S(2)}) collective-permute-start(bf16[4,368,128]{2,1,0:T(8,128)(2,1)} %collective-permute-done.15.refs_7_), channel_id=1, source_target_pairs={{0,1},{1,0},{2,3},{3,2},{4,5},{5,4},{6,7},{7,6},{8,9},{9,8},{10,11... | collective-permute-start | bytes 1130504 | tf_op jit(solution)/shard_map/ppermute | solution.py:32
  82.1 7.1 %copy-start = (bf16[1024,576]{1,0:T(8,128)(2,1)S(1)}, bf16[1024,576]{1,0:T(8,128)(2,1)}, u32[]{:S(2)}) copy-start(bf16[1024,576]{1,0:T(8,128)(2,1)} %copy.37.tokens_in.tokens_ref) | copy-start | bytes 3538948
  82.1 7.1 %copy-start.11 = (bf16[1024,192]{1,0:T(8,128)(2,1)S(1)}, bf16[1024,192]{1,0:T(8,128)(2,1)}, u32[]{:S(2)}) copy-start(bf16[1024,192]{1,0:T(8,128)(2,1)} %get-tuple-element.137.mixed_ref) | copy-start | bytes 1179652
  82.1 7.1 %copy-start.12 = (bf16[1024,192]{1,0:T(8,128)(2,1)S(1)}, bf16[1024,192]{1,0:T(8,128)(2,1)}, u32[]{:S(2)}) copy-start(bf16[1024,192]{1,0:T(8,128)(2,1)} %get-tuple-element.139.mixed_ref) | copy-start | bytes 1179652
  89.3 2.9 %copy-start.20 = (bf16[1536,576]{1,0:T(8,128)(2,1)S(1)}, bf16[1536,576]{1,0:T(8,128)(2,1)}, u32[]{:S(2)}) copy-start(bf16[1536,576]{1,0:T(8,128)(2,1)} %get-tuple-element.149) | copy-start | bytes 5308420
  94.8 1.5 copy-start.21
  96.3 5.1 %copy-start.22 = (bf16[576,1536]{1,0:T(8,128)(2,1)S(1)}, bf16[576,1536]{1,0:T(8,128)(2,1)}, u32[]{:S(2)}) copy-start(bf16[576,1536]{1,0:T(8,128)(2,1)} %get-tuple-element.150) | copy-start | bytes 5308420
  119.7 4.9 %copy-start.1 = (f32[1024,576]{1,0:T(8,128)}, f32[1024,576]{1,0:T(8,128)S(1)}, u32[]{:S(2)}) copy-start(f32[1024,576]{1,0:T(8,128)S(1)} %subtract_add_fusion.mid_back_ref) | copy-start | bytes 7077892
  119.7 2.4 %copy-start.13 = (bf16[1024,192]{1,0:T(8,128)(2,1)S(1)}, bf16[1024,192]{1,0:T(8,128)(2,1)}, u32[]{:S(2)}) copy-start(bf16[1024,192]{1,0:T(8,128)(2,1)} %get-tuple-element.136.mixed_ref) | copy-start | bytes 1179652
  122.1 2.5 %copy-start.25 = (bf16[1024,1536]{0,1:T(8,128)(2,1)S(1)}, bf16[1024,1536]{0,1:T(8,128)(2,1)}, u32[]{:S(2)}) copy-start(bf16[1024,1536]{0,1:T(8,128)(2,1)} %get-tuple-element.240) | copy-start | bytes 9437188
  128.8 4.2 %copy-start.24 = (bf16[1024,1536]{0,1:T(8,128)(2,1)S(1)}, bf16[1024,1536]{0,1:T(8,128)(2,1)}, u32[]{:S(2)}) copy-start(bf16[1024,1536]{0,1:T(8,128)(2,1)} %get-tuple-element.238) | copy-start | bytes 9437188
  147.8 11.2 %copy-start.2 = (bf16[16,736,128]{2,1,0:T(8,128)(2,1)S(1)}, bf16[16,736,128]{2,1,0:T(8,128)(2,1)}, u32[]{:S(2)}) copy-start(bf16[16,736,128]{2,1,0:T(8,128)(2,1)} %get-tuple-element.154) | copy-start | bytes 9043972
  147.8 11.2 %collective-permute-start.24 = (bf16[16,736,128]{2,1,0:T(8,128)(2,1)}, bf16[16,736,128]{2,1,0:T(8,128)(2,1)}, u32[]{:S(2)}, u32[]{:S(2)}) collective-permute-start(bf16[16,736,128]{2,1,0:T(8,128)(2,1)} %get-tuple-element.155), channel_id=1, source_target_pairs={{0,1},{1,0},{2,3},{3,2},{4,5},{5,4},{6,7},{7,6},{8,9},{9,8},{10,11... | collective-permute-start | bytes 9043976 | tf_op jit(solution)/shard_map/ppermute | solution.py:32
  162.4 15.3 %collective-permute-start.27 = (bf16[4,368,128]{2,1,0:T(8,128)(2,1)}, bf16[4,368,128]{2,1,0:T(8,128)(2,1)S(1)}, u32[]{:S(2)}, u32[]{:S(2)}) collective-permute-start(bf16[4,368,128]{2,1,0:T(8,128)(2,1)} %get-tuple-element.166), channel_id=1, source_target_pairs={{0,4},{1,5},{2,6},{3,7},{4,0},{5,1},{6,2},{7,3},{8,12},{9,13},{10,... | collective-permute-start | bytes 1130504 | tf_op jit(solution)/shard_map/ppermute | solution.py:32
  162.9 14.9 %collective-permute-start.26 = (bf16[4,368,128]{2,1,0:T(8,128)(2,1)S(1)}, bf16[4,368,128]{2,1,0:T(8,128)(2,1)S(1)}, u32[]{:S(2)}, u32[]{:S(2)}) collective-permute-start(bf16[4,368,128]{2,1,0:T(8,128)(2,1)S(1)} %get-tuple-element.164), channel_id=1, source_target_pairs={{0,2},{1,3},{2,0},{3,1},{4,6},{5,7},{6,4},{7,5},{8,10},{9,11},{10,... | collective-permute-start | bytes 1130504 | tf_op jit(solution)/shard_map/ppermute | solution.py:32
  163.5 31.6 %collective-permute-start.25 = (bf16[4,368,128]{2,1,0:T(8,128)(2,1)S(1)}, bf16[4,368,128]{2,1,0:T(8,128)(2,1)S(1)}, u32[]{:S(2)}, u32[]{:S(2)}) collective-permute-start(bf16[4,368,128]{2,1,0:T(8,128)(2,1)S(1)} %get-tuple-element.162), channel_id=1, source_target_pairs={{0,2},{1,3},{2,0},{3,1},{4,6},{5,7},{6,4},{7,5},{8,10},{9,11},{10,... | collective-permute-start | bytes 1130504 | tf_op jit(solution)/shard_map/ppermute | solution.py:32
  165.0 30.3 %collective-permute-start.29 = (bf16[4,368,128]{2,1,0:T(8,128)(2,1)S(1)}, bf16[4,368,128]{2,1,0:T(8,128)(2,1)S(1)}, u32[]{:S(2)}, u32[]{:S(2)}) collective-permute-start(bf16[4,368,128]{2,1,0:T(8,128)(2,1)S(1)} %get-tuple-element.173), channel_id=1, source_target_pairs={{0,4},{1,5},{2,6},{3,7},{4,0},{5,1},{6,2},{7,3},{8,12},{9,13},{10,... | collective-permute-start | bytes 1130504 | tf_op jit(solution)/shard_map/ppermute | solution.py:32
  177.9 17.2 %collective-permute-start.28 = (bf16[4,368,128]{2,1,0:T(8,128)(2,1)S(1)}, bf16[4,368,128]{2,1,0:T(8,128)(2,1)S(1)}, u32[]{:S(2)}, u32[]{:S(2)}) collective-permute-start(bf16[4,368,128]{2,1,0:T(8,128)(2,1)S(1)} %add_convert_fusion.2), channel_id=1, source_target_pairs={{0,4},{1,5},{2,6},{3,7},{4,0},{5,1},{6,2},{7,3},{8,12},{9,13},{10,... | collective-permute-start | bytes 1130504 | tf_op jit(solution)/shard_map/ppermute | solution.py:32
  178.5 16.8 %collective-permute-start.30 = (bf16[4,368,128]{2,1,0:T(8,128)(2,1)S(1)}, bf16[4,368,128]{2,1,0:T(8,128)(2,1)S(1)}, u32[]{:S(2)}, u32[]{:S(2)}) collective-permute-start(bf16[4,368,128]{2,1,0:T(8,128)(2,1)S(1)} %add_convert_fusion.1), channel_id=1, source_target_pairs={{0,2},{1,3},{2,0},{3,1},{4,6},{5,7},{6,4},{7,5},{8,10},{9,11},{10,... | collective-permute-start | bytes 1130504 | tf_op jit(solution)/shard_map/ppermute | solution.py:32
  195.5 23.3 %collective-permute-start.31 = (bf16[736,128]{1,0:T(8,128)(2,1)S(1)}, bf16[736,128]{1,0:T(8,128)(2,1)S(1)}, u32[]{:S(2)}, u32[]{:S(2)}) collective-permute-start(bf16[736,128]{1,0:T(8,128)(2,1)S(1)} %pad_maximum_fusion.9), channel_id=1, source_target_pairs={{0,8},{1,9},{2,10},{3,11},{4,12},{5,13},{6,14},{7,15},{8,0},{9,1},... | collective-permute-start | bytes 565256 | tf_op jit(solution)/shard_map/ppermute | solution.py:32
  198.1 20.7 %collective-permute-start.32 = (bf16[736,128]{1,0:T(8,128)(2,1)S(1)}, bf16[736,128]{1,0:T(8,128)(2,1)S(1)}, u32[]{:S(2)}, u32[]{:S(2)}) collective-permute-start(bf16[736,128]{1,0:T(8,128)(2,1)S(1)} %pad_maximum_fusion.10), channel_id=1, source_target_pairs={{0,16},{1,17},{2,18},{3,19},{4,20},{5,21},{6,22},{7,23},{8,24},{9,... | collective-permute-start | bytes 565256 | tf_op jit(solution)/shard_map/ppermute | solution.py:32
  198.2 20.6 %collective-permute-start.33 = (bf16[736,128]{1,0:T(8,128)(2,1)S(1)}, bf16[736,128]{1,0:T(8,128)(2,1)S(1)}, u32[]{:S(2)}, u32[]{:S(2)}) collective-permute-start(bf16[736,128]{1,0:T(8,128)(2,1)S(1)} %pad_maximum_fusion.11), channel_id=1, source_target_pairs={{0,24},{1,25},{2,26},{3,27},{4,28},{5,29},{6,30},{7,31},{8,16},{9,... | collective-permute-start | bytes 565256 | tf_op jit(solution)/shard_map/ppermute | solution.py:32
  218.8 2.3 copy-start.9
  218.8 2.3 collective-permute-start.34
  220.3 16.4 %copy-start.5 = (bf16[1024,576]{1,0:T(8,128)(2,1)S(1)}, bf16[1024,576]{1,0:T(8,128)(2,1)}, u32[]{:S(2)}) copy-start(bf16[1024,576]{1,0:T(8,128)(2,1)} %get-tuple-element.227) | copy-start | bytes 3538948
  221.3 6.7 %collective-permute-start.35 = (bf16[4,144,128]{2,1,0:T(8,128)(2,1)S(1)}, bf16[4,144,128]{2,1,0:T(8,128)(2,1)S(1)}, u32[]{:S(2)}, u32[]{:S(2)}) collective-permute-start(bf16[4,144,128]{2,1,0:T(8,128)(2,1)S(1)} %get-tuple-element.203), channel_id=1, source_target_pairs={{0,2},{1,3},{2,0},{3,1},{4,6},{5,7},{6,4},{7,5},{8,10},{9,11},{10,... | collective-permute-start | bytes 442376 | tf_op jit(solution)/shard_map/ppermute | solution.py:32
  222.8 8.8 %collective-permute-start.36 = (bf16[4,144,128]{2,1,0:T(8,128)(2,1)S(1)}, bf16[4,144,128]{2,1,0:T(8,128)(2,1)S(1)}, u32[]{:S(2)}, u32[]{:S(2)}) collective-permute-start(bf16[4,144,128]{2,1,0:T(8,128)(2,1)S(1)} %get-tuple-element.204), channel_id=1, source_target_pairs={{0,4},{1,5},{2,6},{3,7},{4,0},{5,1},{6,2},{7,3},{8,12},{9,13},{10,... | collective-permute-start | bytes 442376 | tf_op jit(solution)/shard_map/ppermute | solution.py:32
  224.4 7.2 %collective-permute-start.37 = (bf16[4,144,128]{2,1,0:T(8,128)(2,1)S(1)}, bf16[4,144,128]{2,1,0:T(8,128)(2,1)S(1)}, u32[]{:S(2)}, u32[]{:S(2)}) collective-permute-start(bf16[4,144,128]{2,1,0:T(8,128)(2,1)S(1)} %get-tuple-element.205), channel_id=1, source_target_pairs={{0,6},{1,7},{2,4},{3,5},{4,2},{5,3},{6,0},{7,1},{8,14},{9,15},{10,... | collective-permute-start | bytes 442376 | tf_op jit(solution)/shard_map/ppermute | solution.py:32
  231.7 6.5 %collective-permute-start.38 = (bf16[144,128]{1,0:T(8,128)(2,1)S(1)}, bf16[144,128]{1,0:T(8,128)(2,1)S(1)}, u32[]{:S(2)}, u32[]{:S(2)}) collective-permute-start(bf16[144,128]{1,0:T(8,128)(2,1)S(1)} %get-tuple-element.209), channel_id=1, source_target_pairs={{0,8},{1,9},{2,10},{3,11},{4,12},{5,13},{6,14},{7,15},{8,0},{9,1},... | collective-permute-start | bytes 110600 | tf_op jit(solution)/shard_map/ppermute | solution.py:32
  232.8 5.4 %collective-permute-start.39 = (bf16[144,128]{1,0:T(8,128)(2,1)S(1)}, bf16[144,128]{1,0:T(8,128)(2,1)S(1)}, u32[]{:S(2)}, u32[]{:S(2)}) collective-permute-start(bf16[144,128]{1,0:T(8,128)(2,1)S(1)} %get-tuple-element.210), channel_id=1, source_target_pairs={{0,16},{1,17},{2,18},{3,19},{4,20},{5,21},{6,22},{7,23},{8,24},{9,... | collective-permute-start | bytes 110600 | tf_op jit(solution)/shard_map/ppermute | solution.py:32
  233.8 5.8 %collective-permute-start.40 = (bf16[144,128]{1,0:T(8,128)(2,1)S(1)}, bf16[144,128]{1,0:T(8,128)(2,1)S(1)}, u32[]{:S(2)}, u32[]{:S(2)}) collective-permute-start(bf16[144,128]{1,0:T(8,128)(2,1)S(1)} %get-tuple-element.211), channel_id=1, source_target_pairs={{0,24},{1,25},{2,26},{3,27},{4,28},{5,29},{6,30},{7,31},{8,16},{9,... | collective-permute-start | bytes 110600 | tf_op jit(solution)/shard_map/ppermute | solution.py:32
  (3 other events, 2.7 us)

commit v3 on v2

--- a/solution.py
+++ b/solution.py
@@ -838,7 +838,7 @@
     tokens = first.plane_stage(tokens)
     tokens = first.core_stage(tokens, True)
     if first.stages:
-        first.got = second.first_half_stage(first.got)
+        tokens = second.first_half_stage(tokens)
     (wide_mat,) = first.result(True)
     resid_in = tokens.astype(jnp.float32)
     cosine, sine = rotary_tables(LENGTH, HEAD_DIM)

time: 245 us -> 244 us (level)
    unnamed x58 -> x56, local copies, waits for them, and re-layouts: 6.44 us -> 5.63 us
where the time goes in v3:
time: 244 us; the launch traced here: 241 us
  Pallas kernels  99.6 us (41%)
  matrix products  50.8 us (21%)
  starting transfers between devices  39.6 us (16%)
  waiting for transfers between devices  27.6 us (11%)
  local copies, waits for them, and re-layouts  12.5 us (5%)
  other arithmetic  9.39 us (4%)
    ppermute x41, starting transfers between devices, swap(): lax.ppermute(field, 'dp', [(place, place ^ mask) for place in range(devic...  39.6 us
    pallas_call x3, Pallas kernels, attend_back(): pl.pallas_call(functools.partial(attend_back_kernel, head=head, group=gro...  32.9 us
    ppermute x41, waiting for transfers between devices, swap(): lax.ppermute(field, 'dp', [(place, place ^ mask) for place in range(devic...  27.6 us
    pallas_call x3, Pallas kernels, attend(): pl.pallas_call(functools.partial(attend_kernel, head=head, group=group),...  21.8 us
    dot_general x4, matrix products, outer_prod(): lax.dot_general(left, right, (((0,), (0,)), ((), ())), preferred_element_...  15.5 us
    pallas_call x2, Pallas kernels, pack_grads(): pl.pallas_call(functools.partial(pack_kernel, devices=devices, shapes=sha...  14.2 us
    pallas_call x1, Pallas kernels, vmem_call(): pl.pallas_call(kernel, out_shape=out_shape, in_specs=[pl.BlockSpec(memory...  13.1 us
    dot_general x4, matrix products, times_transposed(): lax.dot_general(left, matrix, (((1,), (1,)), ((), ())), preferred_element...  13.1 us
  transfers between devices with their start and end apart: 41, of which 13 were waited for; matrix products, arithmetic and copies ran while one was open for 7% of the time, Pallas kernels for 34%

profile of v3, /device:TPU:0, one launch (start us, length us, event | category | flops | bytes accessed | tf_op | source)
XLA Modules:
  0.0 241.0 jit_solution(5128288564789674290)
XLA Ops:
  0.6 0.8 fusion.34
  1.4 3.1 %collective-permute-start = (bf16[144,128]{1,0:T(8,128)(2,1)S(1)}, bf16[144,128]{1,0:T(8,128)(2,1)S(1)}, u32[]{:S(2)}, u32[]{:S(2)}) collective-permute-start(bf16[144,128]{1,0:T(8,128)(2,1)S(1)} %fusion.34), channel_id=1, source_target_pairs={{0,8},{1,9},{2,10},{3,11},{4,12},{5,13},{6,14},{7,15},{8,0},{9,1},... | collective-permute-start | bytes 110600 | tf_op jit(solution)/shard_map/ppermute | solution.py:32
  4.5 2.6 %collective-permute-start.4 = (bf16[144,128]{1,0:T(8,128)(2,1)S(1)}, bf16[144,128]{1,0:T(8,128)(2,1)S(1)}, u32[]{:S(2)}, u32[]{:S(2)}) collective-permute-start(bf16[144,128]{1,0:T(8,128)(2,1)S(1)} %fusion.34), channel_id=1, source_target_pairs={{0,16},{1,17},{2,18},{3,19},{4,20},{5,21},{6,22},{7,23},{8,24},{9,... | collective-permute-start | bytes 110600 | tf_op jit(solution)/shard_map/ppermute | solution.py:32
  7.1 0.9 fusion.14
  8.0 2.0 collective-permute-done.4
  10.0 2.8 %collective-permute-done.5 = bf16[144,128]{1,0:T(8,128)(2,1)S(1)} collective-permute-done((bf16[144,128]{1,0:T(8,128)(2,1)S(1)}, bf16[144,128]{1,0:T(8,128)(2,1)S(1)}, u32[]{:S(2)}, u32[]{:S(2)}) %collective-permute-start.5) | collective-permute-done | bytes 36896 | tf_op jit(solution)/shard_map/ppermute | solution.py:32
  12.9 1.6 collective-permute-start.6
  14.4 1.5 collective-permute-start.7
  16.4 1.1 collective-permute-start.2
  17.5 1.8 collective-permute-done.6
  19.3 1.6 collective-permute-start.3
  20.9 1.2 collective-permute-done.7
  22.3 1.6 collective-permute-done.1
  24.0 7.5 %collective-permute-done.2 = bf16[736,128]{1,0:T(8,128)(2,1)S(1)} collective-permute-done((bf16[736,128]{1,0:T(8,128)(2,1)S(1)}, bf16[736,128]{1,0:T(8,128)(2,1)S(1)}, u32[]{:S(2)}, u32[]{:S(2)}) %collective-permute-start.2) | collective-permute-done | bytes 188448 | tf_op jit(solution)/shard_map/ppermute | solution.py:32
  31.7 1.6 collective-permute-start.10
  33.3 1.5 collective-permute-start.9
  35.4 1.0 copy.40.sine_in.sine_ref
  36.5 1.0 copy.39.cosine_in.cosine_ref
  37.5 1.4 copy.37.tokens_in.tokens_ref
  39.0 3.5 %unpack.2.wide_ref = bf16[576,1152]{1,0:T(8,128)(2,1)} custom-call(s32[1]{0:T(128)} %bitcast.place_ref, bf16[16,144,128]{2,1,0:T(8,128)(2,1)} %copy-done.8, bf16[16,144,128]{2,1,0:T(8,128)(2,1)} %collective-permute-done.11.refs_1_), custom_call_target="tpu_custom_call" | custom-call | flops 100000000 | bytes 1000000 | tf_op jit(solution)/shard_map/unpack/pallas_call | solution.py:145
  42.5 7.2 %project.1.fields_ref = bf16[1024,1152]{1,0:T(8,128)(2,1)} custom-call(bf16[1024,576]{1,0:T(8,128)(2,1)} %copy.37.tokens_in.tokens_ref, f32[1024,128]{1,0:T(8,128)} %copy.39.cosine_in.cosine_ref, f32[1024,128]{1,0:T(8,128)} %copy.40.sine_in.sine_ref, bf16[2,576]{1,0:T(2,128)(2,1)} %gains_ref.3, bf16[576,1152]{1,0:T(8,128)(2,1)} %unpack.2.wide_ref), custom_call_target="tpu_custom_call" | custom-call | flops 100000000 | bytes 1000000 | tf_op jit(solution)/shard_map/project/pallas_call | solution.py:489
  50.2 1.5 collective-permute-start.13
  52.3 1.5 collective-permute-start.15
  53.8 7.2 %attend.3 = (bf16[1024,192]{1,0:T(8,128)(2,1)}, f32[1024,128]{1,0:T(8,128)}) custom-call(bf16[1024,1152]{1,0:T(8,128)(2,1)} %project.1.fields_ref), custom_call_target="tpu_custom_call" | custom-call | flops 100000000 | bytes 1000000 | tf_op jit(solution)/shard_map/attend/pallas_call | solution.py:324
  61.0 7.4 %attend.4 = (bf16[1024,192]{1,0:T(8,128)(2,1)}, f32[1024,128]{1,0:T(8,128)}) custom-call(bf16[1024,1152]{1,0:T(8,128)(2,1)} %project.1.fields_ref), custom_call_target="tpu_custom_call" | custom-call | flops 100000000 | bytes 1000000 | tf_op jit(solution)/shard_map/attend/pallas_call | solution.py:324
  71.1 1.5 collective-permute-done.18.refs_10_
  74.2 7.2 %attend.5 = (bf16[1024,192]{1,0:T(8,128)(2,1)}, f32[1024,128]{1,0:T(8,128)}) custom-call(bf16[1024,1152]{1,0:T(8,128)(2,1)} %project.1.fields_ref), custom_call_target="tpu_custom_call" | custom-call | flops 100000000 | bytes 1000000 | tf_op jit(solution)/shard_map/attend/pallas_call | solution.py:324
  81.5 7.0 %unpack.3 = (bf16[576,1536]{1,0:T(8,128)(2,1)}, bf16[576,1536]{1,0:T(8,128)(2,1)}, bf16[1536,576]{1,0:T(8,128)(2,1)}, bf16[576,576]{1,0:T(8,128)(2,1)}) custom-call(s32[1]{0:T(128)} %bitcast.place_ref, bf16[4,368,128]{2,1,0:T(8,128)(2,1)} %copy-done.3, bf16[4,368,128]{2,1,0:T(8,128)(2,1)} %copy-done.13, bf16[4,368,128]{2,1,0:T(8,128)(2,1)} %copy-done.14, ...), custom_call_target="tpu_custom_call" | custom-call | flops 100000000 | bytes 1000000 | tf_op jit(solution)/shard_map/unpack/pallas_call | solution.py:145
  88.6 2.8 %multiply_reduce_fusion.2 = (f32[1024]{0:T(1024)S(1)}, f32[1024,576]{1,0:T(8,128)S(1)}) fusion(bf16[576,576]{1,0:T(8,128)(2,1)} %get-tuple-element.148, bf16[1024,192]{1,0:T(8,128)(2,1)S(1)} %copy-done.11, bf16[1024,192]{1,0:T(8,128)(2,1)S(1)} %copy-done.10, bf16[1024,192]{1,0:T(8,128)(2,1)} %get-tuple-element.136.mixed_ref, bf16[1024,576]{1,0:T(8,128)(2,1)S(1)} %copy-done), kind=kOutput, calls=%fused_computation.14 | convolution fusion | flops 685374464 | bytes 5386240 | tf_op jit(solution)/shard_map/dot_general | solution.py:855
  91.5 2.7 %fusion.37 = f32[1536,1024]{1,0:T(8,128)S(1)} fusion(bf16[1536,576]{1,0:T(8,128)(2,1)S(1)} %copy-done.19, bf16[1024,576]{0,1:T(8,128)(2,1)S(1)} %copy-done.7), kind=kOutput, calls=%fused_computation.115 | convolution fusion | flops 1811939328 | bytes 9240576 | tf_op jit(solution)/shard_map/dot_general | solution.py:613
  94.5 1.2 copy-done.20
  95.6 5.1 %fusion.38 = f32[1024,1536]{0,1:T(8,128)} fusion(bf16[1024,576]{1,0:T(8,128)(2,1)S(1)} %multiply_convert_fusion.1, bf16[576,1536]{1,0:T(8,128)(2,1)S(1)} %copy-done.20), kind=kOutput, calls=%fused_computation.116 | convolution fusion | flops 1811939328 | bytes 9240576 | tf_op jit(solution)/shard_map/dot_general | solution.py:859
  100.7 9.2 %multiply_convert_fusion = (bf16[1024,1536]{0,1:T(8,128)(2,1)}, bf16[1024,1536]{0,1:T(8,128)(2,1)S(1)}, bf16[1024,1536]{0,1:T(8,128)(2,1)}) fusion(f32[1024,1536]{0,1:T(8,128)} %fusion.38, f32[1536,1024]{1,0:T(8,128)S(1)} %fusion.37, bf16[1024,576]{1,0:T(8,128)(2,1)S(1)} %multiply_convert_fusion.1, bf16[576,1536]{1,0:T(8,128)(2,1)S(1)} %copy-done.21), kind=kOutput, calls=%fused_computation.6 | convolution fusion | flops 1835532288 | bytes 24969216 | tf_op jit(solution)/shard_map/dot_general | solution.py:860
  109.9 4.6 %fusion.42 = f32[1024,576]{1,0:T(8,128)S(1)} fusion(bf16[1024,1536]{0,1:T(8,128)(2,1)} %get-tuple-element.240, bf16[576,1536]{1,0:T(8,128)(2,1)S(1)} %copy-done.21), kind=kOutput, calls=%fused_computation.120 | convolution fusion | flops 1811939328 | bytes 7274496 | tf_op jit(solution)/shard_map/dot_general | solution.py:613
  114.5 3.4 %multiply_reduce_fusion = (f32[576]{0:T(1024)S(1)}, f32[1024]{0:T(1024)S(1)}, f32[1024,576]{1,0:T(8,128)S(1)}) fusion(f32[1024,576]{1,0:T(8,128)S(1)} %get-tuple-element.284, f32[1024]{0:T(1024)S(1)} %get-tuple-element.279, f32[576]{0:T(1024)S(1)} %convert_reduce_fusion, f32[1024,576]{1,0:T(8,128)S(1)} %fusion.42, ...), kind=kOutput, calls=%fused_computation.9 | convolution fusion | flops 1816066560 | bytes 12005888 | tf_op jit(solution)/shard_map/dot_general | solution.py:613
  117.9 1.1 subtract_add_fusion.mid_back_ref
  119.0 2.4 %convolution_convert_fusion.back_ref = bf16[1024,576]{1,0:T(8,128)(2,1)} fusion(bf16[576,576]{1,0:T(8,128)(2,1)S(1)} %copy-done.22, f32[1024,576]{1,0:T(8,128)S(1)} %subtract_add_fusion.mid_back_ref), kind=kOutput, calls=%fused_computation.17 | convolution fusion | flops 680656896 | bytes 4202496 | tf_op jit(solution)/shard_map/dot_general | solution.py:613
  121.4 2.5 %fusion.6.refs_3_ = f32[576,576]{1,0:T(8,128)} fusion(f32[1024,576]{1,0:T(8,128)S(1)} %subtract_add_fusion.mid_back_ref, bf16[1024,192]{1,0:T(8,128)(2,1)S(1)} %copy-done.11, bf16[1024,192]{1,0:T(8,128)(2,1)S(1)} %copy-done.10, bf16[1024,192]{1,0:T(8,128)(2,1)S(1)} %copy-done.12), kind=kOutput, calls=%fused_computation.30 | convolution fusion | flops 683606016 | bytes 4866048 | tf_op jit(solution)/shard_map/dot_general | solution.py:607
  123.9 4.1 %fusion.40.refs_1_ = f32[576,1536]{1,0:T(8,128)} fusion(bf16[1024,576]{1,0:T(8,128)(2,1)S(1)} %multiply_convert_fusion.1, bf16[1024,1536]{0,1:T(8,128)(2,1)S(1)} %copy-done.24), kind=kOutput, calls=%fused_computation.118 | convolution fusion | flops 1811939328 | bytes 7864320 | tf_op jit(solution)/shard_map/dot_general | solution.py:607
  128.1 4.2 %fusion.39.refs_0_ = f32[576,1536]{1,0:T(8,128)} fusion(bf16[1024,576]{1,0:T(8,128)(2,1)S(1)} %multiply_convert_fusion.1, bf16[1024,1536]{0,1:T(8,128)(2,1)S(1)} %get-tuple-element.239), kind=kOutput, calls=%fused_computation.117 | convolution fusion | flops 1811939328 | bytes 7864320 | tf_op jit(solution)/shard_map/dot_general | solution.py:607
  132.3 4.6 %fusion.41.refs_2_ = f32[1536,576]{1,0:T(8,128)} fusion(bf16[1024,1536]{0,1:T(8,128)(2,1)S(1)} %copy-done.23, bf16[1024,576]{0,1:T(8,128)(2,1)S(1)} %copy-done.7), kind=kOutput, calls=%fused_computation.119 | convolution fusion | flops 1811939328 | bytes 7864320 | tf_op jit(solution)/shard_map/dot_general | solution.py:607
  136.9 10.2 %pack.2 = (bf16[16,736,128]{2,1,0:T(8,128)(2,1)}, bf16[16,736,128]{2,1,0:T(8,128)(2,1)}) custom-call(s32[1]{0:T(128)} %bitcast.place_ref, f32[576,1536]{1,0:T(8,128)} %fusion.39.refs_0_, f32[576,1536]{1,0:T(8,128)} %fusion.40.refs_1_, f32[1536,576]{1,0:T(8,128)} %fusion.41.refs_2_, f32[576,576]{1,0:T(8,128)} %fusion.6.refs_3_), custom_call_target="tpu_custom_call" | custom-call | flops 100000000 | bytes 1000000 | tf_op jit(solution)/shard_map/pack/pallas_call | solution.py:244
  147.5 10.8 %attend_back.3 = (f32[1024,192]{1,0:T(8,128)}, f32[1024,128]{1,0:T(8,128)}) custom-call(bf16[1024,1152]{1,0:T(8,128)(2,1)} %project.1.fields_ref, bf16[1024,576]{1,0:T(8,128)(2,1)} %convolution_convert_fusion.back_ref, bf16[1024,192]{1,0:T(8,128)(2,1)} %get-tuple-element.136.mixed_ref, f32[1024,128]{1,0:T(8,128)} %get-tuple-element.157.total_ref), custom_call_target="tpu_custom_call" | custom-call | flops 100000000 | bytes 1000000 | tf_op jit(solution)/shard_map/attend_back/pallas_call | solution.py:400
  158.3 3.4 %add_convert_fusion.3 = (bf16[4,368,128]{2,1,0:T(8,128)(2,1)}, bf16[4,368,128]{2,1,0:T(8,128)(2,1)S(1)}, bf16[4,368,128]{2,1,0:T(8,128)(2,1)S(1)}, bf16[4,368,12...) fusion(bf16[16,736,128]{2,1,0:T(8,128)(2,1)} %collective-permut, ...), kind=kLoop, calls=%fused_computation.21 | loop fusion | flops 6029312 | bytes 9043968 | tf_op jit(solution)/shard_map/convert_element_type | solution.py:750
  162.7 1.5 collective-permute-start.25
  164.2 1.5 collective-permute-start.29
  165.8 11.2 %attend_back.4 = (f32[1024,192]{1,0:T(8,128)}, f32[1024,128]{1,0:T(8,128)}) custom-call(bf16[1024,1152]{1,0:T(8,128)(2,1)} %project.1.fields_ref, bf16[1024,576]{1,0:T(8,128)(2,1)} %convolution_convert_fusion.back_ref, bf16[1024,192]{1,0:T(8,128)(2,1)} %get-tuple-element.137.mixed_ref, f32[1024,128]{1,0:T(8,128)} %get-tuple-element.168.total_ref), custom_call_target="tpu_custom_call" | custom-call | flops 100000000 | bytes 1000000 | tf_op jit(solution)/shard_map/attend_back/pallas_call | solution.py:400
  178.3 5.1 %add_convert_fusion = bf16[1024,576]{1,0:T(8,128)(2,1)S(1)} fusion(f32[1024,576]{1,0:T(8,128)S(1)} %get-tuple-element.284, bf16[1024,1536]{0,1:T(8,128)(2,1)} %get-tuple-element.238, bf16[1536,576]{1,0:T(8,128)(2,1)} %get-tuple-element.149), kind=kOutput, calls=%fused_computation.10 | convolution fusion | flops 1813118976 | bytes 8454144 | tf_op jit(solution)/shard_map/dot_general | solution.py:864
  183.4 10.9 %attend_back.5 = (f32[1024,192]{1,0:T(8,128)}, f32[1024,128]{1,0:T(8,128)}) custom-call(bf16[1024,1152]{1,0:T(8,128)(2,1)} %project.1.fields_ref, bf16[1024,576]{1,0:T(8,128)(2,1)} %convolution_convert_fusion.back_ref, bf16[1024,192]{1,0:T(8,128)(2,1)} %get-tuple-element.139.mixed_ref, f32[1024,128]{1,0:T(8,128)} %get-tuple-element.180.total_ref), custom_call_target="tpu_custom_call" | custom-call | flops 100000000 | bytes 1000000 | tf_op jit(solution)/shard_map/attend_back/pallas_call | solution.py:400
  194.8 2.6 %collective-permute-start.31 = (bf16[736,128]{1,0:T(8,128)(2,1)S(1)}, bf16[736,128]{1,0:T(8,128)(2,1)S(1)}, u32[]{:S(2)}, u32[]{:S(2)}) collective-permute-start(bf16[736,128]{1,0:T(8,128)(2,1)S(1)} %pad_maximum_fusion.7), channel_id=1, source_target_pairs={{0,8},{1,9},{2,10},{3,11},{4,12},{5,13},{6,14},{7,15},{8,0},{9,1},... | collective-permute-start | bytes 565256 | tf_op jit(solution)/shard_map/ppermute | solution.py:32
  197.5 2.4 collective-permute-start.33
  199.8 13.1 %finish.1 = (bf16[1024,576]{1,0:T(8,128)(2,1)}, f32[1,576]{1,0:T(1,128)}, f32[5,576,128]{2,1,0:T(8,128)}, f32[2,576,128]{2,1,0:T(8,128)}, f32[2,576,128]{2,1,0:T(8,128)}) custom-call(bf16[1024,576]{1,0:T(8,128)(2,1)} %copy.37.tokens_in.tokens_ref, bf16[2,576]{1,0:T(2,128)(2,1)} %gains_ref.3, bf16[576,1152]{1,0:T(8,128)(2,1)} %unpack.2.wide_ref, ...), custom_call_target="tpu_custom_call" | custom-call | flops 100000000 | bytes 1000000 | tf_op jit(solution)/shard_map/finish/pallas_call | solution.py:474
  212.9 1.3 pad_maximum_fusion.11.refs_3_
  214.2 3.9 %pack.3 = (bf16[16,144,128]{2,1,0:T(8,128)(2,1)}, bf16[16,144,128]{2,1,0:T(8,128)(2,1)}) custom-call(s32[1]{0:T(128)} %bitcast.place_ref, f32[5,576,128]{2,1,0:T(8,128)} %get-tuple-element.190.refs_0_, f32[2,576,128]{2,1,0:T(8,128)} %get-tuple-element.191.refs_1_, f32[2,576,128]{2,1,0:T(8,128)} %get-tuple-element.192.refs_2_, ...), custom_call_target="tpu_custom_call" | custom-call | flops 100000000 | bytes 1000000 | tf_op jit(solution)/shard_map/pack/pallas_call | solution.py:244
  218.2 1.4 copy.56
  220.6 1.5 collective-permute-start.35
  222.1 1.5 collective-permute-start.36
  224.9 2.4 collective-permute-done.35
  227.3 3.6 %collective-permute-done.36 = bf16[4,144,128]{2,1,0:T(8,128)(2,1)S(1)} collective-permute-done((bf16[4,144,128]{2,1,0:T(8,128)(2,1)S(1)}, bf16[4,144,128]{2,1,0:T(8,128)(2,1)S(1)}, u32[]{:S(2)}, u32[]{:S(2)}) %collective-permute-start.36) | collective-permute-done | bytes 147488 | tf_op jit(solution)/shard_map/ppermute | solution.py:32
  231.0 1.1 collective-permute-start.38
  232.1 1.0 collective-permute-start.39
  233.1 2.3 collective-permute-start.40
  236.1 1.4 copy.57
  237.5 1.4 collective-permute-done.40
  (141 shorter events, 15.4 us)
Async XLA Ops:
  1.4 6.6 %collective-permute-start = (bf16[144,128]{1,0:T(8,128)(2,1)S(1)}, bf16[144,128]{1,0:T(8,128)(2,1)S(1)}, u32[]{:S(2)}, u32[]{:S(2)}) collective-permute-start(bf16[144,128]{1,0:T(8,128)(2,1)S(1)} %fusion.34), channel_id=1, source_target_pairs={{0,8},{1,9},{2,10},{3,11},{4,12},{5,13},{6,14},{7,15},{8,0},{9,1},... | collective-permute-start | bytes 110600 | tf_op jit(solution)/shard_map/ppermute | solution.py:32
  4.5 5.5 %collective-permute-start.4 = (bf16[144,128]{1,0:T(8,128)(2,1)S(1)}, bf16[144,128]{1,0:T(8,128)(2,1)S(1)}, u32[]{:S(2)}, u32[]{:S(2)}) collective-permute-start(bf16[144,128]{1,0:T(8,128)(2,1)S(1)} %fusion.34), channel_id=1, source_target_pairs={{0,16},{1,17},{2,18},{3,19},{4,20},{5,21},{6,22},{7,23},{8,24},{9,... | collective-permute-start | bytes 110600 | tf_op jit(solution)/shard_map/ppermute | solution.py:32
  7.1 5.8 %collective-permute-start.5 = (bf16[144,128]{1,0:T(8,128)(2,1)S(1)}, bf16[144,128]{1,0:T(8,128)(2,1)S(1)}, u32[]{:S(2)}, u32[]{:S(2)}) collective-permute-start(bf16[144,128]{1,0:T(8,128)(2,1)S(1)} %fusion.34), channel_id=1, source_target_pairs={{0,24},{1,25},{2,26},{3,27},{4,28},{5,29},{6,30},{7,31},{8,16},{9,... | collective-permute-start | bytes 110600 | tf_op jit(solution)/shard_map/ppermute | solution.py:32
  12.9 6.4 %collective-permute-start.6 = (bf16[4,144,128]{2,1,0:T(8,128)(2,1)S(1)}, bf16[4,144,128]{2,1,0:T(8,128)(2,1)S(1)}, u32[]{:S(2)}, u32[]{:S(2)}) collective-permute-start(bf16[4,144,128]{2,1,0:T(8,128)(2,1)S(1)} %pad_maximum_fusion.10), channel_id=1, source_target_pairs={{0,2},{1,3},{2,0},{3,1},{4,6},{5,7},{6,4},{7,5},{8,10},{9,11},{10,... | collective-permute-start | bytes 442376 | tf_op jit(solution)/shard_map/ppermute | solution.py:32
  14.4 7.7 %collective-permute-start.7 = (bf16[4,144,128]{2,1,0:T(8,128)(2,1)S(1)}, bf16[4,144,128]{2,1,0:T(8,128)(2,1)S(1)}, u32[]{:S(2)}, u32[]{:S(2)}) collective-permute-start(bf16[4,144,128]{2,1,0:T(8,128)(2,1)S(1)} %pad_maximum_fusion.10), channel_id=1, source_target_pairs={{0,4},{1,5},{2,6},{3,7},{4,0},{5,1},{6,2},{7,3},{8,12},{9,13},{10,... | collective-permute-start | bytes 442376 | tf_op jit(solution)/shard_map/ppermute | solution.py:32
  16.0 6.2 %collective-permute-start.8 = (bf16[4,144,128]{2,1,0:T(8,128)(2,1)S(1)}, bf16[4,144,128]{2,1,0:T(8,128)(2,1)S(1)}, u32[]{:S(2)}, u32[]{:S(2)}) collective-permute-start(bf16[4,144,128]{2,1,0:T(8,128)(2,1)S(1)} %pad_maximum_fusion.10), channel_id=1, source_target_pairs={{0,6},{1,7},{2,4},{3,5},{4,2},{5,3},{6,0},{7,1},{8,14},{9,15},{10,... | collective-permute-start | bytes 442376 | tf_op jit(solution)/shard_map/ppermute | solution.py:32
  16.4 7.5 %collective-permute-start.1 = (bf16[736,128]{1,0:T(8,128)(2,1)S(1)}, bf16[736,128]{1,0:T(8,128)(2,1)S(1)}, u32[]{:S(2)}, u32[]{:S(2)}) collective-permute-start(bf16[736,128]{1,0:T(8,128)(2,1)S(1)} %fusion.14), channel_id=1, source_target_pairs={{0,8},{1,9},{2,10},{3,11},{4,12},{5,13},{6,14},{7,15},{8,0},{9,1},... | collective-permute-start | bytes 565256 | tf_op jit(solution)/shard_map/ppermute | solution.py:32
  16.4 15.1 %collective-permute-start.2 = (bf16[736,128]{1,0:T(8,128)(2,1)S(1)}, bf16[736,128]{1,0:T(8,128)(2,1)S(1)}, u32[]{:S(2)}, u32[]{:S(2)}) collective-permute-start(bf16[736,128]{1,0:T(8,128)(2,1)S(1)} %fusion.14), channel_id=1, source_target_pairs={{0,16},{1,17},{2,18},{3,19},{4,20},{5,21},{6,22},{7,23},{8,24},{9,... | collective-permute-start | bytes 565256 | tf_op jit(solution)/shard_map/ppermute | solution.py:32
  19.3 12.2 %collective-permute-start.3 = (bf16[736,128]{1,0:T(8,128)(2,1)S(1)}, bf16[736,128]{1,0:T(8,128)(2,1)S(1)}, u32[]{:S(2)}, u32[]{:S(2)}) collective-permute-start(bf16[736,128]{1,0:T(8,128)(2,1)S(1)} %fusion.14), channel_id=1, source_target_pairs={{0,24},{1,25},{2,26},{3,27},{4,28},{5,29},{6,30},{7,31},{8,16},{9,... | collective-permute-start | bytes 565256 | tf_op jit(solution)/shard_map/ppermute | solution.py:32
  22.2 14.2 %copy-start.8 = (bf16[16,144,128]{2,1,0:T(8,128)(2,1)}, bf16[16,144,128]{2,1,0:T(8,128)(2,1)S(1)}, u32[]{:S(2)}) copy-start(bf16[16,144,128]{2,1,0:T(8,128)(2,1)S(1)} %constant_dynamic-update-slice_fusion.refs_0_) | copy-start | bytes 1769476
  22.3 16.7 %collective-permute-start.11 = (bf16[16,144,128]{2,1,0:T(8,128)(2,1)S(1)}, bf16[16,144,128]{2,1,0:T(8,128)(2,1)}, u32[]{:S(2)}, u32[]{:S(2)}) collective-permute-start(bf16[16,144,128]{2,1,0:T(8,128)(2,1)S(1)} %constant_dynamic-update-slice_fusion.refs_0_), channel_id=1, source_target_pairs={{0,1},{1,0},{2,3},{3,2},{4,5},{5,4},{6,7},{7,6},{8,9},{9,8},{10,11... | collective-permute-start | bytes 1769480 | tf_op jit(solution)/shard_map/ppermute | solution.py:32
  31.6 5.9 %copy-start.6 = (bf16[1024,576]{0,1:T(8,128)(2,1)S(1)}, bf16[1024,576]{0,1:T(8,128)(2,1)}, u32[]{:S(2)}) copy-start(bf16[1024,576]{0,1:T(8,128)(2,1)} %param.10) | copy-start | bytes 3538948
  31.7 36.7 %copy-start.3 = (bf16[4,368,128]{2,1,0:T(8,128)(2,1)}, bf16[4,368,128]{2,1,0:T(8,128)(2,1)S(1)}, u32[]{:S(2)}) copy-start(bf16[4,368,128]{2,1,0:T(8,128)(2,1)S(1)} %get-tuple-element.140.refs_0_) | copy-start | bytes 1130500
  31.7 38.1 %copy-start.4 = (bf16[4,368,128]{2,1,0:T(8,128)(2,1)}, bf16[4,368,128]{2,1,0:T(8,128)(2,1)S(1)}, u32[]{:S(2)}) copy-start(bf16[4,368,128]{2,1,0:T(8,128)(2,1)S(1)} %get-tuple-element.144.refs_4_) | copy-start | bytes 1130500
  31.7 17.9 %collective-permute-start.10 = (bf16[4,368,128]{2,1,0:T(8,128)(2,1)S(1)}, bf16[4,368,128]{2,1,0:T(8,128)(2,1)}, u32[]{:S(2)}, u32[]{:S(2)}) collective-permute-start(bf16[4,368,128]{2,1,0:T(8,128)(2,1)S(1)} %get-tuple-element.144.refs_4_), channel_id=1, source_target_pairs={{0,4},{1,5},{2,6},{3,7},{4,0},{5,1},{6,2},{7,3},{8,12},{9,13},{10,... | collective-permute-start | bytes 1130504 | tf_op jit(solution)/shard_map/ppermute | solution.py:32
  33.3 16.4 %collective-permute-start.9 = (bf16[4,368,128]{2,1,0:T(8,128)(2,1)S(1)}, bf16[4,368,128]{2,1,0:T(8,128)(2,1)S(1)}, u32[]{:S(2)}, u32[]{:S(2)}) collective-permute-start(bf16[4,368,128]{2,1,0:T(8,128)(2,1)S(1)} %get-tuple-element.140.refs_0_), channel_id=1, source_target_pairs={{0,2},{1,3},{2,0},{3,1},{4,6},{5,7},{6,4},{7,5},{8,10},{9,11},{10,... | collective-permute-start | bytes 1130504 | tf_op jit(solution)/shard_map/ppermute | solution.py:32
  49.6 23.9 %copy-start.7 = (bf16[1024,576]{0,1:T(8,128)(2,1)S(1)}, bf16[1024,576]{0,1:T(8,128)(2,1)}, u32[]{:S(2)}) copy-start(bf16[1024,576]{0,1:T(8,128)(2,1)} %param.11) | copy-start | bytes 3538948
  49.7 24.5 %copy-start.13 = (bf16[4,368,128]{2,1,0:T(8,128)(2,1)}, bf16[4,368,128]{2,1,0:T(8,128)(2,1)S(1)}, u32[]{:S(2)}) copy-start(bf16[4,368,128]{2,1,0:T(8,128)(2,1)S(1)} %collective-permute-done.9.refs_1_) | copy-start | bytes 1130500
  49.7 18.7 %collective-permute-start.12 = (bf16[4,368,128]{2,1,0:T(8,128)(2,1)S(1)}, bf16[4,368,128]{2,1,0:T(8,128)(2,1)S(1)}, u32[]{:S(2)}, u32[]{:S(2)}) collective-permute-start(bf16[4,368,128]{2,1,0:T(8,128)(2,1)S(1)} %get-tuple-element.140.refs_0_), channel_id=1, source_target_pairs={{0,4},{1,5},{2,6},{3,7},{4,0},{5,1},{6,2},{7,3},{8,12},{9,13},{10,... | collective-permute-start | bytes 1130504 | tf_op jit(solution)/shard_map/ppermute | solution.py:32
  50.2 18.1 %collective-permute-start.13 = (bf16[4,368,128]{2,1,0:T(8,128)(2,1)S(1)}, bf16[4,368,128]{2,1,0:T(8,128)(2,1)}, u32[]{:S(2)}, u32[]{:S(2)}) collective-permute-start(bf16[4,368,128]{2,1,0:T(8,128)(2,1)S(1)} %collective-permute-done.9.refs_1_), channel_id=1, source_target_pairs={{0,4},{1,5},{2,6},{3,7},{4,0},{5,1},{6,2},{7,3},{8,12},{9,13},{10,... | collective-permute-start | bytes 1130504 | tf_op jit(solution)/shard_map/ppermute | solution.py:32
  51.8 16.6 %collective-permute-start.14 = (bf16[4,368,128]{2,1,0:T(8,128)(2,1)S(1)}, bf16[4,368,128]{2,1,0:T(8,128)(2,1)}, u32[]{:S(2)}, u32[]{:S(2)}) collective-permute-start(bf16[4,368,128]{2,1,0:T(8,128)(2,1)S(1)} %get-tuple-element.144.refs_4_), channel_id=1, source_target_pairs={{0,2},{1,3},{2,0},{3,1},{4,6},{5,7},{6,4},{7,5},{8,10},{9,11},{10,... | collective-permute-start | bytes 1130504 | tf_op jit(solution)/shard_map/ppermute | solution.py:32
  52.3 16.1 %collective-permute-start.15 = (bf16[4,368,128]{2,1,0:T(8,128)(2,1)}, bf16[4,368,128]{2,1,0:T(8,128)(2,1)}, u32[]{:S(2)}, u32[]{:S(2)}) collective-permute-start(bf16[4,368,128]{2,1,0:T(8,128)(2,1)} %collective-permute-done.10.refs_5_), channel_id=1, source_target_pairs={{0,2},{1,3},{2,0},{3,1},{4,6},{5,7},{6,4},{7,5},{8,10},{9,11},{10,... | collective-permute-start | bytes 1130504 | tf_op jit(solution)/shard_map/ppermute | solution.py:32
  61.0 13.2 %copy-start.18 = (bf16[2,576]{1,0:T(2,128)(2,1)S(1)}, bf16[2,576]{1,0:T(2,128)(2,1)}, u32[]{:S(2)}) copy-start(bf16[2,576]{1,0:T(2,128)(2,1)} %gains_ref.3) | copy-start | bytes 6916
  68.4 4.2 %copy-start.14 = (bf16[4,368,128]{2,1,0:T(8,128)(2,1)}, bf16[4,368,128]{2,1,0:T(8,128)(2,1)S(1)}, u32[]{:S(2)}) copy-start(bf16[4,368,128]{2,1,0:T(8,128)(2,1)S(1)} %collective-permute-done.12.refs_2_) | copy-start | bytes 1130500
  68.4 2.0 collective-permute-start.16
  68.7 2.2 collective-permute-start.17
  69.2 3.3 %collective-permute-start.18 = (bf16[4,368,128]{2,1,0:T(8,128)(2,1)S(1)}, bf16[4,368,128]{2,1,0:T(8,128)(2,1)S(1)}, u32[]{:S(2)}, u32[]{:S(2)}) collective-permute-start(bf16[4,368,128]{2,1,0:T(8,128)(2,1)S(1)} %collective-permute-done.12.refs_2_), channel_id=1, source_target_pairs={{0,1},{1,0},{2,3},{3,2},{4,5},{5,4},{6,7},{7,6},{8,9},{9,8},{10,11... | collective-permute-start | bytes 1130504 | tf_op jit(solution)/shard_map/ppermute | solution.py:32
  69.3 12.1 %collective-permute-start.19 = (bf16[4,368,128]{2,1,0:T(8,128)(2,1)}, bf16[4,368,128]{2,1,0:T(8,128)(2,1)}, u32[]{:S(2)}, u32[]{:S(2)}) collective-permute-start(bf16[4,368,128]{2,1,0:T(8,128)(2,1)} %collective-permute-done.13.refs_3_), channel_id=1, source_target_pairs={{0,1},{1,0},{2,3},{3,2},{4,5},{5,4},{6,7},{7,6},{8,9},{9,8},{10,11... | collective-permute-start | bytes 1130504 | tf_op jit(solution)/shard_map/ppermute | solution.py:32
  69.8 11.7 %collective-permute-start.20 = (bf16[4,368,128]{2,1,0:T(8,128)(2,1)S(1)}, bf16[4,368,128]{2,1,0:T(8,128)(2,1)}, u32[]{:S(2)}, u32[]{:S(2)}) collective-permute-start(bf16[4,368,128]{2,1,0:T(8,128)(2,1)S(1)} %get-tuple-element.144.refs_4_), channel_id=1, source_target_pairs={{0,1},{1,0},{2,3},{3,2},{4,5},{5,4},{6,7},{7,6},{8,9},{9,8},{10,11... | collective-permute-start | bytes 1130504 | tf_op jit(solution)/shard_map/ppermute | solution.py:32
  70.4 2.2 copy-start.15
  70.4 11.0 %collective-permute-start.21 = (bf16[4,368,128]{2,1,0:T(8,128)(2,1)}, bf16[4,368,128]{2,1,0:T(8,128)(2,1)}, u32[]{:S(2)}, u32[]{:S(2)}) collective-permute-start(bf16[4,368,128]{2,1,0:T(8,128)(2,1)} %collective-permute-done.10.refs_5_), channel_id=1, source_target_pairs={{0,1},{1,0},{2,3},{3,2},{4,5},{5,4},{6,7},{7,6},{8,9},{9,8},{10,11... | collective-permute-start | bytes 1130504 | tf_op jit(solution)/shard_map/ppermute | solution.py:32
  71.0 1.6 copy-start.16
  71.0 10.5 %collective-permute-start.22 = (bf16[4,368,128]{2,1,0:T(8,128)(2,1)}, bf16[4,368,128]{2,1,0:T(8,128)(2,1)}, u32[]{:S(2)}, u32[]{:S(2)}) collective-permute-start(bf16[4,368,128]{2,1,0:T(8,128)(2,1)} %collective-permute-done.14.refs_6_), channel_id=1, source_target_pairs={{0,1},{1,0},{2,3},{3,2},{4,5},{5,4},{6,7},{7,6},{8,9},{9,8},{10,11... | collective-permute-start | bytes 1130504 | tf_op jit(solution)/shard_map/ppermute | solution.py:32
  73.3 8.1 %collective-permute-start.23 = (bf16[4,368,128]{2,1,0:T(8,128)(2,1)}, bf16[4,368,128]{2,1,0:T(8,128)(2,1)}, u32[]{:S(2)}, u32[]{:S(2)}) collective-permute-start(bf16[4,368,128]{2,1,0:T(8,128)(2,1)} %collective-permute-done.15.refs_7_), channel_id=1, source_target_pairs={{0,1},{1,0},{2,3},{3,2},{4,5},{5,4},{6,7},{7,6},{8,9},{9,8},{10,11... | collective-permute-start | bytes 1130504 | tf_op jit(solution)/shard_map/ppermute | solution.py:32
  81.4 7.1 %copy-start = (bf16[1024,576]{1,0:T(8,128)(2,1)S(1)}, bf16[1024,576]{1,0:T(8,128)(2,1)}, u32[]{:S(2)}) copy-start(bf16[1024,576]{1,0:T(8,128)(2,1)} %copy.37.tokens_in.tokens_ref) | copy-start | bytes 3538948
  81.4 7.1 %copy-start.10 = (bf16[1024,192]{1,0:T(8,128)(2,1)S(1)}, bf16[1024,192]{1,0:T(8,128)(2,1)}, u32[]{:S(2)}) copy-start(bf16[1024,192]{1,0:T(8,128)(2,1)} %get-tuple-element.137.mixed_ref) | copy-start | bytes 1179652
  81.4 7.1 %copy-start.11 = (bf16[1024,192]{1,0:T(8,128)(2,1)S(1)}, bf16[1024,192]{1,0:T(8,128)(2,1)}, u32[]{:S(2)}) copy-start(bf16[1024,192]{1,0:T(8,128)(2,1)} %get-tuple-element.139.mixed_ref) | copy-start | bytes 1179652
  88.6 2.9 %copy-start.19 = (bf16[1536,576]{1,0:T(8,128)(2,1)S(1)}, bf16[1536,576]{1,0:T(8,128)(2,1)}, u32[]{:S(2)}) copy-start(bf16[1536,576]{1,0:T(8,128)(2,1)} %get-tuple-element.149) | copy-start | bytes 5308420
  94.1 1.5 copy-start.20
  95.6 5.1 %copy-start.21 = (bf16[576,1536]{1,0:T(8,128)(2,1)S(1)}, bf16[576,1536]{1,0:T(8,128)(2,1)}, u32[]{:S(2)}) copy-start(bf16[576,1536]{1,0:T(8,128)(2,1)} %get-tuple-element.150) | copy-start | bytes 5308420
  119.0 4.9 %copy-start.1 = (f32[1024,576]{1,0:T(8,128)}, f32[1024,576]{1,0:T(8,128)S(1)}, u32[]{:S(2)}) copy-start(f32[1024,576]{1,0:T(8,128)S(1)} %subtract_add_fusion.mid_back_ref) | copy-start | bytes 7077892
  119.0 2.4 %copy-start.12 = (bf16[1024,192]{1,0:T(8,128)(2,1)S(1)}, bf16[1024,192]{1,0:T(8,128)(2,1)}, u32[]{:S(2)}) copy-start(bf16[1024,192]{1,0:T(8,128)(2,1)} %get-tuple-element.136.mixed_ref) | copy-start | bytes 1179652
  121.4 2.5 %copy-start.24 = (bf16[1024,1536]{0,1:T(8,128)(2,1)S(1)}, bf16[1024,1536]{0,1:T(8,128)(2,1)}, u32[]{:S(2)}) copy-start(bf16[1024,1536]{0,1:T(8,128)(2,1)} %get-tuple-element.240) | copy-start | bytes 9437188
  128.1 4.2 %copy-start.23 = (bf16[1024,1536]{0,1:T(8,128)(2,1)S(1)}, bf16[1024,1536]{0,1:T(8,128)(2,1)}, u32[]{:S(2)}) copy-start(bf16[1024,1536]{0,1:T(8,128)(2,1)} %get-tuple-element.238) | copy-start | bytes 9437188
  147.1 11.2 %copy-start.2 = (bf16[16,736,128]{2,1,0:T(8,128)(2,1)S(1)}, bf16[16,736,128]{2,1,0:T(8,128)(2,1)}, u32[]{:S(2)}) copy-start(bf16[16,736,128]{2,1,0:T(8,128)(2,1)} %get-tuple-element.154) | copy-start | bytes 9043972
  147.1 11.2 %collective-permute-start.24 = (bf16[16,736,128]{2,1,0:T(8,128)(2,1)}, bf16[16,736,128]{2,1,0:T(8,128)(2,1)}, u32[]{:S(2)}, u32[]{:S(2)}) collective-permute-start(bf16[16,736,128]{2,1,0:T(8,128)(2,1)} %get-tuple-element.155), channel_id=1, source_target_pairs={{0,1},{1,0},{2,3},{3,2},{4,5},{5,4},{6,7},{7,6},{8,9},{9,8},{10,11... | collective-permute-start | bytes 9043976 | tf_op jit(solution)/shard_map/ppermute | solution.py:32
  161.7 15.2 %collective-permute-start.27 = (bf16[4,368,128]{2,1,0:T(8,128)(2,1)}, bf16[4,368,128]{2,1,0:T(8,128)(2,1)S(1)}, u32[]{:S(2)}, u32[]{:S(2)}) collective-permute-start(bf16[4,368,128]{2,1,0:T(8,128)(2,1)} %get-tuple-element.166), channel_id=1, source_target_pairs={{0,4},{1,5},{2,6},{3,7},{4,0},{5,1},{6,2},{7,3},{8,12},{9,13},{10,... | collective-permute-start | bytes 1130504 | tf_op jit(solution)/shard_map/ppermute | solution.py:32
  162.2 14.8 %collective-permute-start.26 = (bf16[4,368,128]{2,1,0:T(8,128)(2,1)S(1)}, bf16[4,368,128]{2,1,0:T(8,128)(2,1)S(1)}, u32[]{:S(2)}, u32[]{:S(2)}) collective-permute-start(bf16[4,368,128]{2,1,0:T(8,128)(2,1)S(1)} %get-tuple-element.164), channel_id=1, source_target_pairs={{0,2},{1,3},{2,0},{3,1},{4,6},{5,7},{6,4},{7,5},{8,10},{9,11},{10,... | collective-permute-start | bytes 1130504 | tf_op jit(solution)/shard_map/ppermute | solution.py:32
  162.7 31.6 %collective-permute-start.25 = (bf16[4,368,128]{2,1,0:T(8,128)(2,1)S(1)}, bf16[4,368,128]{2,1,0:T(8,128)(2,1)S(1)}, u32[]{:S(2)}, u32[]{:S(2)}) collective-permute-start(bf16[4,368,128]{2,1,0:T(8,128)(2,1)S(1)} %get-tuple-element.162), channel_id=1, source_target_pairs={{0,2},{1,3},{2,0},{3,1},{4,6},{5,7},{6,4},{7,5},{8,10},{9,11},{10,... | collective-permute-start | bytes 1130504 | tf_op jit(solution)/shard_map/ppermute | solution.py:32
  164.2 30.3 %collective-permute-start.29 = (bf16[4,368,128]{2,1,0:T(8,128)(2,1)S(1)}, bf16[4,368,128]{2,1,0:T(8,128)(2,1)S(1)}, u32[]{:S(2)}, u32[]{:S(2)}) collective-permute-start(bf16[4,368,128]{2,1,0:T(8,128)(2,1)S(1)} %get-tuple-element.173), channel_id=1, source_target_pairs={{0,4},{1,5},{2,6},{3,7},{4,0},{5,1},{6,2},{7,3},{8,12},{9,13},{10,... | collective-permute-start | bytes 1130504 | tf_op jit(solution)/shard_map/ppermute | solution.py:32
  177.2 17.2 %collective-permute-start.28 = (bf16[4,368,128]{2,1,0:T(8,128)(2,1)S(1)}, bf16[4,368,128]{2,1,0:T(8,128)(2,1)S(1)}, u32[]{:S(2)}, u32[]{:S(2)}) collective-permute-start(bf16[4,368,128]{2,1,0:T(8,128)(2,1)S(1)} %add_convert_fusion.2), channel_id=1, source_target_pairs={{0,4},{1,5},{2,6},{3,7},{4,0},{5,1},{6,2},{7,3},{8,12},{9,13},{10,... | collective-permute-start | bytes 1130504 | tf_op jit(solution)/shard_map/ppermute | solution.py:32
  177.8 16.8 %collective-permute-start.30 = (bf16[4,368,128]{2,1,0:T(8,128)(2,1)S(1)}, bf16[4,368,128]{2,1,0:T(8,128)(2,1)S(1)}, u32[]{:S(2)}, u32[]{:S(2)}) collective-permute-start(bf16[4,368,128]{2,1,0:T(8,128)(2,1)S(1)} %add_convert_fusion.1), channel_id=1, source_target_pairs={{0,2},{1,3},{2,0},{3,1},{4,6},{5,7},{6,4},{7,5},{8,10},{9,11},{10,... | collective-permute-start | bytes 1130504 | tf_op jit(solution)/shard_map/ppermute | solution.py:32
  194.8 23.4 %collective-permute-start.31 = (bf16[736,128]{1,0:T(8,128)(2,1)S(1)}, bf16[736,128]{1,0:T(8,128)(2,1)S(1)}, u32[]{:S(2)}, u32[]{:S(2)}) collective-permute-start(bf16[736,128]{1,0:T(8,128)(2,1)S(1)} %pad_maximum_fusion.7), channel_id=1, source_target_pairs={{0,8},{1,9},{2,10},{3,11},{4,12},{5,13},{6,14},{7,15},{8,0},{9,1},... | collective-permute-start | bytes 565256 | tf_op jit(solution)/shard_map/ppermute | solution.py:32
  197.4 20.7 %collective-permute-start.32 = (bf16[736,128]{1,0:T(8,128)(2,1)S(1)}, bf16[736,128]{1,0:T(8,128)(2,1)S(1)}, u32[]{:S(2)}, u32[]{:S(2)}) collective-permute-start(bf16[736,128]{1,0:T(8,128)(2,1)S(1)} %pad_maximum_fusion.8), channel_id=1, source_target_pairs={{0,16},{1,17},{2,18},{3,19},{4,20},{5,21},{6,22},{7,23},{8,24},{9,... | collective-permute-start | bytes 565256 | tf_op jit(solution)/shard_map/ppermute | solution.py:32
  197.5 20.7 %collective-permute-start.33 = (bf16[736,128]{1,0:T(8,128)(2,1)S(1)}, bf16[736,128]{1,0:T(8,128)(2,1)S(1)}, u32[]{:S(2)}, u32[]{:S(2)}) collective-permute-start(bf16[736,128]{1,0:T(8,128)(2,1)S(1)} %pad_maximum_fusion.9), channel_id=1, source_target_pairs={{0,24},{1,25},{2,26},{3,27},{4,28},{5,29},{6,30},{7,31},{8,16},{9,... | collective-permute-start | bytes 565256 | tf_op jit(solution)/shard_map/ppermute | solution.py:32
  218.1 2.3 copy-start.9
  218.1 2.3 collective-permute-start.34
  219.6 16.4 %copy-start.5 = (bf16[1024,576]{1,0:T(8,128)(2,1)S(1)}, bf16[1024,576]{1,0:T(8,128)(2,1)}, u32[]{:S(2)}) copy-start(bf16[1024,576]{1,0:T(8,128)(2,1)} %get-tuple-element.227) | copy-start | bytes 3538948
  220.6 6.7 %collective-permute-start.35 = (bf16[4,144,128]{2,1,0:T(8,128)(2,1)S(1)}, bf16[4,144,128]{2,1,0:T(8,128)(2,1)S(1)}, u32[]{:S(2)}, u32[]{:S(2)}) collective-permute-start(bf16[4,144,128]{2,1,0:T(8,128)(2,1)S(1)} %get-tuple-element.203), channel_id=1, source_target_pairs={{0,2},{1,3},{2,0},{3,1},{4,6},{5,7},{6,4},{7,5},{8,10},{9,11},{10,... | collective-permute-start | bytes 442376 | tf_op jit(solution)/shard_map/ppermute | solution.py:32
  222.1 8.8 %collective-permute-start.36 = (bf16[4,144,128]{2,1,0:T(8,128)(2,1)S(1)}, bf16[4,144,128]{2,1,0:T(8,128)(2,1)S(1)}, u32[]{:S(2)}, u32[]{:S(2)}) collective-permute-start(bf16[4,144,128]{2,1,0:T(8,128)(2,1)S(1)} %get-tuple-element.204), channel_id=1, source_target_pairs={{0,4},{1,5},{2,6},{3,7},{4,0},{5,1},{6,2},{7,3},{8,12},{9,13},{10,... | collective-permute-start | bytes 442376 | tf_op jit(solution)/shard_map/ppermute | solution.py:32
  223.7 7.2 %collective-permute-start.37 = (bf16[4,144,128]{2,1,0:T(8,128)(2,1)S(1)}, bf16[4,144,128]{2,1,0:T(8,128)(2,1)S(1)}, u32[]{:S(2)}, u32[]{:S(2)}) collective-permute-start(bf16[4,144,128]{2,1,0:T(8,128)(2,1)S(1)} %get-tuple-element.205), channel_id=1, source_target_pairs={{0,6},{1,7},{2,4},{3,5},{4,2},{5,3},{6,0},{7,1},{8,14},{9,15},{10,... | collective-permute-start | bytes 442376 | tf_op jit(solution)/shard_map/ppermute | solution.py:32
  231.0 6.5 %collective-permute-start.38 = (bf16[144,128]{1,0:T(8,128)(2,1)S(1)}, bf16[144,128]{1,0:T(8,128)(2,1)S(1)}, u32[]{:S(2)}, u32[]{:S(2)}) collective-permute-start(bf16[144,128]{1,0:T(8,128)(2,1)S(1)} %get-tuple-element.209), channel_id=1, source_target_pairs={{0,8},{1,9},{2,10},{3,11},{4,12},{5,13},{6,14},{7,15},{8,0},{9,1},... | collective-permute-start | bytes 110600 | tf_op jit(solution)/shard_map/ppermute | solution.py:32
  232.1 5.4 %collective-permute-start.39 = (bf16[144,128]{1,0:T(8,128)(2,1)S(1)}, bf16[144,128]{1,0:T(8,128)(2,1)S(1)}, u32[]{:S(2)}, u32[]{:S(2)}) collective-permute-start(bf16[144,128]{1,0:T(8,128)(2,1)S(1)} %get-tuple-element.210), channel_id=1, source_target_pairs={{0,16},{1,17},{2,18},{3,19},{4,20},{5,21},{6,22},{7,23},{8,24},{9,... | collective-permute-start | bytes 110600 | tf_op jit(solution)/shard_map/ppermute | solution.py:32
  233.1 5.8 %collective-permute-start.40 = (bf16[144,128]{1,0:T(8,128)(2,1)S(1)}, bf16[144,128]{1,0:T(8,128)(2,1)S(1)}, u32[]{:S(2)}, u32[]{:S(2)}) collective-permute-start(bf16[144,128]{1,0:T(8,128)(2,1)S(1)} %get-tuple-element.211), channel_id=1, source_target_pairs={{0,24},{1,25},{2,26},{3,27},{4,28},{5,29},{6,30},{7,31},{8,16},{9,... | collective-permute-start | bytes 110600 | tf_op jit(solution)/shard_map/ppermute | solution.py:32
  (2 other events, 1.9 us)
